TPU v7x, 32 devices: a whole 2x2x4 slice. The times are simulated.
32 devices in a mesh: ctx: 8 (over z, y), head: 4 (over x, core).
Axes of the slice: x: 2, y: 2, z: 4, core: 2. Of those that a mesh axis runs over, the one named last changes fastest.
Arguments:
- queries: bfloat16 [2048, 4096], P('ctx', 'head'), may hold values from -8 to 8
- keys: bfloat16 [2048, 1024], P('ctx', 'head'), may hold values from -6 to 6
- values: bfloat16 [2048, 1024], P('ctx', 'head'), may hold values from -6 to 6
- segment_ids: int32 [2048], P('ctx'), may hold values from 0 to 31, never falling along the last dimension, each value on 1 to 256 neighbouring positions
- out_weight: bfloat16 [4096, 4096], P('head'), may hold values from -0.125 to 0.125
Outputs:
- mixed: bfloat16 [2048, 4096], P('ctx', 'head')
Inputs may be any that keep to these rules, and one draw needn't show every extreme that they name: `segment_ids`: documents are contiguous runs of tokens; none is longer than 256 tokens and one is exactly that long.
All inputs are finite; a program needn't handle non-finite values.
Results may differ from a plain program's by a relative error of at most 0.015.
Values may be sent and summed in bfloat16 or wider, within the bound.
No kernel may reach another device: no remote copies, remote signals or barrier semaphores. Data moves between devices by JAX's collectives and lax.ppermute only.
A program may use at most 64 MiB of HBM per device.

v0:
```python
import math

import jax
import jax.numpy as jnp
from jax import lax
from jax.sharding import PartitionSpec as P

HEAD_DIM = 128


def shifted(array, axis, by):
    count = lax.axis_size(axis)
    pairs = [(i, i + by) for i in range(count) if 0 <= i + by < count]
    return lax.ppermute(array, axis, pairs)


def body(queries, keys, values, segment_ids, out_weight):
    tokens = queries.shape[0]
    kv_width = keys.shape[1]
    kv_local = kv_width // HEAD_DIM
    repeats = queries.shape[1] // kv_width
    scale = 1.0 / math.sqrt(HEAD_DIM)
    place = lax.axis_index("ctx")
    span = max(lax.axis_size("ctx") // 16, 2)
    grouped = queries.reshape(tokens, kv_local, repeats, HEAD_DIM)
    query_pos = place * tokens + jnp.arange(tokens, dtype=jnp.int32)

    def absorb(carry, packed, key_doc, key_pos):
        count = packed.shape[1]
        visible = (key_pos[None, :] <= query_pos[:, None]) & (key_pos[None, :] >= 0)
        visible = visible & (key_doc[None, :] == segment_ids[:, None])
        top, total, summed = carry
        keyset = packed[0].reshape(count, kv_local, HEAD_DIM)
        valset = packed[1].reshape(count, kv_local, HEAD_DIM)
        scores = (
            jnp.einsum("qgrd,kgd->grqk", grouped, keyset, preferred_element_type=jnp.float32)
            * scale
        )
        fresh = jnp.maximum(top, jnp.max(jnp.where(visible, scores, -1e30), axis=-1))
        weights = jnp.where(visible, jnp.exp(scores - fresh[..., None]), 0.0)
        factor = jnp.exp(top - fresh)
        total = total * factor + jnp.sum(weights, axis=-1)
        update = jnp.einsum(
            "grqk,kgd->grqd",
            weights.astype(jnp.bfloat16),
            valset,
            preferred_element_type=jnp.float32,
        )
        summed = summed * factor[..., None] + update
        return (fresh, total, summed)

    start_top = jnp.full((kv_local, repeats, tokens), -1e30, jnp.float32)
    start_total = jnp.zeros((kv_local, repeats, tokens), jnp.float32)
    start_sum = jnp.zeros((kv_local, repeats, tokens, HEAD_DIM), jnp.float32)
    own_pair = jnp.stack([keys, values], axis=0)
    carry = absorb((start_top, start_total, start_sum), own_pair, segment_ids, query_pos)
    offsets = jnp.arange(tokens, dtype=jnp.int32)

    def turn(step, state):
        inner, pair, docs = state
        pair, docs = shifted((pair, docs), "ctx", 1)
        key_pos = (place - step) * tokens + offsets
        return (absorb(inner, pair, docs, key_pos), pair, docs)

    carry, last_pair, last_docs = lax.fori_loop(1, span, turn, (carry, own_pair, segment_ids))
    final_top, final_total, final_sum = carry
    attended = final_sum / final_total[..., None]
    attended = jnp.transpose(attended, (2, 0, 1, 3)).reshape(tokens, kv_local * repeats * HEAD_DIM)
    attended = attended.astype(jnp.bfloat16)
    partial_out = jnp.dot(attended, out_weight, preferred_element_type=jnp.float32)
    mixed = lax.psum_scatter(
        partial_out.astype(jnp.bfloat16), "head", scatter_dimension=1, tiled=True
    )
    return mixed


def solution(mesh):
    in_specs = (P("ctx", "head"), P("ctx", "head"), P("ctx", "head"), P("ctx"), P("head", None))
    out_specs = P("ctx", "head")
    return jax.shard_map(body, mesh=mesh, in_specs=in_specs, out_specs=out_specs, check_vma=False)
```

profile of v0, /device:TPU:0, one launch (start us, length us, event | category | flops | bytes accessed | tf_op | source)
XLA Modules:
  0.0 70.5 jit_solution(13779438067169032126)
XLA Ops:
  6.5 0.0 copy-start
  6.5 0.0 reduce-scatter.2.cloned.1.call-start
  6.5 5.0 %collective-permute-start = (s32[256]{0:T(256)}, s32[256]{0:T(256)S(1)}, u32[]{:S(2)}, u32[]{:S(2)}) collective-permute-start(s32[256]{0:T(256)} %param.8), channel_id=1, source_target_pairs={{0,4},{4,8},{8,12},{12,16},{16,20},{20,24},{24,28},{1,5},{5,9},{9,... | collective-permute-start | bytes 3080 | tf_op jit(solution)/shard_map/while/body/eval_jaxpr/ppermute | solution.py:14
  11.5 1.0 %copy.30 = bf16[256,256]{0,1:T(8,128)(2,1)S(1)} copy(bf16[256,256]{1,0:T(8,128)(2,1)} %param.7) | data formatting | bytes 262144 | tf_op jit(solution)/shard_map/reshape;squeeze;stack | solution.py:34
  12.5 1.0 %copy.17 = bf16[256,256]{0,1:T(8,128)(2,1)S(1)} copy(bf16[256,256]{1,0:T(8,128)(2,1)} %param.6) | data formatting | bytes 262144 | tf_op args[1]
  13.6 3.4 %collective-permute-start.1 = (bf16[2,256,256]{1,2,0:T(8,128)(2,1)S(1)}, bf16[2,256,256]{1,2,0:T(8,128)(2,1)S(1)}, u32[]{:S(2)}, u32[]{:S(2)}) collective-permute-start(bf16[2,256,256]{1,2,0:T(8,128)(2,1)S(1)} %pad_maximum_fusion), channel_id=1, source_target_pairs={{0,4},{4,8},{8,12},{12,16},{16,20},{20,24},{24,28},{1,5},{5,9},{9,... | collective-permute-start | bytes 786440 | tf_op jit(solution)/shard_map/while/body/eval_jaxpr/ppermute | solution.py:14
  17.1 0.9 %reshape_squeeze_stack.6 = bf16[256,2,128]{2,1,0:T(2,128)(2,1)S(1)} reshape(bf16[256,256]{1,0:T(8,128)(2,1)} %param.6) | data formatting | bytes 262144 | tf_op jit(solution)/shard_map/reshape;squeeze;stack | solution.py:33
  18.1 1.4 %reshape.58 = bf16[256,2,4,128]{3,2,1,0:T(4,128)(2,1)S(1)} reshape(bf16[256,1024]{1,0:T(8,128)(2,1)} %param.5) | data formatting | bytes 1048576 | tf_op jit(solution)/shard_map/reshape | solution.py:25
  19.5 0.0 collective-permute-done
  19.5 0.0 copy-done
  19.5 0.3 compare_and_fusion
  19.8 0.5 fusion.3
  20.3 2.0 %collective-permute-done.1 = bf16[2,256,256]{1,2,0:T(8,128)(2,1)S(1)} collective-permute-done((bf16[2,256,256]{1,2,0:T(8,128)(2,1)S(1)}, bf16[2,256,256]{1,2,0:T(8,128)(2,1)S(1)}, u32[]{:S(2)}, u32[]{:S(2)}) %collective-permute-start.1) | collective-permute-done | bytes 262176 | tf_op jit(solution)/shard_map/while/body/eval_jaxpr/ppermute | solution.py:14
  22.3 0.0 slice-start
  22.3 0.6 fusion
  22.9 0.9 %fusion.6 = (f32[2,4,256]{2,1,0:T(4,128)S(1)}, f32[2,4,256]{2,1,0:T(4,128)S(1)}) fusion(f32[2,256,256,4]{2,1,3,0:T(8,128)S(1)} %get-tuple-element.53, f32[2,4,256]{2,1,0:T(4,128)S(1)} %get-tuple-element.33, pred[256,256]{0,1:T(8,128)(4,1)S(1)} %get-tuple-element.35, f32[2,4,256]{2,1,0:T(4,128)S(1)} %get-tuple-element.32, ...), kind=kLoop, calls=%fused_computation.11 | loop fusion | flops 4190208 | bytes 4358144 | tf_op jit(solution)/shard_map/reduce_sum | solution.py:42
  23.8 0.0 slice-start.1
  23.8 0.6 fusion.13
  24.4 0.6 fusion.14
  25.0 0.0 slice-done
  25.0 1.2 %slice-done.1 = s8[4194304]{0:T(1024)(128)(4,1)S(1)} async-done(((s8[8388608]{0:T(1024)(128)(4,1)}), s8[4194304]{0:T(1024)(128)(4,1)S(1)}, s32[]{:S(2)}) %slice-start.1) | async-done | bytes 4194328
  26.2 3.7 %convolution_convert_fusion = bf16[256,4096]{1,0:T(8,128)(2,1)} fusion(bf16[256,1024]{0,1:T(8,128)(2,1)S(1)} %bitcast.89, bf16[1024,4096]{1,0:T(8,128)(2,1)S(1)} %bitcast.88), kind=kOutput, calls=%fused_computation | convolution fusion | flops 2148532224 | bytes 11010048 | tf_op jit(solution)/shard_map/dot_general | solution.py:70
  29.9 0.0 reduce-scatter.2.cloned.1.call-update
  29.9 33.8 %reduce-scatter.2.cloned.1.call-done = bf16[256,1024]{1,0:T(8,128)(2,1)} async-done(((bf16[256,4096]{1,0:T(8,128)(2,1)}), bf16[256,1024]{1,0:T(8,128)(2,1)}) %reduce-scatter.2.cloned.1.call-update) | async-done | bytes 524304 | tf_op jit(solution)/shard_map/reduce_scatter | solution.py:71
  (9 shorter events, 0.1 us)
Async XLA Ops:
  6.5 12.9 %copy-start = (s32[256]{0:T(256)S(1)}, s32[256]{0:T(256)}, u32[]{:S(2)}) copy-start(s32[256]{0:T(256)} %param.8) | copy-start | bytes 3076
  6.5 57.2 %reduce-scatter.2.cloned.1.call-start = ((), (), s32[]{:S(2)}) async-start(), calls=%async_computation.1 | async-start | bytes 2621440 | tf_op jit(solution)/shard_map/reduce_scatter | solution.py:71
  6.5 12.9 %collective-permute-start = (s32[256]{0:T(256)}, s32[256]{0:T(256)S(1)}, u32[]{:S(2)}, u32[]{:S(2)}) collective-permute-start(s32[256]{0:T(256)} %param.8), channel_id=1, source_target_pairs={{0,4},{4,8},{8,12},{12,16},{16,20},{20,24},{24,28},{1,5},{5,9},{9,... | collective-permute-start | bytes 3080 | tf_op jit(solution)/shard_map/while/body/eval_jaxpr/ppermute | solution.py:14
  13.6 8.7 %collective-permute-start.1 = (bf16[2,256,256]{1,2,0:T(8,128)(2,1)S(1)}, bf16[2,256,256]{1,2,0:T(8,128)(2,1)S(1)}, u32[]{:S(2)}, u32[]{:S(2)}) collective-permute-start(bf16[2,256,256]{1,2,0:T(8,128)(2,1)S(1)} %pad_maximum_fusion), channel_id=1, source_target_pairs={{0,4},{4,8},{8,12},{12,16},{16,20},{20,24},{24,28},{1,5},{5,9},{9,... | collective-permute-start | bytes 786440 | tf_op jit(solution)/shard_map/while/body/eval_jaxpr/ppermute | solution.py:14
  22.3 2.7 %slice-start = ((s8[8388608]{0:T(1024)(128)(4,1)}), s8[4194304]{0:T(1024)(128)(4,1)S(1)}, s32[]{:S(2)}) async-start(s8[8388608]{0:T(1024)(128)(4,1)} %bitcast.87), calls=%async_computation.2 | async-start | bytes 8388608
  23.8 2.4 %slice-start.1 = ((s8[8388608]{0:T(1024)(128)(4,1)}), s8[4194304]{0:T(1024)(128)(4,1)S(1)}, s32[]{:S(2)}) async-start(s8[8388608]{0:T(1024)(128)(4,1)} %bitcast.87), calls=%async_computation.3 | async-start | bytes 8388608
Sparse Core Ops, SparseCore 0:
  30.1 33.5 reduce-scatter.1
where the time goes:
time: 70.8 us; the launch traced here: 70.5 us
  waiting for transfers between devices  35.8 us (51%)
  between operations  13.6 us (19%)
  starting transfers between devices  8.44 us (12%)
  matrix products  5.98 us (8%)
  local copies, waits for them, and re-layouts  5.54 us (8%)
  other arithmetic  1.25 us (2%)
    reduce_scatter x1, waiting for transfers between devices, body(): lax.psum_scatter(partial_out.astype(jnp.bfloat16), 'head', scatter_dimens...  33.8 us
    ppermute x2, starting transfers between devices, shifted(): return lax.ppermute(array, axis, pairs)  8.43 us
    dot_general x1, matrix products, body(): jnp.dot(attended, out_weight, preferred_element_type=jnp.float32)  3.72 us
    unnamed x7, local copies, waits for them, and re-layouts  2.17 us
    ppermute x2, waiting for transfers between devices, shifted(): return lax.ppermute(array, axis, pairs)  2.01 us
  transfers between devices with their start and end apart: 3, of which 2 were waited for; matrix products, arithmetic and copies ran while one was open for 7% of the time, Pallas kernels for 0%

commit v1 on v0

v1 whole, which is shorter than its diff:
```python
import math

import jax
import jax.numpy as jnp
from jax import lax
from jax.experimental import pallas as pl
from jax.experimental.pallas import tpu as pltpu
from jax.sharding import PartitionSpec as P

HEAD_DIM = 128
CORES = 2
HALVES = 2
DOC_ROWS = 16
LOG2_SCALE = math.log2(math.e) / math.sqrt(HEAD_DIM)
HIDDEN = -1e30
NT = (((1,), (1,)), ((), ()))
VMEM = pl.BlockSpec(memory_space=pltpu.VMEM)
ANY = pl.BlockSpec(memory_space=pl.ANY)
HBM = pl.BlockSpec(memory_space=pltpu.HBM)


def near(x):
    return pltpu.with_memory_space_constraint(x, pltpu.VMEM)


def far(x):
    return pltpu.with_memory_space_constraint(x, pltpu.HBM)


def call(kernel, out_shape, in_specs, args, flops, bytes_accessed, vmem_mib=16, scratch=()):
    return pl.pallas_call(
        kernel,
        out_shape=out_shape,
        in_specs=in_specs,
        out_specs=jax.tree.map(lambda _: VMEM, out_shape),
        scratch_shapes=scratch,
        compiler_params=pltpu.CompilerParams(vmem_limit_bytes=vmem_mib * 2**20),
        cost_estimate=pl.CostEstimate(
            flops=flops, bytes_accessed=bytes_accessed, transcendentals=0
        ),
    )(*args)


def pack_kernel(k_ref, v_ref, doc_ref, out_ref, held, sem):
    tokens, width = k_ref.shape
    copies = [
        pltpu.make_async_copy(k_ref, out_ref.at[:tokens], sem.at[0]),
        pltpu.make_async_copy(v_ref, out_ref.at[tokens : 2 * tokens], sem.at[1]),
        pltpu.make_async_copy(doc_ref, held, sem.at[2]),
    ]
    for copy in copies:
        copy.start()
    copies[2].wait()
    rows = [
        (held[:, i * width : (i + 1) * width] + 1).astype(jnp.float32)
        for i in range(tokens // width)
    ]
    rows.append(jnp.zeros((DOC_ROWS - len(rows), width), jnp.float32))
    out_ref[2 * tokens :, :] = jnp.concatenate(rows, axis=0).astype(jnp.bfloat16)
    copies[0].wait()
    copies[1].wait()


def doc_column(docs):
    count = docs.shape[1]
    return jnp.transpose(jnp.broadcast_to(docs, (count, count)))[:, :1]


def stacked(q_ref, r0, rows, first, repeats):
    heads = [
        q_ref[r0 : r0 + rows, h * HEAD_DIM : (h + 1) * HEAD_DIM]
        for h in range(first, first + repeats)
    ]
    return jnp.concatenate(heads, axis=0)


def with_ones(v):
    return jnp.concatenate([v, jnp.ones_like(v)], axis=1)


def hide(scores, bias):
    rows, count = bias.shape
    shape = (scores.shape[0] // rows, rows, count)
    return (scores.reshape(shape) + bias[None]).reshape(scores.shape)


def weights_of(scores, top):
    return jnp.exp2((scores - top) * LOG2_SCALE).astype(jnp.bfloat16)


def own_kernel(
    chips, q_hbm, k_hbm, v_hbm, doc_hbm, w_ref,
    acc_ref, top_ref, total_ref, q_ref, doc_ref, held_ref, k_ref, v_ref, in_sem, sem,
):
    inputs = [
        pltpu.make_async_copy(source, target, in_sem.at[i])
        for i, (source, target) in enumerate(
            ((doc_hbm, doc_ref), (q_hbm, q_ref), (k_hbm, k_ref), (v_hbm, v_ref))
        )
    ]
    for copy in inputs:
        copy.start()
    me = lax.axis_index("head")
    chip, core = me // CORES, me % CORES
    block = w_ref.shape[1] // (chips * CORES)
    copies = []
    for d in range(chips):
        for which in range(CORES):
            target = lax.rem(chip + d, chips) * CORES + lax.rem(core + which, CORES)
            start = pl.multiple_of(target * block, block)
            copy = pltpu.make_async_copy(
                w_ref.at[:, pl.ds(start, block)], held_ref.at[d, which], sem.at[d, which]
            )
            copy.start()
            copies.append(copy)
    for copy in inputs:
        copy.wait()

    tokens, width = q_ref.shape
    groups = k_ref.shape[1] // HEAD_DIM
    repeats = width // HEAD_DIM // groups
    rows = tokens // HALVES
    docs = doc_ref[...].astype(jnp.float32)
    column = doc_column(docs)
    for half in range(HALVES):
        r0, count = half * rows, (half + 1) * rows
        at = r0 + lax.broadcasted_iota(jnp.int32, (rows, count), 0)
        key = lax.broadcasted_iota(jnp.int32, (rows, count), 1)
        visible = (key <= at) & (docs[:, :count] == column[r0 : r0 + rows])
        bias = jnp.where(visible, 0.0, HIDDEN)
        for g in range(groups):
            lanes = slice(g * HEAD_DIM, (g + 1) * HEAD_DIM)
            q = stacked(q_ref, r0, rows, g * repeats, repeats)
            scores = lax.dot_general(q, k_ref[:count, lanes], NT, preferred_element_type=jnp.float32)
            scores = hide(scores, bias)
            top = jnp.max(scores, axis=1, keepdims=True)
            v1 = with_ones(v_ref[:count, lanes])
            summed = jnp.dot(weights_of(scores, top), v1, preferred_element_type=jnp.float32)
            acc_ref[half, g] = summed[:, :HEAD_DIM]
            total_ref[half, g] = summed[:, HEAD_DIM:]
            top_ref[half, g] = jnp.broadcast_to(top, (q.shape[0], HEAD_DIM))
    for copy in copies:
        copy.wait()


def cross_kernel(q_ref, doc_ref, acc_ref, top_ref, total_ref, *rest):
    prev_refs, att_ref = rest[:-1], rest[-1]
    tokens, width = q_ref.shape
    groups = prev_refs[0].shape[1] // HEAD_DIM
    repeats = width // HEAD_DIM // groups
    rows = tokens // HALVES
    column = doc_column(doc_ref[...].astype(jnp.float32))
    key_docs = []
    for prev in prev_refs:
        wide = prev[2 * tokens : 2 * tokens + DOC_ROWS, :].astype(jnp.float32)
        parts = [wide[i : i + 1, :] for i in range(tokens // prev.shape[1])]
        key_docs.append(jnp.concatenate(parts, axis=1) - 1.0)
    for half in reversed(range(HALVES)):
        r0 = half * rows
        for g in range(groups):
            lanes = slice(g * HEAD_DIM, (g + 1) * HEAD_DIM)
            q = stacked(q_ref, r0, rows, g * repeats, repeats)
            acc, top, total = acc_ref[half, g], top_ref[half, g], total_ref[half, g]
            for i, prev in enumerate(prev_refs):
                first = r0 if i == len(prev_refs) - 1 else 0
                visible = key_docs[i][:, first:] == column[r0 : r0 + rows]
                bias = jnp.where(visible, 0.0, HIDDEN)
                scores = lax.dot_general(
                    q, prev[first:tokens, lanes], NT, preferred_element_type=jnp.float32
                )
                scores = hide(scores, bias)
                fresh = jnp.maximum(top, jnp.max(scores, axis=1, keepdims=True))
                factor = jnp.exp2((top - fresh) * LOG2_SCALE)
                v1 = with_ones(prev[tokens + first : 2 * tokens, lanes])
                summed = jnp.dot(
                    weights_of(scores, fresh[:, :1]), v1, preferred_element_type=jnp.float32
                )
                acc = acc * factor + summed[:, :HEAD_DIM]
                total = total * factor + summed[:, HEAD_DIM:]
                top = fresh
            result = (acc / total).astype(jnp.bfloat16)
            for r in range(repeats):
                h = g * repeats + r
                att_ref[r0 : r0 + rows, h * HEAD_DIM : (h + 1) * HEAD_DIM] = result[
                    r * rows : (r + 1) * rows
                ]


def project_kernel(d, c0, att_ref, held_ref, *rest):
    keep_ref, give_ref = rest[-2:]
    cols = keep_ref.shape[1]
    att = att_ref[...]
    for which, out in ((1, give_ref), (0, keep_ref)):
        out[...] = jnp.dot(
            att, held_ref[d, which, :, c0 : c0 + cols], preferred_element_type=jnp.float32
        ).astype(jnp.bfloat16)


def body(queries, keys, values, segment_ids, out_weight):
    tokens, width = queries.shape
    kv_width = keys.shape[1]
    groups = kv_width // HEAD_DIM
    place_count = lax.axis_size("ctx")
    devices = lax.axis_size("head")
    chips = devices // CORES
    rows, columns = out_weight.shape
    block = columns // devices
    span = max(place_count // 16, 2)
    bf16, f32 = jnp.bfloat16, jnp.float32
    dma = pltpu.SemaphoreType.DMA

    doc_row = segment_ids.reshape(1, tokens)
    packed = call(
        pack_kernel,
        pltpu.VMEM((2 * tokens + DOC_ROWS, kv_width), bf16),
        [HBM] * 3,
        (far(keys), far(values), far(doc_row)),
        0,
        8 * tokens * kv_width,
        scratch=[pltpu.VMEM((1, tokens), jnp.int32), dma((3,))],
    )
    prevs = [
        lax.ppermute(packed, "ctx", [(i, i + s) for i in range(place_count - s)])
        for s in range(1, span)
    ]

    attention_flops = 4 * tokens * tokens * width
    state = pltpu.VMEM((HALVES, groups, tokens // HALVES * (width // kv_width), HEAD_DIM), f32)
    acc, top, total, near_q, near_doc, held = call(
        lambda *refs: own_kernel(chips, *refs),
        [
            state,
            state,
            state,
            pltpu.VMEM((tokens, width), bf16),
            pltpu.VMEM((1, tokens), jnp.int32),
            pltpu.VMEM((chips, CORES, rows, block), bf16),
        ],
        [HBM] * 5,
        (far(queries), far(keys), far(values), far(doc_row), far(out_weight)),
        attention_flops,
        2 * rows * columns,
        scratch=[
            pltpu.VMEM((tokens, kv_width), bf16),
            pltpu.VMEM((tokens, kv_width), bf16),
            dma((4,)),
            dma((chips, CORES)),
        ],
    )

    att = call(
        cross_kernel,
        pltpu.VMEM((tokens, width), bf16),
        [VMEM] * (5 + len(prevs)),
        (near(near_q), near(near_doc), near(acc), near(top), near(total), *map(near, prevs)),
        attention_flops,
        4 * tokens * width,
    )

    def project(d, c0, cols, *after):
        out = pltpu.VMEM((tokens, cols), bf16)
        return call(
            lambda *refs: project_kernel(d, c0, *refs),
            [out, out],
            [VMEM] * 2 + [ANY] * len(after),
            (near(att), near(held), *after),
            4 * tokens * rows * cols,
            4 * rows * cols,
        )

    other_core = [(i, i ^ 1) for i in range(devices)]
    cols = block // HALVES
    parts = [[] for _ in range(HALVES)]
    after = []
    for d in list(range(1, chips)) + [0]:
        for c in range(HALVES):
            keep, give = project(d, c * cols, cols, *(after if d == 0 else []))
            got = lax.ppermute(give, "head", other_core)
            summed = keep.astype(f32) + got.astype(f32)
            if d > 0:
                pairs = [(i, (i + d * CORES) % devices) for i in range(devices)]
                summed = summed.astype(bf16)
                after = [summed]
                summed = lax.ppermute(summed, "head", pairs).astype(f32)
            parts[c].append(summed)
    outs = []
    for c in range(HALVES):
        result = parts[c][0]
        for part in parts[c][1:]:
            result = result + part
        outs.append(result.astype(bf16))
    return jnp.concatenate(outs, axis=1)


def solution(mesh):
    in_specs = (P("ctx", "head"), P("ctx", "head"), P("ctx", "head"), P("ctx"), P("head", None))
    out_specs = P("ctx", "head")
    return jax.shard_map(body, mesh=mesh, in_specs=in_specs, out_specs=out_specs, check_vma=False)
```

time: 70.8 us -> 32.4 us (0.46)
  waiting for transfers between devices: 35.8 us -> 13 us
  between operations: 13.6 us -> 0.1 us
  Pallas kernels: 0 us -> 9.59 us
  matrix products: 5.98 us -> 0 us
  local copies, waits for them, and re-layouts: 5.54 us -> 0 us
    reduce_scatter x1 -> x0, waiting for transfers between devices: 33.8 us -> none  [body(): lax.psum_scatter(partial_out.astype(jnp.bfloat16), 'head', scatter_dimens...]
    ppermute x2 -> x7, waiting for transfers between devices: 2.01 us -> 13 us  [the longest x2 11.3 us: body(): summed = lax.ppermute(summed, 'head', pairs).astype(f32)]
    pallas_call x0 -> x7, Pallas kernels: none -> 9.59 us  [call(): pl.pallas_call(kernel, out_shape=out_shape, in_specs=in_specs, out_specs=...]
    dot_general x5 -> x0, matrix products: 5.98 us -> none  [the longest x1 3.72 us: body(): jnp.dot(attended, out_weight, preferred_element_type=jnp.float32)]
    unnamed x7 -> x0, local copies, waits for them, and re-layouts: 2.17 us -> none
    another operation x2 -> x0, local copies, waits for them, and re-layouts: 1.94 us -> none  [the longest x1 1 us: absorb(): valset = packed[1].reshape(count, kv_local, HEAD_DIM)]
    reshape x1 -> x0, local copies, waits for them, and re-layouts: 1.41 us -> none  [body(): grouped = queries.reshape(tokens, kv_local, repeats, HEAD_DIM)]
    reduce_sum x1 -> x0, other arithmetic: 0.9 us -> none  [absorb(): total = total * factor + jnp.sum(weights, axis=-1)]
  transfers between devices with their start and end apart: 3 -> 7, of which waited for: 2 -> 4; matrix products, arithmetic and copies ran while one was open for 7% -> 1% of each run, Pallas kernels for 0% -> 20%
where the time goes in v1:
time: 32.4 us; the launch traced here: 31.8 us
  waiting for transfers between devices  13 us (40%)
  Pallas kernels  9.59 us (30%)
  starting transfers between devices  7.89 us (24%)
  other arithmetic  1.2 us (4%)
    ppermute x2, waiting for transfers between devices, body(): summed = lax.ppermute(summed, 'head', pairs).astype(f32)  11.3 us
    pallas_call x7, Pallas kernels, call(): pl.pallas_call(kernel, out_shape=out_shape, in_specs=in_specs, out_specs=...  9.59 us
    ppermute x1, starting transfers between devices, body(): lax.ppermute(packed, 'ctx', [(i, i + s) for i in range(place_count - s)])  4.89 us
    ppermute x2, starting transfers between devices, body(): summed = lax.ppermute(summed, 'head', pairs).astype(f32)  2.11 us
    ppermute x1, waiting for transfers between devices, body(): lax.ppermute(packed, 'ctx', [(i, i + s) for i in range(place_count - s)])  1.54 us
    ppermute x4, starting transfers between devices, body(): got = lax.ppermute(give, 'head', other_core)  0.89 us
    concatenate x1, other arithmetic, body(): return jnp.concatenate(outs, axis=1)  0.86 us
  transfers between devices with their start and end apart: 7, of which 4 were waited for; matrix products, arithmetic and copies ran while one was open for 1% of the time, Pallas kernels for 20%

profile of v1, /device:TPU:0, one launch (start us, length us, event | category | flops | bytes accessed | tf_op | source)
XLA Modules:
  0.0 31.8 jit_solution(17097117334654897932)
XLA Ops:
  0.0 1.0 %shard_map.56 = bf16[528,256]{1,0:T(8,128)(2,1)S(1)} custom-call(bf16[256,256]{1,0:T(8,128)(2,1)} %k_ref.1, bf16[256,256]{1,0:T(8,128)(2,1)} %v_ref.1, s32[1,256]{1,0:T(1,128)} %bitcast.1), custom_call_target="tpu_custom_call" | custom-call | bytes 524288 | tf_op jit(solution)/shard_map/pallas_call | solution.py:31
  1.0 4.9 %collective-permute-start = (bf16[528,256]{1,0:T(8,128)(2,1)S(1)}, bf16[528,256]{1,0:T(8,128)(2,1)S(1)}, u32[]{:S(2)}, u32[]{:S(2)}) collective-permute-start(bf16[528,256]{1,0:T(8,128)(2,1)S(1)} %shard_map.56), channel_id=1, source_target_pairs={{0,4},{4,8},{8,12},{12,16},{16,20},{20,24},{24,28},{1,5},{5,9},{9,... | collective-permute-start | bytes 811016 | tf_op jit(solution)/shard_map/ppermute | solution.py:223
  5.9 4.2 %shard_map.55 = (f32[2,2,512,128]{3,2,1,0:T(8,128)S(1)}, f32[2,2,512,128]{3,2,1,0:T(8,128)S(1)}, f32[2,2,512,128]{3,2,1,0:T(8,128)S(1)}, bf16[256,1024]{1,0:T(8,...) custom-call(bf16[256,1024]{1,0:T(8,128)(2,1)} %refs_0_.1, bf16[256,256]{1,0:T(8,128)(2,1)} %k_ref.1, ...), custom_call_target="tpu_custom_call" | custom-call | flops 268435456 | bytes 8388608 | tf_op jit(solution)/shard_map/pallas_call | solution.py:31
  10.1 1.5 %collective-permute-done.rest_0_ = bf16[528,256]{1,0:T(8,128)(2,1)S(1)} collective-permute-done((bf16[528,256]{1,0:T(8,128)(2,1)S(1)}, bf16[528,256]{1,0:T(8,128)(2,1)S(1)}, u32[]{:S(2)}, u32[]{:S(2)}) %collective-permute-start) | collective-permute-done | bytes 270368 | tf_op jit(solution)/shard_map/ppermute | solution.py:223
  11.6 1.6 %shard_map.57.refs_0_ = bf16[256,1024]{1,0:T(8,128)(2,1)S(1)} custom-call(bf16[256,1024]{1,0:T(8,128)(2,1)S(1)} %get-tuple-element.19.q_ref, s32[1,256]{1,0:T(1,128)S(1)} %get-tuple-element.20.doc_ref, f32[2,2,512,128]{3,2,1,0:T(8,128)S(1)} %get-tuple-element.21.acc_ref, f32[2,2,512,128]{3,2,1,0:T(8,128)S(1)} %get-tuple-element.22.top_ref, ...), custom_call_target="tpu_custom_call" | custom-call | flops 268435456 | bytes 1048576 | tf_op jit(solution)/shard_map/pallas_call | solution.py:31
  13.2 0.7 %shard_map.59 = (bf16[256,512]{1,0:T(8,128)(2,1)S(1)}, bf16[256,512]{1,0:T(8,128)(2,1)S(1)}) custom-call(bf16[256,1024]{1,0:T(8,128)(2,1)S(1)} %shard_map.57.refs_0_, bf16[2,2,1024,1024]{3,2,1,0:T(8,128)(2,1)S(1)} %get-tuple-element.24.refs_1_), custom_call_target="tpu_custom_call" | custom-call | flops 536870912 | bytes 2097152 | tf_op jit(solution)/shard_map/pallas_call | solution.py:31
  13.9 0.1 collective-permute-start.3
  14.0 0.7 %shard_map.58 = (bf16[256,512]{1,0:T(8,128)(2,1)S(1)}, bf16[256,512]{1,0:T(8,128)(2,1)S(1)}) custom-call(bf16[256,1024]{1,0:T(8,128)(2,1)S(1)} %shard_map.57.refs_0_, bf16[2,2,1024,1024]{3,2,1,0:T(8,128)(2,1)S(1)} %get-tuple-element.24.refs_1_), custom_call_target="tpu_custom_call" | custom-call | flops 536870912 | bytes 2097152 | tf_op jit(solution)/shard_map/pallas_call | solution.py:31
  14.7 0.6 %collective-permute-start.1 = (bf16[256,512]{1,0:T(8,128)(2,1)S(1)}, bf16[256,512]{1,0:T(8,128)(2,1)S(1)}, u32[]{:S(2)}, u32[]{:S(2)}) collective-permute-start(bf16[256,512]{1,0:T(8,128)(2,1)S(1)} %get-tuple-element.26), channel_id=1, source_target_pairs={{0,1},{1,0},{2,3},{3,2},{4,5},{5,4},{6,7},{7,6},{8,9},{9,8},{10,11... | collective-permute-start | bytes 786440 | tf_op jit(solution)/shard_map/ppermute | solution.py:278
  15.3 0.2 collective-permute-done.3
  15.5 0.1 add_convert_fusion.2.refs_2_
  15.6 0.7 %shard_map.60 = (bf16[256,512]{1,0:T(8,128)(2,1)S(1)}, bf16[256,512]{1,0:T(8,128)(2,1)S(1)}) custom-call(bf16[256,1024]{1,0:T(8,128)(2,1)S(1)} %shard_map.57.refs_0_, bf16[2,2,1024,1024]{3,2,1,0:T(8,128)(2,1)S(1)} %get-tuple-element.24.refs_1_, bf16[256,512]{1,0:T(8,128)(2,1)S(1)} %add_convert_fusion.2.refs_2_), custom_call_target="tpu_custom_call" | custom-call | flops 536870912 | bytes 2097152 | tf_op jit(solution)/shard_map/pallas_call | solution.py:31
  16.3 0.2 collective-permute-start.4
  16.5 0.0 collective-permute-done.1
  16.5 0.1 add_convert_fusion.3
  16.6 1.6 %collective-permute-start.2 = (bf16[256,512]{1,0:T(8,128)(2,1)S(1)}, bf16[256,512]{1,0:T(8,128)(2,1)S(1)}, u32[]{:S(2)}, u32[]{:S(2)}) collective-permute-start(bf16[256,512]{1,0:T(8,128)(2,1)S(1)} %add_convert_fusion.3), channel_id=1, source_target_pairs={{0,2},{1,3},{2,0},{3,1},{4,6},{5,7},{6,4},{7,5},{8,10},{9,11},{10,... | collective-permute-start | bytes 786440 | tf_op jit(solution)/shard_map/ppermute | solution.py:284
  18.1 0.5 %collective-permute-start.5 = (bf16[256,512]{1,0:T(8,128)(2,1)S(1)}, bf16[256,512]{1,0:T(8,128)(2,1)S(1)}, u32[]{:S(2)}, u32[]{:S(2)}) collective-permute-start(bf16[256,512]{1,0:T(8,128)(2,1)S(1)} %add_convert_fusion.2.refs_2_), channel_id=1, source_target_pairs={{0,2},{1,3},{2,0},{3,1},{4,6},{5,7},{6,4},{7,5},{8,10},{9,11},{10,... | collective-permute-start | bytes 786440 | tf_op jit(solution)/shard_map/ppermute | solution.py:284
  18.7 0.7 %shard_map.61 = (bf16[256,512]{1,0:T(8,128)(2,1)S(1)}, bf16[256,512]{1,0:T(8,128)(2,1)S(1)}) custom-call(bf16[256,1024]{1,0:T(8,128)(2,1)S(1)} %shard_map.57.refs_0_, bf16[2,2,1024,1024]{3,2,1,0:T(8,128)(2,1)S(1)} %get-tuple-element.24.refs_1_, bf16[256,512]{1,0:T(8,128)(2,1)S(1)} %add_convert_fusion.2.refs_2_), custom_call_target="tpu_custom_call" | custom-call | flops 536870912 | bytes 2097152 | tf_op jit(solution)/shard_map/pallas_call | solution.py:31
  19.4 0.1 collective-permute-start.6
  19.5 0.0 collective-permute-done.4
  19.5 6.3 %collective-permute-done.2 = bf16[256,512]{1,0:T(8,128)(2,1)S(1)} collective-permute-done((bf16[256,512]{1,0:T(8,128)(2,1)S(1)}, bf16[256,512]{1,0:T(8,128)(2,1)S(1)}, u32[]{:S(2)}, u32[]{:S(2)}) %collective-permute-start.2) | collective-permute-done | bytes 262176 | tf_op jit(solution)/shard_map/ppermute | solution.py:284
  25.8 0.1 add_convert_fusion.1
  25.9 5.0 %collective-permute-done.5 = bf16[256,512]{1,0:T(8,128)(2,1)S(1)} collective-permute-done((bf16[256,512]{1,0:T(8,128)(2,1)S(1)}, bf16[256,512]{1,0:T(8,128)(2,1)S(1)}, u32[]{:S(2)}, u32[]{:S(2)}) %collective-permute-start.5) | collective-permute-done | bytes 262176 | tf_op jit(solution)/shard_map/ppermute | solution.py:284
  30.8 0.0 collective-permute-done.6
  30.8 0.1 add_convert_fusion
  30.9 0.9 %pad_maximum_fusion = bf16[256,1024]{1,0:T(8,128)(2,1)} fusion(bf16[256,512]{1,0:T(8,128)(2,1)S(1)} %add_convert_fusion, bf16[256,512]{1,0:T(8,128)(2,1)S(1)} %add_convert_fusion.1), kind=kLoop, calls=%fused_computation | loop fusion | flops 1048576 | bytes 1048576 | tf_op jit(solution)/shard_map/concatenate | solution.py:292
Async XLA Ops:
  1.0 10.6 %collective-permute-start = (bf16[528,256]{1,0:T(8,128)(2,1)S(1)}, bf16[528,256]{1,0:T(8,128)(2,1)S(1)}, u32[]{:S(2)}, u32[]{:S(2)}) collective-permute-start(bf16[528,256]{1,0:T(8,128)(2,1)S(1)} %shard_map.56), channel_id=1, source_target_pairs={{0,4},{4,8},{8,12},{12,16},{16,20},{20,24},{24,28},{1,5},{5,9},{9,... | collective-permute-start | bytes 811016 | tf_op jit(solution)/shard_map/ppermute | solution.py:223
  13.9 1.6 %collective-permute-start.3 = (bf16[256,512]{1,0:T(8,128)(2,1)S(1)}, bf16[256,512]{1,0:T(8,128)(2,1)S(1)}, u32[]{:S(2)}, u32[]{:S(2)}) collective-permute-start(bf16[256,512]{1,0:T(8,128)(2,1)S(1)} %get-tuple-element.28), channel_id=1, source_target_pairs={{0,1},{1,0},{2,3},{3,2},{4,5},{5,4},{6,7},{7,6},{8,9},{9,8},{10,11... | collective-permute-start | bytes 786440 | tf_op jit(solution)/shard_map/ppermute | solution.py:278
  14.7 1.8 %collective-permute-start.1 = (bf16[256,512]{1,0:T(8,128)(2,1)S(1)}, bf16[256,512]{1,0:T(8,128)(2,1)S(1)}, u32[]{:S(2)}, u32[]{:S(2)}) collective-permute-start(bf16[256,512]{1,0:T(8,128)(2,1)S(1)} %get-tuple-element.26), channel_id=1, source_target_pairs={{0,1},{1,0},{2,3},{3,2},{4,5},{5,4},{6,7},{7,6},{8,9},{9,8},{10,11... | collective-permute-start | bytes 786440 | tf_op jit(solution)/shard_map/ppermute | solution.py:278
  16.3 3.2 %collective-permute-start.4 = (bf16[256,512]{1,0:T(8,128)(2,1)S(1)}, bf16[256,512]{1,0:T(8,128)(2,1)S(1)}, u32[]{:S(2)}, u32[]{:S(2)}) collective-permute-start(bf16[256,512]{1,0:T(8,128)(2,1)S(1)} %get-tuple-element.30), channel_id=1, source_target_pairs={{0,1},{1,0},{2,3},{3,2},{4,5},{5,4},{6,7},{7,6},{8,9},{9,8},{10,11... | collective-permute-start | bytes 786440 | tf_op jit(solution)/shard_map/ppermute | solution.py:278
  16.6 9.2 %collective-permute-start.2 = (bf16[256,512]{1,0:T(8,128)(2,1)S(1)}, bf16[256,512]{1,0:T(8,128)(2,1)S(1)}, u32[]{:S(2)}, u32[]{:S(2)}) collective-permute-start(bf16[256,512]{1,0:T(8,128)(2,1)S(1)} %add_convert_fusion.3), channel_id=1, source_target_pairs={{0,2},{1,3},{2,0},{3,1},{4,6},{5,7},{6,4},{7,5},{8,10},{9,11},{10,... | collective-permute-start | bytes 786440 | tf_op jit(solution)/shard_map/ppermute | solution.py:284
  18.1 12.7 %collective-permute-start.5 = (bf16[256,512]{1,0:T(8,128)(2,1)S(1)}, bf16[256,512]{1,0:T(8,128)(2,1)S(1)}, u32[]{:S(2)}, u32[]{:S(2)}) collective-permute-start(bf16[256,512]{1,0:T(8,128)(2,1)S(1)} %add_convert_fusion.2.refs_2_), channel_id=1, source_target_pairs={{0,2},{1,3},{2,0},{3,1},{4,6},{5,7},{6,4},{7,5},{8,10},{9,11},{10,... | collective-permute-start | bytes 786440 | tf_op jit(solution)/shard_map/ppermute | solution.py:284
  19.4 11.5 %collective-permute-start.6 = (bf16[256,512]{1,0:T(8,128)(2,1)S(1)}, bf16[256,512]{1,0:T(8,128)(2,1)S(1)}, u32[]{:S(2)}, u32[]{:S(2)}) collective-permute-start(bf16[256,512]{1,0:T(8,128)(2,1)S(1)} %get-tuple-element.32), channel_id=1, source_target_pairs={{0,1},{1,0},{2,3},{3,2},{4,5},{5,4},{6,7},{7,6},{8,9},{9,8},{10,11... | collective-permute-start | bytes 786440 | tf_op jit(solution)/shard_map/ppermute | solution.py:278

commit v2 on v0

v2 whole, which is shorter than its diff:
```python
import functools
import math

import jax
import jax.numpy as jnp
from jax import lax
from jax.experimental import pallas as pl
from jax.experimental.pallas import tpu as pltpu
from jax.sharding import PartitionSpec as P

HEAD_DIM = 128
CORES = 2
HALVES = 2
DOC_ROWS = 16
LOG2_SCALE = math.log2(math.e) / math.sqrt(HEAD_DIM)
HIDDEN = -1e30
NT = (((1,), (1,)), ((), ()))
VMEM = pl.BlockSpec(memory_space=pltpu.VMEM)
ANY = pl.BlockSpec(memory_space=pl.ANY)
HBM = pl.BlockSpec(memory_space=pltpu.HBM)


def near(x):
    return pltpu.with_memory_space_constraint(x, pltpu.VMEM)


def far(x):
    return pltpu.with_memory_space_constraint(x, pltpu.HBM)


def call(kernel, out_shape, in_specs, args, flops=0, moved=0, vmem_mib=32, scratch=()):
    return pl.pallas_call(
        kernel,
        out_shape=out_shape,
        in_specs=in_specs,
        out_specs=jax.tree.map(lambda _: VMEM, out_shape),
        scratch_shapes=scratch,
        compiler_params=pltpu.CompilerParams(vmem_limit_bytes=vmem_mib * 2**20),
        cost_estimate=pl.CostEstimate(
            flops=flops, bytes_accessed=moved, transcendentals=0
        ),
    )(*args)


def pack_kernel(k_hbm, v_hbm, doc_hbm, out_ref, held, sem):
    halves, size, width = out_ref.shape
    tokens = k_hbm.shape[0]
    rows = tokens // halves
    copies = [pltpu.make_async_copy(doc_hbm, held, sem.at[2 * halves])]
    for half in range(halves):
        for i, source in enumerate((k_hbm, v_hbm)):
            copies.append(
                pltpu.make_async_copy(
                    source.at[half * rows : (half + 1) * rows],
                    out_ref.at[half, i * rows : (i + 1) * rows],
                    sem.at[2 * half + i],
                )
            )
    for copy in copies:
        copy.start()
    copies[0].wait()
    docs = (held[...] + 1).astype(jnp.float32)
    for half in range(halves):
        parts = []
        for at in range(half * rows, (half + 1) * rows, width):
            part = docs[:, at : min(at + width, (half + 1) * rows)]
            if part.shape[1] < width:
                part = jnp.concatenate([part, jnp.zeros((1, width - part.shape[1]))], axis=1)
            parts.append(part)
        parts.append(jnp.zeros((DOC_ROWS - len(parts), width), jnp.float32))
        out_ref[half, 2 * rows :, :] = jnp.concatenate(parts, axis=0).astype(jnp.bfloat16)
    for copy in copies[1:]:
        copy.wait()


def doc_column(docs):
    count = docs.shape[1]
    return jnp.transpose(jnp.broadcast_to(docs, (count, count)))[:, :1]


def stacked(q_ref, r0, rows, first, repeats):
    heads = [
        q_ref[r0 : r0 + rows, h * HEAD_DIM : (h + 1) * HEAD_DIM]
        for h in range(first, first + repeats)
    ]
    return jnp.concatenate(heads, axis=0)


def with_ones(v):
    return jnp.concatenate([v, jnp.ones_like(v)], axis=1)


def hide(scores, bias):
    rows, count = bias.shape
    shape = (scores.shape[0] // rows, rows, count)
    return (scores.reshape(shape) + bias[None]).reshape(scores.shape)


def weights_of(scores, top):
    return jnp.exp2((scores - top) * LOG2_SCALE).astype(jnp.bfloat16)


def key_docs(ref, rows):
    wide = ref[2 * rows :, :].astype(jnp.float32)
    width = ref.shape[1]
    parts = [wide[i : i + 1, : min(width, rows)] for i in range(-(-rows // width))]
    return jnp.concatenate(parts, axis=1)


def attend(half, rows, q_ref, docs, own_k, own_v, prev_refs, att_ref):
    r0, count = half * rows, (half + 1) * rows
    groups = own_k.shape[1] // HEAD_DIM
    repeats = q_ref.shape[1] // HEAD_DIM // groups
    at = r0 + lax.broadcasted_iota(jnp.int32, (rows, count), 0)
    key = lax.broadcasted_iota(jnp.int32, (rows, count), 1)
    column = doc_column(docs)[r0 : r0 + rows]
    masks = [(key <= at) & (docs[:, :count] == column)]
    masks += [key_docs(prev, rows) == column for prev in prev_refs]
    bias = jnp.concatenate([jnp.where(mask, 0.0, HIDDEN) for mask in masks], axis=1)
    for g in range(groups):
        lanes = slice(g * HEAD_DIM, (g + 1) * HEAD_DIM)
        q = stacked(q_ref, r0, rows, g * repeats, repeats)
        k = jnp.concatenate([own_k[:count, lanes]] + [p[:rows, lanes] for p in prev_refs], axis=0)
        v = jnp.concatenate(
            [own_v[:count, lanes]] + [p[rows : 2 * rows, lanes] for p in prev_refs], axis=0
        )
        scores = lax.dot_general(q, k, NT, preferred_element_type=jnp.float32)
        scores = hide(scores, bias)
        top = jnp.max(scores, axis=1, keepdims=True)
        summed = jnp.dot(weights_of(scores, top), with_ones(v), preferred_element_type=jnp.float32)
        result = (summed[:, :HEAD_DIM] / summed[:, HEAD_DIM:]).astype(jnp.bfloat16)
        for r in range(repeats):
            h = g * repeats + r
            att_ref[:, h * HEAD_DIM : (h + 1) * HEAD_DIM] = result[r * rows : (r + 1) * rows]


def owner(d, which):
    chips = lax.axis_size("head") // CORES
    me = lax.axis_index("head")
    chip, core = me // CORES, me % CORES
    return lax.rem(chip + d, chips) * CORES + lax.rem(core + which, CORES)


def project(att, w_ref, d, which, out_ref):
    block = w_ref.shape[1] // lax.axis_size("head")
    start = pl.multiple_of(owner(d, which) * block, block)
    out_ref[...] = jnp.dot(
        att, w_ref[:, pl.ds(start, block)], preferred_element_type=jnp.float32
    ).astype(jnp.bfloat16)


def give_kernel(half, chips, q_ref, k_ref, v_ref, doc_ref, w_ref, *rest):
    outs = rest[-chips:]
    att_ref, gives = outs[0], outs[1:]
    prev_refs = rest[:-chips]
    if half < HALVES - 1:
        prev_refs = prev_refs[1:]
    rows = q_ref.shape[0] // HALVES
    docs = doc_ref[...].astype(jnp.float32) + 1.0
    attend(half, rows, q_ref, docs, k_ref, v_ref, prev_refs, att_ref)
    att = att_ref[...]
    for d in range(1, chips):
        project(att, w_ref, d, 1, gives[d - 1])


def keep_kernel(first, att_ref, w_ref, *outs):
    att = att_ref[...]
    for i, out_ref in enumerate(outs):
        project(att, w_ref, first + i, 0, out_ref)


def local_kernel(low_ref, high_ref, w_ref, after, give_ref, att_ref):
    rows = low_ref.shape[0]
    att_ref[:rows] = low_ref[...]
    att_ref[rows:] = high_ref[...]
    project(att_ref[...], w_ref, 0, 1, give_ref)


def sum_kernel(keep_ref, got_ref, out_ref):
    total = keep_ref[...].astype(jnp.float32) + got_ref[...].astype(jnp.float32)
    out_ref[...] = total.astype(out_ref.dtype)


def final_kernel(half, local_ref, *rest):
    out_hbm, held, sem = rest[-3:]
    arrived = rest[:-3] if half == HALVES - 1 else rest[:-4]
    rows = held.shape[0]
    here = pl.ds(half * rows, rows)
    total = local_ref[here, :]
    for got in arrived:
        total = total + got[...].astype(jnp.float32)
    held[...] = total.astype(jnp.bfloat16)
    copy = pltpu.make_async_copy(held, out_hbm.at[here], sem)
    copy.start()
    copy.wait()


def body(queries, keys, values, segment_ids, out_weight):
    tokens, width = queries.shape
    kv_width = keys.shape[1]
    place_count = lax.axis_size("ctx")
    devices = lax.axis_size("head")
    chips = devices // CORES
    columns = out_weight.shape[1]
    block = columns // devices
    span = max(place_count // 16, 2)
    part = tokens // HALVES
    bf16, f32 = jnp.bfloat16, jnp.float32
    dma = pltpu.SemaphoreType.DMA

    doc_row = segment_ids.reshape(1, tokens)
    packed = call(
        pack_kernel,
        pltpu.VMEM((HALVES, 2 * part + DOC_ROWS, kv_width), bf16),
        [HBM] * 3,
        (far(keys), far(values), far(doc_row)),
        flops=2**33,
        scratch=[pltpu.VMEM((1, tokens), jnp.int32), dma((2 * HALVES + 1,))],
    )
    late, early = [], []
    for s in range(1, span):
        pairs = [(i, i + s) for i in range(place_count - s)]
        late.append(lax.ppermute(packed[1], "ctx", pairs))
        early.append(lax.ppermute(packed[0], "ctx", pairs))

    other_core = [(i, i ^ 1) for i in range(devices)]

    def keep_shares(att, first, count):
        keep = pltpu.VMEM((att.shape[0], block), bf16)
        return call(
            functools.partial(keep_kernel, first),
            [keep] * count,
            [VMEM] * 2,
            (near(att), out_weight),
            flops=2**33,
        )

    def add(keep, got, dtype):
        return call(
            sum_kernel, pltpu.VMEM(keep.shape, dtype), [VMEM] * 2, (near(keep), near(got))
        )

    def shares(half, prevs, *after):
        att, *gives = call(
            functools.partial(give_kernel, half, chips),
            [pltpu.VMEM((part, width), bf16)] + [pltpu.VMEM((part, block), bf16)] * (chips - 1),
            [VMEM] * 5 + [ANY] * len(after) + [VMEM] * len(prevs),
            (queries, keys, values, doc_row, out_weight, *after, *map(near, prevs)),
            flops=8 * tokens * width * block,
        )
        keeps = keep_shares(att, 1, chips - 1)
        sums, arrived = [], []
        for d in range(1, chips):
            total = add(keeps[d - 1], lax.ppermute(gives[d - 1], "head", other_core), bf16)
            pairs = [(i, (i + d * CORES) % devices) for i in range(devices)]
            sums.append(total)
            arrived.append(lax.ppermute(total, "head", pairs))
        return att, sums, arrived

    att_high, sums, high = shares(HALVES - 1, early[:-1] + late)
    att_low, sums, low = shares(0, early + late, sums[-1])

    give, att = call(
        local_kernel,
        [pltpu.VMEM((tokens, block), bf16), pltpu.VMEM((tokens, width), bf16)],
        [VMEM] * 3 + [ANY],
        (near(att_low), near(att_high), out_weight, high[-1]),
        flops=4 * tokens * width * block,
    )
    (keep,) = keep_shares(att, 0, 1)
    local = add(keep, lax.ppermute(give, "head", other_core), f32)

    def finish(half, arrived, *out):
        return pl.pallas_call(
            functools.partial(final_kernel, half),
            out_shape=pltpu.HBM((tokens, block), bf16),
            in_specs=[VMEM] * (1 + len(arrived)) + [HBM] * len(out),
            out_specs=HBM,
            scratch_shapes=[pltpu.VMEM((part, block), bf16), dma],
            input_output_aliases={1 + len(arrived): 0} if out else {},
            cost_estimate=pl.CostEstimate(flops=0, bytes_accessed=0, transcendentals=0),
        )(near(local), *map(near, arrived), *out)

    return finish(0, low, finish(HALVES - 1, high))


def solution(mesh):
    in_specs = (P("ctx", "head"), P("ctx", "head"), P("ctx", "head"), P("ctx"), P("head", None))
    out_specs = P("ctx", "head")
    return jax.shard_map(body, mesh=mesh, in_specs=in_specs, out_specs=out_specs, check_vma=False)
```

time: 70.8 us -> 28 us (0.40)
  waiting for transfers between devices: 35.8 us -> 8.42 us
  between operations: 13.6 us -> 0.18 us
  Pallas kernels: 0 us -> 8.14 us
  matrix products: 5.98 us -> 0 us
  local copies, waits for them, and re-layouts: 5.54 us -> 0.04 us
  starting transfers between devices: 8.44 us -> 11 us
  other arithmetic: 1.25 us -> 0 us
    reduce_scatter x1 -> x0, waiting for transfers between devices: 33.8 us -> none  [body(): lax.psum_scatter(partial_out.astype(jnp.bfloat16), 'head', scatter_dimens...]
    pallas_call x0 -> x12, Pallas kernels: none -> 8.14 us  [the longest x10 6.63 us: call(): pl.pallas_call(kernel, out_shape=out_shape, in_specs=in_specs, out_specs=...]
    ppermute x2 -> x7, waiting for transfers between devices: 2.01 us -> 8.42 us  [the longest x2 5.19 us: shares(): arrived.append(lax.ppermute(total, 'head', pairs))]
    dot_general x5 -> x0, matrix products: 5.98 us -> none  [the longest x1 3.72 us: body(): jnp.dot(attended, out_weight, preferred_element_type=jnp.float32)]
    ppermute x2 -> x7, starting transfers between devices: 8.43 us -> 11 us  [the longest x1 5.16 us: body(): late.append(lax.ppermute(packed[1], 'ctx', pairs))]
    unnamed x7 -> x10, local copies, waits for them, and re-layouts: 2.17 us -> 0.02 us
    another operation x2 -> x0, local copies, waits for them, and re-layouts: 1.94 us -> none  [the longest x1 1 us: absorb(): valset = packed[1].reshape(count, kv_local, HEAD_DIM)]
    reshape x1 -> x0, local copies, waits for them, and re-layouts: 1.41 us -> none  [body(): grouped = queries.reshape(tokens, kv_local, repeats, HEAD_DIM)]
  transfers between devices with their start and end apart: 3 -> 7, of which waited for: 2 -> 5; matrix products, arithmetic and copies ran while one was open for 7% -> 0% of each run, Pallas kernels for 0% -> 23%
where the time goes in v2:
time: 28 us; the launch traced here: 27.7 us
  starting transfers between devices  11 us (39%)
  waiting for transfers between devices  8.42 us (30%)
  Pallas kernels  8.14 us (29%)
    pallas_call x10, Pallas kernels, call(): pl.pallas_call(kernel, out_shape=out_shape, in_specs=in_specs, out_specs=...  6.63 us
    ppermute x2, waiting for transfers between devices, shares(): arrived.append(lax.ppermute(total, 'head', pairs))  5.19 us
    ppermute x1, starting transfers between devices, body(): late.append(lax.ppermute(packed[1], 'ctx', pairs))  5.16 us
    ppermute x1, starting transfers between devices, body(): early.append(lax.ppermute(packed[0], 'ctx', pairs))  3.43 us
    ppermute x2, starting transfers between devices, shares(): arrived.append(lax.ppermute(total, 'head', pairs))  2.16 us
    ppermute x2, waiting for transfers between devices, shares(): lax.ppermute(gives[d - 1], 'head', other_core)  2.08 us
    pallas_call x2, Pallas kernels, finish(): pl.pallas_call(functools.partial(final_kernel, half), out_shape=pltpu.HBM...  1.52 us
    ppermute x1, waiting for transfers between devices, body(): local = add(keep, lax.ppermute(give, 'head', other_core), f32)  1.15 us
  transfers between devices with their start and end apart: 7, of which 5 were waited for; matrix products, arithmetic and copies ran while one was open for 0% of the time, Pallas kernels for 23%

profile of v2, /device:TPU:0, one launch (start us, length us, event | category | flops | bytes accessed | tf_op | source)
XLA Modules:
  0.0 27.7 jit_solution(2694755670467633197)
XLA Ops:
  0.0 0.0 copy-start
  0.0 1.1 %shard_map.55 = bf16[2,272,256]{2,1,0:T(8,128)(2,1)S(1)} custom-call(bf16[256,256]{1,0:T(8,128)(2,1)} %k_ref.3, bf16[256,256]{1,0:T(8,128)(2,1)} %v_ref.3, s32[1,256]{1,0:T(1,128)} %bitcast.5), custom_call_target="tpu_custom_call" | custom-call | flops 8589934592 | tf_op jit(solution)/shard_map/pallas_call | solution.py:32
  1.2 5.2 %collective-permute-start = (bf16[272,256]{1,0:T(8,128)(2,1)S(1)}, bf16[272,256]{1,0:T(8,128)(2,1)S(1)}, u32[]{:S(2)}, u32[]{:S(2)}) collective-permute-start(bf16[272,256]{1,0:T(8,128)(2,1)S(1)} %get-tuple-element.18), channel_id=1, source_target_pairs={{0,4},{4,8},{8,12},{12,16},{16,20},{20,24},{24,28},{1,5},{5,9},{9,... | collective-permute-start | bytes 417800 | tf_op jit(solution)/shard_map/ppermute | solution.py:223
  6.4 3.4 %collective-permute-start.2 = (bf16[272,256]{1,0:T(8,128)(2,1)S(1)}, bf16[272,256]{1,0:T(8,128)(2,1)S(1)}, u32[]{:S(2)}, u32[]{:S(2)}) collective-permute-start(bf16[272,256]{1,0:T(8,128)(2,1)S(1)} %get-tuple-element.17), channel_id=1, source_target_pairs={{0,4},{4,8},{8,12},{12,16},{16,20},{20,24},{24,28},{1,5},{5,9},{9,... | collective-permute-start | bytes 417800 | tf_op jit(solution)/shard_map/ppermute | solution.py:224
  9.8 0.0 collective-permute-done.rest_0_.rest_2_
  9.8 0.0 copy-done
  9.8 0.0 copy-done.1
  9.8 0.0 copy-done.2
  9.8 0.0 copy-done.3
  9.8 0.0 copy-done.4
  9.9 1.4 %shard_map.56 = (bf16[128,1024]{1,0:T(8,128)(2,1)S(1)}, bf16[128,1024]{1,0:T(8,128)(2,1)S(1)}) custom-call(bf16[256,1024]{1,0:T(8,128)(2,1)S(1)} %copy-done.1, bf16[256,256]{1,0:T(8,128)(2,1)S(1)} %copy-done.2, bf16[256,256]{1,0:T(8,128)(2,1)S(1)} %copy-done.3, s32[1,256]{1,0:T(1,128)S(1)} %bitcast.6, bf16[1024,4096]{1,0:T(8,128)(2,1)S(1)} %copy-done, ...), custom_call_target="tpu_custom_call" | custom-call | flops 2147483648 | tf_op jit(solution)/shard_map/pallas_call | solution.py:32
  11.3 0.1 collective-permute-start.1
  11.4 0.5 %shard_map.57.keep_ref = bf16[128,1024]{1,0:T(8,128)(2,1)S(1)} custom-call(bf16[128,1024]{1,0:T(8,128)(2,1)S(1)} %get-tuple-element.11.att_ref.high_ref, bf16[1024,4096]{1,0:T(8,128)(2,1)S(1)} %copy-done), custom_call_target="tpu_custom_call" | custom-call | flops 8589934592 | tf_op jit(solution)/shard_map/pallas_call | solution.py:32
  11.8 1.0 %collective-permute-done.1.got_ref = bf16[128,1024]{1,0:T(8,128)(2,1)S(1)} collective-permute-done((bf16[128,1024]{1,0:T(8,128)(2,1)S(1)}, bf16[128,1024]{1,0:T(8,128)(2,1)S(1)}, u32[]{:S(2)}, u32[]{:S(2)}) %collective-permute-start.1) | collective-permute-done | bytes 262176 | tf_op jit(solution)/shard_map/ppermute | solution.py:254
  12.9 0.1 shard_map.58.rest_0_
  12.9 1.6 %collective-permute-start.3 = (bf16[128,1024]{1,0:T(8,128)(2,1)S(1)}, bf16[128,1024]{1,0:T(8,128)(2,1)S(1)}, u32[]{:S(2)}, u32[]{:S(2)}) collective-permute-start(bf16[128,1024]{1,0:T(8,128)(2,1)S(1)} %shard_map.58.rest_0_), channel_id=1, source_target_pairs={{0,2},{1,3},{2,0},{3,1},{4,6},{5,7},{6,4},{7,5},{8,10},{9,11},{10,... | collective-permute-start | bytes 786440 | tf_op jit(solution)/shard_map/ppermute | solution.py:257
  14.5 0.0 collective-permute-done.2.rest_1_
  14.5 1.4 %shard_map.59 = (bf16[128,1024]{1,0:T(8,128)(2,1)S(1)}, bf16[128,1024]{1,0:T(8,128)(2,1)S(1)}) custom-call(bf16[256,1024]{1,0:T(8,128)(2,1)S(1)} %copy-done.1, bf16[256,256]{1,0:T(8,128)(2,1)S(1)} %copy-done.2, bf16[256,256]{1,0:T(8,128)(2,1)S(1)} %copy-done.3, s32[1,256]{1,0:T(1,128)S(1)} %bitcast.7, bf16[1024,4096]{1,0:T(8,128)(2,1)S(1)} %copy-done, ...), custom_call_target="tpu_custom_call" | custom-call | flops 2147483648 | tf_op jit(solution)/shard_map/pallas_call | solution.py:32
  15.9 0.1 collective-permute-start.5
  16.0 0.5 %shard_map.63.keep_ref = bf16[128,1024]{1,0:T(8,128)(2,1)S(1)} custom-call(bf16[128,1024]{1,0:T(8,128)(2,1)S(1)} %get-tuple-element.13.low_ref.att_ref, bf16[1024,4096]{1,0:T(8,128)(2,1)S(1)} %copy-done), custom_call_target="tpu_custom_call" | custom-call | flops 8589934592 | tf_op jit(solution)/shard_map/pallas_call | solution.py:32
  16.5 1.0 %collective-permute-done.5.got_ref = bf16[128,1024]{1,0:T(8,128)(2,1)S(1)} collective-permute-done((bf16[128,1024]{1,0:T(8,128)(2,1)S(1)}, bf16[128,1024]{1,0:T(8,128)(2,1)S(1)}, u32[]{:S(2)}, u32[]{:S(2)}) %collective-permute-start.5) | collective-permute-done | bytes 262176 | tf_op jit(solution)/shard_map/ppermute | solution.py:254
  17.5 0.1 shard_map.64
  17.6 0.6 %collective-permute-start.6 = (bf16[128,1024]{1,0:T(8,128)(2,1)S(1)}, bf16[128,1024]{1,0:T(8,128)(2,1)S(1)}, u32[]{:S(2)}, u32[]{:S(2)}) collective-permute-start(bf16[128,1024]{1,0:T(8,128)(2,1)S(1)} %shard_map.64), channel_id=1, source_target_pairs={{0,2},{1,3},{2,0},{3,1},{4,6},{5,7},{6,4},{7,5},{8,10},{9,11},{10,... | collective-permute-start | bytes 786440 | tf_op jit(solution)/shard_map/ppermute | solution.py:257
  18.2 4.0 %collective-permute-done.3.after.rest_0_ = bf16[128,1024]{1,0:T(8,128)(2,1)S(1)} collective-permute-done((bf16[128,1024]{1,0:T(8,128)(2,1)S(1)}, bf16[128,1024]{1,0:T(8,128)(2,1)S(1)}, u32[]{:S(2)}, u32[]{:S(2)}) %collective-permute-start.3) | collective-permute-done | bytes 262176 | tf_op jit(solution)/shard_map/ppermute | solution.py:257
  22.2 0.7 %shard_map.60 = (bf16[256,1024]{1,0:T(8,128)(2,1)S(1)}, bf16[256,1024]{1,0:T(8,128)(2,1)S(1)}) custom-call(bf16[128,1024]{1,0:T(8,128)(2,1)S(1)} %get-tuple-element.13.low_ref.att_ref, bf16[128,1024]{1,0:T(8,128)(2,1)S(1)} %get-tuple-element.11.att_ref.high_ref, bf16[1024,4096]{1,0:T(8,128)(2,1)S(1)} %copy-done, ...), custom_call_target="tpu_custom_call" | custom-call | flops 1073741824 | tf_op jit(solution)/shard_map/pallas_call | solution.py:32
  22.9 0.1 collective-permute-start.4
  23.0 0.7 %shard_map.61.keep_ref = bf16[256,1024]{1,0:T(8,128)(2,1)S(1)} custom-call(bf16[256,1024]{1,0:T(8,128)(2,1)S(1)} %get-tuple-element.14.att_ref, bf16[1024,4096]{1,0:T(8,128)(2,1)S(1)} %copy-done), custom_call_target="tpu_custom_call" | custom-call | flops 8589934592 | tf_op jit(solution)/shard_map/pallas_call | solution.py:32
  23.7 1.2 %collective-permute-done.4.got_ref = bf16[256,1024]{1,0:T(8,128)(2,1)S(1)} collective-permute-done((bf16[256,1024]{1,0:T(8,128)(2,1)S(1)}, bf16[256,1024]{1,0:T(8,128)(2,1)S(1)}, u32[]{:S(2)}, u32[]{:S(2)}) %collective-permute-start.4) | collective-permute-done | bytes 524320 | tf_op jit(solution)/shard_map/ppermute | solution.py:271
  24.9 0.1 shard_map.62.local_ref
  25.0 0.8 %shard_map.65.rest_1_ = bf16[256,1024]{1,0:T(8,128)(2,1)} custom-call(f32[256,1024]{1,0:T(8,128)S(1)} %shard_map.62.local_ref, bf16[128,1024]{1,0:T(8,128)(2,1)S(1)} %collective-permute-done.3.after.rest_0_), custom_call_target="tpu_custom_call" | custom-call | tf_op jit(solution)/shard_map/pallas_call | solution.py:274
  25.8 1.2 %collective-permute-done.6.rest_0_ = bf16[128,1024]{1,0:T(8,128)(2,1)S(1)} collective-permute-done((bf16[128,1024]{1,0:T(8,128)(2,1)S(1)}, bf16[128,1024]{1,0:T(8,128)(2,1)S(1)}, u32[]{:S(2)}, u32[]{:S(2)}) %collective-permute-start.6) | collective-permute-done | bytes 262176 | tf_op jit(solution)/shard_map/ppermute | solution.py:257
  27.0 0.8 %shard_map.66 = bf16[256,1024]{1,0:T(8,128)(2,1)} custom-call(f32[256,1024]{1,0:T(8,128)S(1)} %shard_map.62.local_ref, bf16[128,1024]{1,0:T(8,128)(2,1)S(1)} %collective-permute-done.6.rest_0_, bf16[256,1024]{1,0:T(8,128)(2,1)} %shard_map.65.rest_1_), custom_call_target="tpu_custom_call", output_to_operand_aliasing={{}: (2, {})} | custom-call | tf_op jit(solution)/shard_map/pallas_call | solution.py:274
  (5 shorter events, 0.0 us)
Async XLA Ops:
  0.0 9.8 %copy-start = (bf16[1024,4096]{1,0:T(8,128)(2,1)S(1)}, bf16[1024,4096]{1,0:T(8,128)(2,1)}, u32[]{:S(2)}) copy-start(bf16[1024,4096]{1,0:T(8,128)(2,1)} %w_ref.11) | copy-start | bytes 25165828
  0.0 9.8 %copy-start.1 = (bf16[256,1024]{1,0:T(8,128)(2,1)S(1)}, bf16[256,1024]{1,0:T(8,128)(2,1)}, u32[]{:S(2)}) copy-start(bf16[256,1024]{1,0:T(8,128)(2,1)} %q_ref.3) | copy-start | bytes 1572868
  0.0 9.8 %copy-start.2 = (bf16[256,256]{1,0:T(8,128)(2,1)S(1)}, bf16[256,256]{1,0:T(8,128)(2,1)}, u32[]{:S(2)}) copy-start(bf16[256,256]{1,0:T(8,128)(2,1)} %k_ref.3) | copy-start | bytes 393220
  0.0 9.8 %copy-start.3 = (bf16[256,256]{1,0:T(8,128)(2,1)S(1)}, bf16[256,256]{1,0:T(8,128)(2,1)}, u32[]{:S(2)}) copy-start(bf16[256,256]{1,0:T(8,128)(2,1)} %v_ref.3) | copy-start | bytes 393220
  0.0 9.8 %copy-start.4 = (s32[256]{0:T(256)S(1)}, s32[256]{0:T(256)}, u32[]{:S(2)}) copy-start(s32[256]{0:T(256)} %param.8) | copy-start | bytes 3076
  1.2 8.6 %collective-permute-start = (bf16[272,256]{1,0:T(8,128)(2,1)S(1)}, bf16[272,256]{1,0:T(8,128)(2,1)S(1)}, u32[]{:S(2)}, u32[]{:S(2)}) collective-permute-start(bf16[272,256]{1,0:T(8,128)(2,1)S(1)} %get-tuple-element.18), channel_id=1, source_target_pairs={{0,4},{4,8},{8,12},{12,16},{16,20},{20,24},{24,28},{1,5},{5,9},{9,... | collective-permute-start | bytes 417800 | tf_op jit(solution)/shard_map/ppermute | solution.py:223
  6.4 8.1 %collective-permute-start.2 = (bf16[272,256]{1,0:T(8,128)(2,1)S(1)}, bf16[272,256]{1,0:T(8,128)(2,1)S(1)}, u32[]{:S(2)}, u32[]{:S(2)}) collective-permute-start(bf16[272,256]{1,0:T(8,128)(2,1)S(1)} %get-tuple-element.17), channel_id=1, source_target_pairs={{0,4},{4,8},{8,12},{12,16},{16,20},{20,24},{24,28},{1,5},{5,9},{9,... | collective-permute-start | bytes 417800 | tf_op jit(solution)/shard_map/ppermute | solution.py:224
  11.3 1.6 %collective-permute-start.1 = (bf16[128,1024]{1,0:T(8,128)(2,1)S(1)}, bf16[128,1024]{1,0:T(8,128)(2,1)S(1)}, u32[]{:S(2)}, u32[]{:S(2)}) collective-permute-start(bf16[128,1024]{1,0:T(8,128)(2,1)S(1)} %get-tuple-element.12), channel_id=1, source_target_pairs={{0,1},{1,0},{2,3},{3,2},{4,5},{5,4},{6,7},{7,6},{8,9},{9,8},{10,11... | collective-permute-start | bytes 786440 | tf_op jit(solution)/shard_map/ppermute | solution.py:254
  12.9 9.2 %collective-permute-start.3 = (bf16[128,1024]{1,0:T(8,128)(2,1)S(1)}, bf16[128,1024]{1,0:T(8,128)(2,1)S(1)}, u32[]{:S(2)}, u32[]{:S(2)}) collective-permute-start(bf16[128,1024]{1,0:T(8,128)(2,1)S(1)} %shard_map.58.rest_0_), channel_id=1, source_target_pairs={{0,2},{1,3},{2,0},{3,1},{4,6},{5,7},{6,4},{7,5},{8,10},{9,11},{10,... | collective-permute-start | bytes 786440 | tf_op jit(solution)/shard_map/ppermute | solution.py:257
  15.9 1.6 %collective-permute-start.5 = (bf16[128,1024]{1,0:T(8,128)(2,1)S(1)}, bf16[128,1024]{1,0:T(8,128)(2,1)S(1)}, u32[]{:S(2)}, u32[]{:S(2)}) collective-permute-start(bf16[128,1024]{1,0:T(8,128)(2,1)S(1)} %get-tuple-element.16), channel_id=1, source_target_pairs={{0,1},{1,0},{2,3},{3,2},{4,5},{5,4},{6,7},{7,6},{8,9},{9,8},{10,11... | collective-permute-start | bytes 786440 | tf_op jit(solution)/shard_map/ppermute | solution.py:254
  17.6 9.4 %collective-permute-start.6 = (bf16[128,1024]{1,0:T(8,128)(2,1)S(1)}, bf16[128,1024]{1,0:T(8,128)(2,1)S(1)}, u32[]{:S(2)}, u32[]{:S(2)}) collective-permute-start(bf16[128,1024]{1,0:T(8,128)(2,1)S(1)} %shard_map.64), channel_id=1, source_target_pairs={{0,2},{1,3},{2,0},{3,1},{4,6},{5,7},{6,4},{7,5},{8,10},{9,11},{10,... | collective-permute-start | bytes 786440 | tf_op jit(solution)/shard_map/ppermute | solution.py:257
  22.9 2.0 %collective-permute-start.4 = (bf16[256,1024]{1,0:T(8,128)(2,1)S(1)}, bf16[256,1024]{1,0:T(8,128)(2,1)S(1)}, u32[]{:S(2)}, u32[]{:S(2)}) collective-permute-start(bf16[256,1024]{1,0:T(8,128)(2,1)S(1)} %get-tuple-element.15), channel_id=1, source_target_pairs={{0,1},{1,0},{2,3},{3,2},{4,5},{5,4},{6,7},{7,6},{8,9},{9,8},{10,11... | collective-permute-start | bytes 1572872 | tf_op jit(solution)/shard_map/ppermute | solution.py:271

commit v3 on v2

v3 whole, which is shorter than its diff:
```python
import functools
import math

import jax
import jax.numpy as jnp
from jax import lax
from jax.experimental import pallas as pl
from jax.experimental.pallas import tpu as pltpu
from jax.sharding import PartitionSpec as P

HEAD_DIM = 128
CORES = 2
CUT = 144 / 256
DOC_ROWS = 16
LOG2_SCALE = math.log2(math.e) / math.sqrt(HEAD_DIM)
HIDDEN = -1e30
NT = (((1,), (1,)), ((), ()))
VMEM = pl.BlockSpec(memory_space=pltpu.VMEM)
ANY = pl.BlockSpec(memory_space=pl.ANY)
HBM = pl.BlockSpec(memory_space=pltpu.HBM)


def near(x):
    return pltpu.with_memory_space_constraint(x, pltpu.VMEM)


def far(x):
    return pltpu.with_memory_space_constraint(x, pltpu.HBM)


def call(kernel, out_shape, in_specs, args, flops=0, moved=0, vmem_mib=32, scratch=()):
    return pl.pallas_call(
        kernel,
        out_shape=out_shape,
        in_specs=in_specs,
        out_specs=jax.tree.map(lambda _: VMEM, out_shape),
        scratch_shapes=scratch,
        compiler_params=pltpu.CompilerParams(vmem_limit_bytes=vmem_mib * 2**20),
        cost_estimate=pl.CostEstimate(
            flops=flops, bytes_accessed=moved, transcendentals=0
        ),
    )(*args)


def pack_kernel(k_hbm, v_hbm, doc_hbm, high_ref, held, sem):
    tokens, width = k_hbm.shape
    rows = (high_ref.shape[0] - DOC_ROWS) // 2
    copies = [pltpu.make_async_copy(doc_hbm, held, sem.at[2])]
    for i, source in enumerate((k_hbm, v_hbm)):
        copies.append(
            pltpu.make_async_copy(
                source.at[tokens - rows :], high_ref.at[i * rows : (i + 1) * rows], sem.at[i]
            )
        )
    for copy in copies:
        copy.start()
    copies[0].wait()
    docs = (held[...] + 1).astype(jnp.float32)
    parts = [docs[:, at : at + width] for at in range(0, tokens, width)]
    parts.append(jnp.zeros((DOC_ROWS - len(parts), width), jnp.float32))
    high_ref[2 * rows :, :] = jnp.concatenate(parts, axis=0).astype(jnp.bfloat16)
    for copy in copies[1:]:
        copy.wait()


def stacked(q_ref, r0, rows, first, repeats):
    heads = [
        q_ref[r0 : r0 + rows, h * HEAD_DIM : (h + 1) * HEAD_DIM]
        for h in range(first, first + repeats)
    ]
    return jnp.concatenate(heads, axis=0)


def with_ones(v):
    return jnp.concatenate([v, jnp.ones_like(v)], axis=1)


def hide(scores, bias):
    rows, count = bias.shape
    shape = (scores.shape[0] // rows, rows, count)
    return (scores.reshape(shape) + bias[None]).reshape(scores.shape)


def weights_of(scores, top):
    return jnp.exp2((scores - top) * LOG2_SCALE).astype(jnp.bfloat16)


def key_docs(high_ref, tokens):
    wide = high_ref[high_ref.shape[0] - DOC_ROWS :, :].astype(jnp.float32)
    parts = [wide[i : i + 1, :] for i in range(tokens // high_ref.shape[1])]
    return jnp.concatenate(parts, axis=1)


def attend(first, q_ref, bias_ref, column_ref, own_k, own_v, highs, lows, att_ref):
    tokens = q_ref.shape[0]
    rows = att_ref.shape[0]
    count = first + rows
    groups = own_k.shape[1] // HEAD_DIM
    repeats = q_ref.shape[1] // HEAD_DIM // groups
    column = column_ref[first:count, :]
    biases, keys, values = [], [], []
    for high, low in zip(highs, lows):
        n = (high.shape[0] - DOC_ROWS) // 2
        seen = tokens if low is not None else n
        if low is not None:
            keys.append(low[: tokens - n, :])
            values.append(low[tokens - n :, :])
        keys.append(high[:n, :])
        values.append(high[n : 2 * n, :])
        same = key_docs(high, tokens)[:, tokens - seen :] == column[:, :seen]
        biases.append(jnp.where(same, 0.0, HIDDEN))
    place = 0 if first else len(biases)
    biases.insert(place, bias_ref[first:count, :count])
    keys.insert(place * 2, own_k[:count, :])
    values.insert(place * 2, own_v[:count, :])
    bias = jnp.concatenate(biases, axis=1)
    all_keys = jnp.concatenate(keys, axis=0)
    all_values = jnp.concatenate(values, axis=0)
    lanes = [slice(g * HEAD_DIM, (g + 1) * HEAD_DIM) for g in range(groups)]
    queries = [stacked(q_ref, first, rows, g * repeats, repeats) for g in range(groups)]
    scores = [
        lax.dot_general(q, all_keys[:, at], NT, preferred_element_type=jnp.float32)
        for q, at in zip(queries, lanes)
    ]
    scores = [hide(s, bias) for s in scores]
    tops = [jnp.max(s, axis=1, keepdims=True) for s in scores]
    weights = [weights_of(s, top) for s, top in zip(scores, tops)]
    summed = [
        jnp.dot(w, with_ones(all_values[:, at]), preferred_element_type=jnp.float32)
        for w, at in zip(weights, lanes)
    ]
    for g in range(groups):
        result = (summed[g][:, :HEAD_DIM] / summed[g][:, HEAD_DIM:]).astype(jnp.bfloat16)
        for r in range(repeats):
            h = g * repeats + r
            att_ref[:, h * HEAD_DIM : (h + 1) * HEAD_DIM] = result[r * rows : (r + 1) * rows]


def mask_kernel(k_ref, v_ref, doc_ref, low_ref, bias_ref, column_ref):
    tokens = doc_ref.shape[1]
    cut = low_ref.shape[0] // 2
    low_ref[:cut] = k_ref[:cut]
    low_ref[cut:] = v_ref[:cut]
    docs = jnp.broadcast_to(doc_ref[...].astype(jnp.float32) + 1.0, (tokens, tokens))
    columns = jnp.transpose(docs)
    at = lax.broadcasted_iota(jnp.int32, (tokens, tokens), 0)
    key = lax.broadcasted_iota(jnp.int32, (tokens, tokens), 1)
    bias_ref[...] = jnp.where((key <= at) & (docs == columns), 0.0, HIDDEN)
    column_ref[...] = columns


def owner(d, which):
    chips = lax.axis_size("head") // CORES
    me = lax.axis_index("head")
    chip, core = me // CORES, me % CORES
    return lax.rem(chip + d, chips) * CORES + lax.rem(core + which, CORES)


def project(att, w_ref, d, which, out_ref):
    block = w_ref.shape[1] // lax.axis_size("head")
    start = pl.multiple_of(owner(d, which) * block, block)
    out_ref[...] = jnp.dot(
        att, w_ref[:, pl.ds(start, block)], preferred_element_type=jnp.float32
    ).astype(jnp.bfloat16)


def give_kernel(
    first, chips, n_high, n_low, q_ref, k_ref, v_ref, bias_ref, column_ref, w_ref, *rest
):
    outs = rest[-chips:]
    att_ref, gives = outs[0], outs[1:]
    highs, lows = list(rest[:n_high]), list(rest[n_high : n_high + n_low])
    lows += [None] * (n_high - n_low)
    here = lax.axis_index("ctx")

    def shares(highs, lows):
        attend(first, q_ref, bias_ref, column_ref, k_ref, v_ref, highs, lows, att_ref)
        att = att_ref[...]
        for d in range(1, chips):
            project(att, w_ref, d, 1, gives[d - 1])

    pl.when(here == 0)(lambda: shares([], []))
    pl.when(here > 0)(lambda: shares(highs, lows))


def keep_kernel(first, att_ref, w_ref, *outs):
    att = att_ref[...]
    for i, out_ref in enumerate(outs):
        project(att, w_ref, first + i, 0, out_ref)


def local_kernel(low_ref, high_ref, w_ref, after, att_ref, *gives):
    rows = low_ref.shape[0]
    att_ref[:rows] = low_ref[...]
    att_ref[rows:] = high_ref[...]
    block = w_ref.shape[1] // lax.axis_size("head")
    cols = block // len(gives)
    for i, give_ref in enumerate(gives):
        start = pl.multiple_of(owner(0, 1) * block + i * cols, cols)
        give_ref[...] = jnp.dot(
            att_ref[...], w_ref[:, pl.ds(start, cols)], preferred_element_type=jnp.float32
        ).astype(jnp.bfloat16)


def sum_kernel(keep_ref, *rest):
    out_ref, at = rest[-1], 0
    for got in rest[:-1]:
        lanes = slice(at, at + got.shape[1])
        total = keep_ref[:, lanes].astype(jnp.float32) + got[...].astype(jnp.float32)
        out_ref[:, lanes] = total.astype(out_ref.dtype)
        at += got.shape[1]


def final_kernel(first, count, local_ref, *rest):
    out_hbm, held, sem = rest[-3:]
    here = pl.ds(first, held.shape[0])
    total = local_ref[here, :]
    for got in rest[:count]:
        total = total + got[...].astype(jnp.float32)
    held[...] = total.astype(jnp.bfloat16)
    copy = pltpu.make_async_copy(held, out_hbm.at[here], sem)
    copy.start()
    copy.wait()


def body(queries, keys, values, segment_ids, out_weight):
    tokens, width = queries.shape
    kv_width = keys.shape[1]
    place_count = lax.axis_size("ctx")
    devices = lax.axis_size("head")
    chips = devices // CORES
    columns = out_weight.shape[1]
    block = columns // devices
    span = max(place_count // 16, 2)
    cut = int(tokens * CUT)
    bf16, f32 = jnp.bfloat16, jnp.float32
    dma = pltpu.SemaphoreType.DMA

    doc_row = segment_ids.reshape(1, tokens)
    groups = kv_width // HEAD_DIM
    packed_high = call(
        pack_kernel,
        pltpu.VMEM((2 * (tokens - cut) + DOC_ROWS, kv_width), bf16),
        [HBM] * 3,
        (far(keys), far(values), far(doc_row)),
        flops=2**33,
        scratch=[pltpu.VMEM((1, tokens), jnp.int32), dma((3,))],
    )
    packed_low, bias, column = call(
        mask_kernel,
        [
            pltpu.VMEM((2 * cut, kv_width), bf16),
            pltpu.VMEM((tokens, tokens), f32),
            pltpu.VMEM((tokens, tokens), f32),
        ],
        [VMEM] * 3,
        (keys, values, doc_row),
        flops=2**27,
    )
    highs, lows = [], []
    for s in range(1, span):
        line = [(i, i + s) for i in range(place_count - s)]
        ring = [(i, (i + s) % place_count) for i in range(place_count)]
        highs.append(lax.ppermute(packed_high, "ctx", line))
        lows.append(lax.ppermute(packed_low, "ctx", line))

    other_core = [(i, i ^ 1) for i in range(devices)]

    def keep_shares(att, first, count, flops):
        keep = pltpu.VMEM((att.shape[0], block), bf16)
        return call(
            functools.partial(keep_kernel, first),
            [keep] * count,
            [VMEM] * 2,
            (near(att), out_weight),
            flops=flops,
        )

    def add(keep, dtype, *got):
        return call(
            sum_kernel,
            pltpu.VMEM(keep.shape, dtype),
            [VMEM] * (1 + len(got)),
            tuple(map(near, (keep, *got))),
        )

    def shares(first, rows, lows, *after):
        prevs = highs + lows
        att, *gives = call(
            functools.partial(give_kernel, first, chips, len(highs), len(lows)),
            [pltpu.VMEM((rows, width), bf16)] + [pltpu.VMEM((rows, block), bf16)] * (chips - 1),
            [VMEM] * (6 + len(prevs)) + [ANY] * len(after),
            (
                *(queries, keys, values, near(bias), near(column), out_weight),
                *map(near, prevs),
                *after,
            ),
            flops=8 * tokens * width * block,
        )
        keeps = keep_shares(att, 1, chips - 1, 2**33)
        sums, arrived = [], []
        for d in range(1, chips):
            total = add(keeps[d - 1], bf16, lax.ppermute(gives[d - 1], "head", other_core))
            pairs = [(i, (i + d * CORES) % devices) for i in range(devices)]
            sums.append(total)
            arrived.append(lax.ppermute(total, "head", pairs))
        return att, sums, arrived

    att_high, sums, high = shares(cut, tokens - cut, lows[:-1])
    att_low, sums, low = shares(0, cut, lows, sums[-1])

    att, *gives = call(
        local_kernel,
        [pltpu.VMEM((tokens, width), bf16)] + [pltpu.VMEM((tokens, block // 2), bf16)] * 2,
        [VMEM] * 3 + [ANY],
        (near(att_low), near(att_high), out_weight, high[-1]),
        flops=4 * tokens * width * block,
    )
    (keep,) = keep_shares(att, 0, 1, 0)
    local = add(keep, f32, *[lax.ppermute(give, "head", other_core) for give in gives])

    def finish(first, rows, arrived, *out):
        return pl.pallas_call(
            functools.partial(final_kernel, first, len(arrived)),
            out_shape=pltpu.HBM((tokens, block), bf16),
            in_specs=[VMEM] * (1 + len(arrived)) + [HBM] * len(out),
            out_specs=HBM,
            scratch_shapes=[pltpu.VMEM((rows, block), bf16), dma],
            input_output_aliases={1 + len(arrived): 0} if out else {},
            cost_estimate=pl.CostEstimate(flops=0, bytes_accessed=0, transcendentals=0),
        )(near(local), *map(near, arrived), *out)

    return finish(0, cut, low, finish(cut, tokens - cut, high))


def solution(mesh):
    in_specs = (P("ctx", "head"), P("ctx", "head"), P("ctx", "head"), P("ctx"), P("head", None))
    out_specs = P("ctx", "head")
    return jax.shard_map(body, mesh=mesh, in_specs=in_specs, out_specs=out_specs, check_vma=False)
```

time: 28 us -> 27.3 us (0.975)
  Pallas kernels: 8.14 us -> 7.11 us
  starting transfers between devices: 11 us -> 11.5 us
    pallas_call x10 -> x11, Pallas kernels: 6.63 us -> 5.6 us  [call(): pl.pallas_call(kernel, out_shape=out_shape, in_specs=in_specs, out_specs=...]
    ppermute x3 -> x4, starting transfers between devices: 8.66 us -> 9.15 us  [the longest x1 5.16 us: body(): highs.append(lax.ppermute(packed_high, 'ctx', line))]
    ppermute x3 -> x4, waiting for transfers between devices: 1.16 us -> 0.68 us  [the longest x2 0.68 us: body(): lax.ppermute(give, 'head', other_core)]
    ppermute x2, waiting for transfers between devices: 5.19 us -> 5.64 us  [shares(): arrived.append(lax.ppermute(total, 'head', pairs))]
  transfers between devices with their start and end apart: 7 -> 8, of which waited for: 5 -> 6; matrix products, arithmetic and copies ran while one was open for 0% -> 0% of each run, Pallas kernels for 23% -> 20%
where the time goes in v3:
time: 27.3 us; the launch traced here: 27.1 us
  starting transfers between devices  11.5 us (42%)
  waiting for transfers between devices  8.38 us (31%)
  Pallas kernels  7.11 us (26%)
    ppermute x2, waiting for transfers between devices, shares(): arrived.append(lax.ppermute(total, 'head', pairs))  5.64 us
    pallas_call x11, Pallas kernels, call(): pl.pallas_call(kernel, out_shape=out_shape, in_specs=in_specs, out_specs=...  5.6 us
    ppermute x1, starting transfers between devices, body(): highs.append(lax.ppermute(packed_high, 'ctx', line))  5.16 us
    ppermute x1, starting transfers between devices, body(): lows.append(lax.ppermute(packed_low, 'ctx', line))  3.43 us
    ppermute x2, starting transfers between devices, shares(): arrived.append(lax.ppermute(total, 'head', pairs))  2.16 us
    ppermute x2, waiting for transfers between devices, shares(): lax.ppermute(gives[d - 1], 'head', other_core)  2.05 us
    pallas_call x2, Pallas kernels, finish(): pl.pallas_call(functools.partial(final_kernel, first, len(arrived)), out_...  1.51 us
    ppermute x2, waiting for transfers between devices, body(): lax.ppermute(give, 'head', other_core)  0.68 us
  transfers between devices with their start and end apart: 8, of which 6 were waited for; matrix products, arithmetic and copies ran while one was open for 0% of the time, Pallas kernels for 20%

profile of v3, /device:TPU:0, one launch (start us, length us, event | category | flops | bytes accessed | tf_op | source)
XLA Modules:
  0.0 27.1 jit_solution(1573604099994964673)
XLA Ops:
  0.0 1.0 %shard_map.56 = bf16[240,256]{1,0:T(8,128)(2,1)S(1)} custom-call(bf16[256,256]{1,0:T(8,128)(2,1)} %k_ref.5, bf16[256,256]{1,0:T(8,128)(2,1)} %v_ref.5, s32[1,256]{1,0:T(1,128)} %bitcast.1), custom_call_target="tpu_custom_call" | custom-call | flops 8589934592 | tf_op jit(solution)/shard_map/pallas_call | solution.py:32
  1.1 5.2 %collective-permute-start = (bf16[240,256]{1,0:T(8,128)(2,1)S(1)}, bf16[240,256]{1,0:T(8,128)(2,1)S(1)}, u32[]{:S(2)}, u32[]{:S(2)}) collective-permute-start(bf16[240,256]{1,0:T(8,128)(2,1)S(1)} %shard_map.56), channel_id=1, source_target_pairs={{0,4},{4,8},{8,12},{12,16},{16,20},{20,24},{24,28},{1,5},{5,9},{9,... | collective-permute-start | bytes 368648 | tf_op jit(solution)/shard_map/ppermute | solution.py:264
  6.2 0.0 copy-done.2
  6.3 0.1 shard_map.55
  6.4 3.4 %collective-permute-start.1 = (bf16[288,256]{1,0:T(8,128)(2,1)S(1)}, bf16[288,256]{1,0:T(8,128)(2,1)S(1)}, u32[]{:S(2)}, u32[]{:S(2)}) collective-permute-start(bf16[288,256]{1,0:T(8,128)(2,1)S(1)} %get-tuple-element.17), channel_id=1, source_target_pairs={{0,4},{4,8},{8,12},{12,16},{16,20},{20,24},{24,28},{1,5},{5,9},{9,... | collective-permute-start | bytes 442376 | tf_op jit(solution)/shard_map/ppermute | solution.py:265
  9.8 0.0 collective-permute-done.rest_0_
  9.8 0.0 copy-done
  9.8 0.0 copy-done.1
  9.8 0.9 %shard_map.57 = (bf16[112,1024]{1,0:T(8,128)(2,1)S(1)}, bf16[112,1024]{1,0:T(8,128)(2,1)S(1)}) custom-call(bf16[256,1024]{1,0:T(8,128)(2,1)S(1)} %copy-done.1, bf16[256,256]{1,0:T(8,128)(2,1)S(1)} %copy-done.2, bf16[256,256]{1,0:T(8,128)(2,1)S(1)} %copy-done.3, f32[256,256]{1,0:T(8,128)S(1)} %get-tuple-element.15.bias_ref, ...), custom_call_target="tpu_custom_call" | custom-call | flops 2147483648 | tf_op jit(solution)/shard_map/pallas_call | solution.py:32
  10.7 0.1 collective-permute-start.2
  10.8 0.5 %shard_map.58.keep_ref = bf16[112,1024]{1,0:T(8,128)(2,1)S(1)} custom-call(bf16[112,1024]{1,0:T(8,128)(2,1)S(1)} %get-tuple-element.18.att_ref.high_ref, bf16[1024,4096]{1,0:T(8,128)(2,1)S(1)} %copy-done), custom_call_target="tpu_custom_call" | custom-call | flops 8589934592 | tf_op jit(solution)/shard_map/pallas_call | solution.py:32
  11.3 1.0 %collective-permute-done.2.rest_0_ = bf16[112,1024]{1,0:T(8,128)(2,1)S(1)} collective-permute-done((bf16[112,1024]{1,0:T(8,128)(2,1)S(1)}, bf16[112,1024]{1,0:T(8,128)(2,1)S(1)}, u32[]{:S(2)}, u32[]{:S(2)}) %collective-permute-start.2) | collective-permute-done | bytes 229408 | tf_op jit(solution)/shard_map/ppermute | solution.py:303
  12.3 0.1 shard_map.59.rest_2_
  12.3 1.6 %collective-permute-start.3 = (bf16[112,1024]{1,0:T(8,128)(2,1)S(1)}, bf16[112,1024]{1,0:T(8,128)(2,1)S(1)}, u32[]{:S(2)}, u32[]{:S(2)}) collective-permute-start(bf16[112,1024]{1,0:T(8,128)(2,1)S(1)} %shard_map.59.rest_2_), channel_id=1, source_target_pairs={{0,2},{1,3},{2,0},{3,1},{4,6},{5,7},{6,4},{7,5},{8,10},{9,11},{10,... | collective-permute-start | bytes 688136 | tf_op jit(solution)/shard_map/ppermute | solution.py:306
  13.9 0.0 collective-permute-done.1.rest_1_
  13.9 0.9 %shard_map.60 = (bf16[144,1024]{1,0:T(8,128)(2,1)S(1)}, bf16[144,1024]{1,0:T(8,128)(2,1)S(1)}) custom-call(bf16[256,1024]{1,0:T(8,128)(2,1)S(1)} %copy-done.1, bf16[256,256]{1,0:T(8,128)(2,1)S(1)} %copy-done.2, bf16[256,256]{1,0:T(8,128)(2,1)S(1)} %copy-done.3, f32[256,256]{1,0:T(8,128)S(1)} %get-tuple-element.15.bias_ref, ...), custom_call_target="tpu_custom_call" | custom-call | flops 2147483648 | tf_op jit(solution)/shard_map/pallas_call | solution.py:32
  14.8 0.1 collective-permute-start.6
  14.9 0.5 %shard_map.64.keep_ref = bf16[144,1024]{1,0:T(8,128)(2,1)S(1)} custom-call(bf16[144,1024]{1,0:T(8,128)(2,1)S(1)} %get-tuple-element.20.low_ref.att_ref, bf16[1024,4096]{1,0:T(8,128)(2,1)S(1)} %copy-done), custom_call_target="tpu_custom_call" | custom-call | flops 8589934592 | tf_op jit(solution)/shard_map/pallas_call | solution.py:32
  15.4 1.1 %collective-permute-done.6.rest_0_ = bf16[144,1024]{1,0:T(8,128)(2,1)S(1)} collective-permute-done((bf16[144,1024]{1,0:T(8,128)(2,1)S(1)}, bf16[144,1024]{1,0:T(8,128)(2,1)S(1)}, u32[]{:S(2)}, u32[]{:S(2)}) %collective-permute-start.6) | collective-permute-done | bytes 294944 | tf_op jit(solution)/shard_map/ppermute | solution.py:303
  16.5 0.1 shard_map.65
  16.6 0.6 %collective-permute-start.7 = (bf16[144,1024]{1,0:T(8,128)(2,1)S(1)}, bf16[144,1024]{1,0:T(8,128)(2,1)S(1)}, u32[]{:S(2)}, u32[]{:S(2)}) collective-permute-start(bf16[144,1024]{1,0:T(8,128)(2,1)S(1)} %shard_map.65), channel_id=1, source_target_pairs={{0,2},{1,3},{2,0},{3,1},{4,6},{5,7},{6,4},{7,5},{8,10},{9,11},{10,... | collective-permute-start | bytes 884744 | tf_op jit(solution)/shard_map/ppermute | solution.py:306
  17.2 3.5 %collective-permute-done.3.after.rest_0_ = bf16[112,1024]{1,0:T(8,128)(2,1)S(1)} collective-permute-done((bf16[112,1024]{1,0:T(8,128)(2,1)S(1)}, bf16[112,1024]{1,0:T(8,128)(2,1)S(1)}, u32[]{:S(2)}, u32[]{:S(2)}) %collective-permute-start.3) | collective-permute-done | bytes 229408 | tf_op jit(solution)/shard_map/ppermute | solution.py:306
  20.6 0.7 %shard_map.61 = (bf16[256,1024]{1,0:T(8,128)(2,1)S(1)}, bf16[256,512]{1,0:T(8,128)(2,1)S(1)}, bf16[256,512]{1,0:T(8,128)(2,1)S(1)}) custom-call(bf16[144,1024]{1,0:T(8,128)(2,1)S(1)} %get-tuple-element.20.low_ref.att_ref, bf16[112,1024]{1,0:T(8,128)(2,1)S(1)} %get-tuple-element.18.att_ref.high_ref, bf16[1024,4096]{1,0:T(8,128)(2,1)S(1)} %copy-done, ...), custom_call_target="tpu_custom_call" | custom-call | flops 1073741824 | tf_op jit(solution)/shard_map/pallas_call | solution.py:32
  21.4 0.1 collective-permute-start.4
  21.4 0.5 %collective-permute-start.5 = (bf16[256,512]{1,0:T(8,128)(2,1)S(1)}, bf16[256,512]{1,0:T(8,128)(2,1)S(1)}, u32[]{:S(2)}, u32[]{:S(2)}) collective-permute-start(bf16[256,512]{1,0:T(8,128)(2,1)S(1)} %get-tuple-element.23), channel_id=1, source_target_pairs={{0,1},{1,0},{2,3},{3,2},{4,5},{5,4},{6,7},{7,6},{8,9},{9,8},{10,11... | collective-permute-start | bytes 786440 | tf_op jit(solution)/shard_map/ppermute | solution.py:320
  21.9 0.7 %shard_map.62.keep_ref = bf16[256,1024]{1,0:T(8,128)(2,1)S(1)} custom-call(bf16[256,1024]{1,0:T(8,128)(2,1)S(1)} %get-tuple-element.21.att_ref, bf16[1024,4096]{1,0:T(8,128)(2,1)S(1)} %copy-done), custom_call_target="tpu_custom_call" | custom-call | tf_op jit(solution)/shard_map/pallas_call | solution.py:32
  22.7 0.3 %collective-permute-done.4.rest_0_ = bf16[256,512]{1,0:T(8,128)(2,1)S(1)} collective-permute-done((bf16[256,512]{1,0:T(8,128)(2,1)S(1)}, bf16[256,512]{1,0:T(8,128)(2,1)S(1)}, u32[]{:S(2)}, u32[]{:S(2)}) %collective-permute-start.4) | collective-permute-done | bytes 262176 | tf_op jit(solution)/shard_map/ppermute | solution.py:320
  23.0 0.4 %collective-permute-done.5.rest_1_ = bf16[256,512]{1,0:T(8,128)(2,1)S(1)} collective-permute-done((bf16[256,512]{1,0:T(8,128)(2,1)S(1)}, bf16[256,512]{1,0:T(8,128)(2,1)S(1)}, u32[]{:S(2)}, u32[]{:S(2)}) %collective-permute-start.5) | collective-permute-done | bytes 262176 | tf_op jit(solution)/shard_map/ppermute | solution.py:320
  23.3 0.1 shard_map.63.local_ref
  23.5 0.7 %shard_map.66.rest_1_ = bf16[256,1024]{1,0:T(8,128)(2,1)} custom-call(f32[256,1024]{1,0:T(8,128)S(1)} %shard_map.63.local_ref, bf16[112,1024]{1,0:T(8,128)(2,1)S(1)} %collective-permute-done.3.after.rest_0_), custom_call_target="tpu_custom_call" | custom-call | tf_op jit(solution)/shard_map/pallas_call | solution.py:323
  24.2 2.2 %collective-permute-done.7.rest_0_ = bf16[144,1024]{1,0:T(8,128)(2,1)S(1)} collective-permute-done((bf16[144,1024]{1,0:T(8,128)(2,1)S(1)}, bf16[144,1024]{1,0:T(8,128)(2,1)S(1)}, u32[]{:S(2)}, u32[]{:S(2)}) %collective-permute-start.7) | collective-permute-done | bytes 294944 | tf_op jit(solution)/shard_map/ppermute | solution.py:306
  26.4 0.8 %shard_map.67 = bf16[256,1024]{1,0:T(8,128)(2,1)} custom-call(f32[256,1024]{1,0:T(8,128)S(1)} %shard_map.63.local_ref, bf16[144,1024]{1,0:T(8,128)(2,1)S(1)} %collective-permute-done.7.rest_0_, bf16[256,1024]{1,0:T(8,128)(2,1)} %shard_map.66.rest_1_), custom_call_target="tpu_custom_call", output_to_operand_aliasing={{}: (2, {})} | custom-call | tf_op jit(solution)/shard_map/pallas_call | solution.py:323
  (7 shorter events, 0.0 us)
Async XLA Ops:
  0.0 6.2 %copy-start.2 = (bf16[256,256]{1,0:T(8,128)(2,1)S(1)}, bf16[256,256]{1,0:T(8,128)(2,1)}, u32[]{:S(2)}) copy-start(bf16[256,256]{1,0:T(8,128)(2,1)} %k_ref.5) | copy-start | bytes 393220
  0.0 6.2 %copy-start.3 = (bf16[256,256]{1,0:T(8,128)(2,1)S(1)}, bf16[256,256]{1,0:T(8,128)(2,1)}, u32[]{:S(2)}) copy-start(bf16[256,256]{1,0:T(8,128)(2,1)} %v_ref.5) | copy-start | bytes 393220
  0.0 6.2 %copy-start.4 = (s32[256]{0:T(256)S(1)}, s32[256]{0:T(256)}, u32[]{:S(2)}) copy-start(s32[256]{0:T(256)} %param.8) | copy-start | bytes 3076
  0.0 9.8 %copy-start = (bf16[1024,4096]{1,0:T(8,128)(2,1)S(1)}, bf16[1024,4096]{1,0:T(8,128)(2,1)}, u32[]{:S(2)}) copy-start(bf16[1024,4096]{1,0:T(8,128)(2,1)} %w_ref.11) | copy-start | bytes 25165828
  0.0 9.8 %copy-start.1 = (bf16[256,1024]{1,0:T(8,128)(2,1)S(1)}, bf16[256,1024]{1,0:T(8,128)(2,1)}, u32[]{:S(2)}) copy-start(bf16[256,1024]{1,0:T(8,128)(2,1)} %q_ref.3) | copy-start | bytes 1572868
  1.1 8.7 %collective-permute-start = (bf16[240,256]{1,0:T(8,128)(2,1)S(1)}, bf16[240,256]{1,0:T(8,128)(2,1)S(1)}, u32[]{:S(2)}, u32[]{:S(2)}) collective-permute-start(bf16[240,256]{1,0:T(8,128)(2,1)S(1)} %shard_map.56), channel_id=1, source_target_pairs={{0,4},{4,8},{8,12},{12,16},{16,20},{20,24},{24,28},{1,5},{5,9},{9,... | collective-permute-start | bytes 368648 | tf_op jit(solution)/shard_map/ppermute | solution.py:264
  6.4 7.5 %collective-permute-start.1 = (bf16[288,256]{1,0:T(8,128)(2,1)S(1)}, bf16[288,256]{1,0:T(8,128)(2,1)S(1)}, u32[]{:S(2)}, u32[]{:S(2)}) collective-permute-start(bf16[288,256]{1,0:T(8,128)(2,1)S(1)} %get-tuple-element.17), channel_id=1, source_target_pairs={{0,4},{4,8},{8,12},{12,16},{16,20},{20,24},{24,28},{1,5},{5,9},{9,... | collective-permute-start | bytes 442376 | tf_op jit(solution)/shard_map/ppermute | solution.py:265
  10.7 1.6 %collective-permute-start.2 = (bf16[112,1024]{1,0:T(8,128)(2,1)S(1)}, bf16[112,1024]{1,0:T(8,128)(2,1)S(1)}, u32[]{:S(2)}, u32[]{:S(2)}) collective-permute-start(bf16[112,1024]{1,0:T(8,128)(2,1)S(1)} %get-tuple-element.19), channel_id=1, source_target_pairs={{0,1},{1,0},{2,3},{3,2},{4,5},{5,4},{6,7},{7,6},{8,9},{9,8},{10,11... | collective-permute-start | bytes 688136 | tf_op jit(solution)/shard_map/ppermute | solution.py:303
  12.3 8.3 %collective-permute-start.3 = (bf16[112,1024]{1,0:T(8,128)(2,1)S(1)}, bf16[112,1024]{1,0:T(8,128)(2,1)S(1)}, u32[]{:S(2)}, u32[]{:S(2)}) collective-permute-start(bf16[112,1024]{1,0:T(8,128)(2,1)S(1)} %shard_map.59.rest_2_), channel_id=1, source_target_pairs={{0,2},{1,3},{2,0},{3,1},{4,6},{5,7},{6,4},{7,5},{8,10},{9,11},{10,... | collective-permute-start | bytes 688136 | tf_op jit(solution)/shard_map/ppermute | solution.py:306
  14.8 1.6 %collective-permute-start.6 = (bf16[144,1024]{1,0:T(8,128)(2,1)S(1)}, bf16[144,1024]{1,0:T(8,128)(2,1)S(1)}, u32[]{:S(2)}, u32[]{:S(2)}) collective-permute-start(bf16[144,1024]{1,0:T(8,128)(2,1)S(1)} %get-tuple-element.24), channel_id=1, source_target_pairs={{0,1},{1,0},{2,3},{3,2},{4,5},{5,4},{6,7},{7,6},{8,9},{9,8},{10,11... | collective-permute-start | bytes 884744 | tf_op jit(solution)/shard_map/ppermute | solution.py:303
  16.6 9.8 %collective-permute-start.7 = (bf16[144,1024]{1,0:T(8,128)(2,1)S(1)}, bf16[144,1024]{1,0:T(8,128)(2,1)S(1)}, u32[]{:S(2)}, u32[]{:S(2)}) collective-permute-start(bf16[144,1024]{1,0:T(8,128)(2,1)S(1)} %shard_map.65), channel_id=1, source_target_pairs={{0,2},{1,3},{2,0},{3,1},{4,6},{5,7},{6,4},{7,5},{8,10},{9,11},{10,... | collective-permute-start | bytes 884744 | tf_op jit(solution)/shard_map/ppermute | solution.py:306
  21.4 1.6 %collective-permute-start.4 = (bf16[256,512]{1,0:T(8,128)(2,1)S(1)}, bf16[256,512]{1,0:T(8,128)(2,1)S(1)}, u32[]{:S(2)}, u32[]{:S(2)}) collective-permute-start(bf16[256,512]{1,0:T(8,128)(2,1)S(1)} %get-tuple-element.22), channel_id=1, source_target_pairs={{0,1},{1,0},{2,3},{3,2},{4,5},{5,4},{6,7},{7,6},{8,9},{9,8},{10,11... | collective-permute-start | bytes 786440 | tf_op jit(solution)/shard_map/ppermute | solution.py:320
  21.4 1.9 %collective-permute-start.5 = (bf16[256,512]{1,0:T(8,128)(2,1)S(1)}, bf16[256,512]{1,0:T(8,128)(2,1)S(1)}, u32[]{:S(2)}, u32[]{:S(2)}) collective-permute-start(bf16[256,512]{1,0:T(8,128)(2,1)S(1)} %get-tuple-element.23), channel_id=1, source_target_pairs={{0,1},{1,0},{2,3},{3,2},{4,5},{5,4},{6,7},{7,6},{8,9},{9,8},{10,11... | collective-permute-start | bytes 786440 | tf_op jit(solution)/shard_map/ppermute | solution.py:320

commit v4 on v3

--- a/solution.py
+++ b/solution.py
@@ -10,7 +10,7 @@
 
 HEAD_DIM = 128
 CORES = 2
-CUT = 144 / 256
+CUT = 160 / 256
 DOC_ROWS = 16
 LOG2_SCALE = math.log2(math.e) / math.sqrt(HEAD_DIM)
 HIDDEN = -1e30
@@ -45,22 +45,30 @@
 def pack_kernel(k_hbm, v_hbm, doc_hbm, high_ref, held, sem):
     tokens, width = k_hbm.shape
     rows = (high_ref.shape[0] - DOC_ROWS) // 2
-    copies = [pltpu.make_async_copy(doc_hbm, held, sem.at[2])]
-    for i, source in enumerate((k_hbm, v_hbm)):
-        copies.append(
-            pltpu.make_async_copy(
-                source.at[tokens - rows :], high_ref.at[i * rows : (i + 1) * rows], sem.at[i]
+    last = lax.axis_index("ctx") == lax.axis_size("ctx") - 1
+
+    @pl.when(last)
+    def _():
+        high_ref[...] = jnp.zeros_like(high_ref)
+
+    @pl.when(jnp.logical_not(last))
+    def _():
+        copies = [pltpu.make_async_copy(doc_hbm, held, sem.at[2])]
+        for i, source in enumerate((k_hbm, v_hbm)):
+            copies.append(
+                pltpu.make_async_copy(
+                    source.at[tokens - rows :], high_ref.at[i * rows : (i + 1) * rows], sem.at[i]
+                )
             )
-        )
-    for copy in copies:
-        copy.start()
-    copies[0].wait()
-    docs = (held[...] + 1).astype(jnp.float32)
-    parts = [docs[:, at : at + width] for at in range(0, tokens, width)]
-    parts.append(jnp.zeros((DOC_ROWS - len(parts), width), jnp.float32))
-    high_ref[2 * rows :, :] = jnp.concatenate(parts, axis=0).astype(jnp.bfloat16)
-    for copy in copies[1:]:
-        copy.wait()
+        for copy in copies:
+            copy.start()
+        copies[0].wait()
+        docs = (held[...] + 1).astype(jnp.float32)
+        parts = [docs[:, at : at + width] for at in range(0, tokens, width)]
+        parts.append(jnp.zeros((DOC_ROWS - len(parts), width), jnp.float32))
+        high_ref[2 * rows :, :] = jnp.concatenate(parts, axis=0).astype(jnp.bfloat16)
+        for copy in copies[1:]:
+            copy.wait()
 
 
 def stacked(q_ref, r0, rows, first, repeats):
@@ -99,7 +107,7 @@
     repeats = q_ref.shape[1] // HEAD_DIM // groups
     column = column_ref[first:count, :]
     biases, keys, values = [], [], []
-    for high, low in zip(highs, lows):
+    for s, (high, low) in enumerate(zip(highs, lows), 1):
         n = (high.shape[0] - DOC_ROWS) // 2
         seen = tokens if low is not None else n
         if low is not None:
@@ -107,7 +115,8 @@
             values.append(low[tokens - n :, :])
         keys.append(high[:n, :])
         values.append(high[n : 2 * n, :])
-        same = key_docs(high, tokens)[:, tokens - seen :] == column[:, :seen]
+        there = (lax.axis_index("ctx") >= s).astype(jnp.float32)
+        same = key_docs(high, tokens)[:, tokens - seen :] * there == column[:, :seen]
         biases.append(jnp.where(same, 0.0, HIDDEN))
     place = 0 if first else len(biases)
     biases.insert(place, bias_ref[first:count, :count])
@@ -164,23 +173,40 @@
     ).astype(jnp.bfloat16)
 
 
+def give_shares(first, chips, refs, highs, lows, w_ref, att_ref, gives):
+    attend(first, *refs, highs, lows, att_ref)
+    att = att_ref[...]
+    for d in range(1, chips):
+        project(att, w_ref, d, 1, gives[d - 1])
+
+
+def first_kernel(first, chips, q_ref, k_ref, v_ref, bias_ref, column_ref, w_ref, att_ref, *gives):
+    @pl.when(lax.axis_index("ctx") == 0)
+    def _():
+        give_shares(first, chips, (q_ref, bias_ref, column_ref, k_ref, v_ref), [], [], w_ref, att_ref, gives)
+
+
 def give_kernel(
-    first, chips, n_high, n_low, q_ref, k_ref, v_ref, bias_ref, column_ref, w_ref, *rest
+    first, chips, n_high, n_low, n_done, q_ref, k_ref, v_ref, bias_ref, column_ref, w_ref, *rest
 ):
     outs = rest[-chips:]
-    att_ref, gives = outs[0], outs[1:]
     highs, lows = list(rest[:n_high]), list(rest[n_high : n_high + n_low])
+    done = rest[n_high + n_low : n_high + n_low + n_done]
     lows += [None] * (n_high - n_low)
+    refs = (q_ref, bias_ref, column_ref, k_ref, v_ref)
     here = lax.axis_index("ctx")
 
-    def shares(highs, lows):
-        attend(first, q_ref, bias_ref, column_ref, k_ref, v_ref, highs, lows, att_ref)
-        att = att_ref[...]
-        for d in range(1, chips):
-            project(att, w_ref, d, 1, gives[d - 1])
-
-    pl.when(here == 0)(lambda: shares([], []))
-    pl.when(here > 0)(lambda: shares(highs, lows))
+    @pl.when(here == 0)
+    def _():
+        if done:
+            for ref, out in zip(done, outs):
+                out[...] = ref[...]
+        else:
+            give_shares(first, chips, refs, [], [], w_ref, outs[0], outs[1:])
+
+    @pl.when(here > 0)
+    def _():
+        give_shares(first, chips, refs, highs, lows, w_ref, outs[0], outs[1:])
 
 
 def keep_kernel(first, att_ref, w_ref, *outs):
@@ -259,10 +285,9 @@
     )
     highs, lows = [], []
     for s in range(1, span):
-        line = [(i, i + s) for i in range(place_count - s)]
         ring = [(i, (i + s) % place_count) for i in range(place_count)]
-        highs.append(lax.ppermute(packed_high, "ctx", line))
-        lows.append(lax.ppermute(packed_low, "ctx", line))
+        highs.append(lax.ppermute(packed_high, "ctx", ring))
+        lows.append(lax.ppermute(packed_low, "ctx", ring[: place_count - s]))
 
     other_core = [(i, i ^ 1) for i in range(devices)]
 
@@ -284,17 +309,25 @@
             tuple(map(near, (keep, *got))),
         )
 
-    def shares(first, rows, lows, *after):
-        prevs = highs + lows
+    def outputs(rows):
+        return [pltpu.VMEM((rows, width), bf16)] + [pltpu.VMEM((rows, block), bf16)] * (chips - 1)
+
+    always = (queries, keys, values, near(bias), near(column), out_weight)
+    done = call(
+        functools.partial(first_kernel, cut, chips),
+        outputs(tokens - cut),
+        [VMEM] * len(always),
+        always,
+        flops=2**27,
+    )
+
+    def shares(first, rows, lows, done, *after):
+        prevs = highs + lows + done
         att, *gives = call(
-            functools.partial(give_kernel, first, chips, len(highs), len(lows)),
-            [pltpu.VMEM((rows, width), bf16)] + [pltpu.VMEM((rows, block), bf16)] * (chips - 1),
-            [VMEM] * (6 + len(prevs)) + [ANY] * len(after),
-            (
-                *(queries, keys, values, near(bias), near(column), out_weight),
-                *map(near, prevs),
-                *after,
-            ),
+            functools.partial(give_kernel, first, chips, len(highs), len(lows), len(done)),
+            outputs(rows),
+            [VMEM] * (len(always) + len(prevs)) + [ANY] * len(after),
+            (*always, *map(near, prevs), *after),
             flops=8 * tokens * width * block,
         )
         keeps = keep_shares(att, 1, chips - 1, 2**33)
@@ -306,8 +339,8 @@
             arrived.append(lax.ppermute(total, "head", pairs))
         return att, sums, arrived
 
-    att_high, sums, high = shares(cut, tokens - cut, lows[:-1])
-    att_low, sums, low = shares(0, cut, lows, sums[-1])
+    att_high, sums, high = shares(cut, tokens - cut, lows[:-1], list(done))
+    att_low, sums, low = shares(0, cut, lows, [], sums[-1])
 
     att, *gives = call(
         local_kernel,

time: 27.3 us -> 26.7 us (0.978)
  starting transfers between devices: 11.5 us -> 9.66 us
  waiting for transfers between devices: 8.38 us -> 9.44 us
    ppermute x2, starting transfers between devices: 8.59 us -> 6.47 us  [the longest x1 3.43 us: body(): lows.append(lax.ppermute(packed_low, 'ctx', ring[:place_count - s]))]
    ppermute x2, waiting for transfers between devices: 0.01 us -> 0.58 us  [the longest x1 0.57 us: body(): highs.append(lax.ppermute(packed_high, 'ctx', ring))]
    ppermute x2, waiting for transfers between devices: 5.64 us -> 6.18 us  [shares(): arrived.append(lax.ppermute(total, 'head', pairs))]
    ppermute x2, starting transfers between devices: 2.16 us -> 2.49 us  [shares(): arrived.append(lax.ppermute(total, 'head', pairs))]
    pallas_call x11 -> x12, Pallas kernels: 5.6 us -> 5.75 us  [call(): pl.pallas_call(kernel, out_shape=out_shape, in_specs=in_specs, out_specs=...]
  transfers between devices with their start and end apart: 8 -> 8, of which waited for: 6 -> 7; matrix products, arithmetic and copies ran while one was open for 0% -> 0% of each run, Pallas kernels for 20% -> 21%
where the time goes in v4:
time: 26.7 us; the launch traced here: 26.5 us
  starting transfers between devices  9.66 us (36%)
  waiting for transfers between devices  9.44 us (35%)
  Pallas kernels  7.26 us (27%)
    ppermute x2, waiting for transfers between devices, shares(): arrived.append(lax.ppermute(total, 'head', pairs))  6.18 us
    pallas_call x12, Pallas kernels, call(): pl.pallas_call(kernel, out_shape=out_shape, in_specs=in_specs, out_specs=...  5.75 us
    ppermute x1, starting transfers between devices, body(): lows.append(lax.ppermute(packed_low, 'ctx', ring[:place_count - s]))  3.43 us
    ppermute x1, starting transfers between devices, body(): highs.append(lax.ppermute(packed_high, 'ctx', ring))  3.03 us
    ppermute x2, starting transfers between devices, shares(): arrived.append(lax.ppermute(total, 'head', pairs))  2.49 us
    ppermute x2, waiting for transfers between devices, shares(): lax.ppermute(gives[d - 1], 'head', other_core)  2.01 us
    pallas_call x2, Pallas kernels, finish(): pl.pallas_call(functools.partial(final_kernel, first, len(arrived)), out_...  1.51 us
    ppermute x2, waiting for transfers between devices, body(): lax.ppermute(give, 'head', other_core)  0.68 us
  transfers between devices with their start and end apart: 8, of which 7 were waited for; matrix products, arithmetic and copies ran while one was open for 0% of the time, Pallas kernels for 21%

profile of v4, /device:TPU:0, one launch (start us, length us, event | category | flops | bytes accessed | tf_op | source)
XLA Modules:
  0.0 26.5 jit_solution(14996195054750598979)
XLA Ops:
  0.0 1.0 %shard_map.56 = bf16[208,256]{1,0:T(8,128)(2,1)S(1)} custom-call(bf16[256,256]{1,0:T(8,128)(2,1)} %k_ref.7, bf16[256,256]{1,0:T(8,128)(2,1)} %v_ref.7, s32[1,256]{1,0:T(1,128)} %bitcast.1), custom_call_target="tpu_custom_call" | custom-call | flops 8589934592 | tf_op jit(solution)/shard_map/pallas_call | solution.py:32
  1.1 3.0 %collective-permute-start = (bf16[208,256]{1,0:T(8,128)(2,1)S(1)}, bf16[208,256]{1,0:T(8,128)(2,1)S(1)}, u32[]{:S(2)}, u32[]{:S(2)}) collective-permute-start(bf16[208,256]{1,0:T(8,128)(2,1)S(1)} %shard_map.56), channel_id=1, source_target_pairs={{0,4},{4,8},{8,12},{12,16},{16,20},{20,24},{24,28},{28,0},{1,5},{5... | collective-permute-start | bytes 319496 | tf_op jit(solution)/shard_map/ppermute | solution.py:289
  4.1 0.0 copy-done.2
  4.1 0.0 copy-done.3
  4.1 0.0 copy-done.4
  4.1 0.1 shard_map.55
  4.2 3.4 %collective-permute-start.1 = (bf16[320,256]{1,0:T(8,128)(2,1)S(1)}, bf16[320,256]{1,0:T(8,128)(2,1)S(1)}, u32[]{:S(2)}, u32[]{:S(2)}) collective-permute-start(bf16[320,256]{1,0:T(8,128)(2,1)S(1)} %get-tuple-element.19), channel_id=1, source_target_pairs={{0,4},{4,8},{8,12},{12,16},{16,20},{20,24},{24,28},{1,5},{5,9},{9,... | collective-permute-start | bytes 491528 | tf_op jit(solution)/shard_map/ppermute | solution.py:290
  7.6 0.0 copy-done
  7.7 0.9 %shard_map.57 = (bf16[96,1024]{1,0:T(8,128)(2,1)S(1)}, bf16[96,1024]{1,0:T(8,128)(2,1)S(1)}) custom-call(bf16[256,1024]{1,0:T(8,128)(2,1)S(1)} %copy-done.1, bf16[256,256]{1,0:T(8,128)(2,1)S(1)} %copy-done.2, bf16[256,256]{1,0:T(8,128)(2,1)S(1)} %copy-done.3, f32[256,256]{1,0:T(8,128)S(1)} %get-tuple-element.17.bias_ref, ...), custom_call_target="tpu_custom_call" | custom-call | flops 134217728 | tf_op jit(solution)/shard_map/pallas_call | solution.py:32
  8.6 0.6 %collective-permute-done.rest_0_ = bf16[208,256]{1,0:T(8,128)(2,1)S(1)} collective-permute-done((bf16[208,256]{1,0:T(8,128)(2,1)S(1)}, bf16[208,256]{1,0:T(8,128)(2,1)S(1)}, u32[]{:S(2)}, u32[]{:S(2)}) %collective-permute-start) | collective-permute-done | bytes 106528 | tf_op jit(solution)/shard_map/ppermute | solution.py:289
  9.2 0.1 collective-permute-start.2
  9.3 0.5 %shard_map.59.keep_ref = bf16[96,1024]{1,0:T(8,128)(2,1)S(1)} custom-call(bf16[96,1024]{1,0:T(8,128)(2,1)S(1)} %get-tuple-element.22.att_ref.high_ref, bf16[1024,4096]{1,0:T(8,128)(2,1)S(1)} %copy-done), custom_call_target="tpu_custom_call" | custom-call | flops 8589934592 | tf_op jit(solution)/shard_map/pallas_call | solution.py:32
  9.8 0.9 %collective-permute-done.2.rest_0_ = bf16[96,1024]{1,0:T(8,128)(2,1)S(1)} collective-permute-done((bf16[96,1024]{1,0:T(8,128)(2,1)S(1)}, bf16[96,1024]{1,0:T(8,128)(2,1)S(1)}, u32[]{:S(2)}, u32[]{:S(2)}) %collective-permute-start.2) | collective-permute-done | bytes 196640 | tf_op jit(solution)/shard_map/ppermute | solution.py:336
  10.7 2.4 %collective-permute-start.3 = (bf16[96,1024]{1,0:T(8,128)(2,1)S(1)}, bf16[96,1024]{1,0:T(8,128)(2,1)S(1)}, u32[]{:S(2)}, u32[]{:S(2)}) collective-permute-start(bf16[96,1024]{1,0:T(8,128)(2,1)S(1)} %shard_map.60.rest_2_), channel_id=1, source_target_pairs={{0,2},{1,3},{2,0},{3,1},{4,6},{5,7},{6,4},{7,5},{8,10},{9,11},{10,... | collective-permute-start | bytes 589832 | tf_op jit(solution)/shard_map/ppermute | solution.py:339
  13.1 0.0 collective-permute-done.1.rest_1_
  13.1 1.0 %shard_map.61 = (bf16[160,1024]{1,0:T(8,128)(2,1)S(1)}, bf16[160,1024]{1,0:T(8,128)(2,1)S(1)}) custom-call(bf16[256,1024]{1,0:T(8,128)(2,1)S(1)} %copy-done.1, bf16[256,256]{1,0:T(8,128)(2,1)S(1)} %copy-done.2, bf16[256,256]{1,0:T(8,128)(2,1)S(1)} %copy-done.3, f32[256,256]{1,0:T(8,128)S(1)} %get-tuple-element.17.bias_ref, ...), custom_call_target="tpu_custom_call" | custom-call | flops 2147483648 | tf_op jit(solution)/shard_map/pallas_call | solution.py:32
  14.1 0.1 collective-permute-start.6
  14.2 0.5 %shard_map.65.keep_ref = bf16[160,1024]{1,0:T(8,128)(2,1)S(1)} custom-call(bf16[160,1024]{1,0:T(8,128)(2,1)S(1)} %get-tuple-element.24.low_ref.att_ref, bf16[1024,4096]{1,0:T(8,128)(2,1)S(1)} %copy-done), custom_call_target="tpu_custom_call" | custom-call | flops 8589934592 | tf_op jit(solution)/shard_map/pallas_call | solution.py:32
  14.8 1.1 %collective-permute-done.6.rest_0_ = bf16[160,1024]{1,0:T(8,128)(2,1)S(1)} collective-permute-done((bf16[160,1024]{1,0:T(8,128)(2,1)S(1)}, bf16[160,1024]{1,0:T(8,128)(2,1)S(1)}, u32[]{:S(2)}, u32[]{:S(2)}) %collective-permute-start.6) | collective-permute-done | bytes 327712 | tf_op jit(solution)/shard_map/ppermute | solution.py:336
  15.8 0.1 shard_map.66
  15.9 0.1 collective-permute-start.7
  16.0 2.4 %collective-permute-done.3.after.rest_0_ = bf16[96,1024]{1,0:T(8,128)(2,1)S(1)} collective-permute-done((bf16[96,1024]{1,0:T(8,128)(2,1)S(1)}, bf16[96,1024]{1,0:T(8,128)(2,1)S(1)}, u32[]{:S(2)}, u32[]{:S(2)}) %collective-permute-start.3) | collective-permute-done | bytes 196640 | tf_op jit(solution)/shard_map/ppermute | solution.py:339
  18.4 0.7 %shard_map.62 = (bf16[256,1024]{1,0:T(8,128)(2,1)S(1)}, bf16[256,512]{1,0:T(8,128)(2,1)S(1)}, bf16[256,512]{1,0:T(8,128)(2,1)S(1)}) custom-call(bf16[160,1024]{1,0:T(8,128)(2,1)S(1)} %get-tuple-element.24.low_ref.att_ref, bf16[96,1024]{1,0:T(8,128)(2,1)S(1)} %get-tuple-element.22.att_ref.high_ref, bf16[1024,4096]{1,0:T(8,128)(2,1)S(1)} %copy-done, ...), custom_call_target="tpu_custom_call" | custom-call | flops 1073741824 | tf_op jit(solution)/shard_map/pallas_call | solution.py:32
  19.1 0.1 collective-permute-start.4
  19.2 0.5 %collective-permute-start.5 = (bf16[256,512]{1,0:T(8,128)(2,1)S(1)}, bf16[256,512]{1,0:T(8,128)(2,1)S(1)}, u32[]{:S(2)}, u32[]{:S(2)}) collective-permute-start(bf16[256,512]{1,0:T(8,128)(2,1)S(1)} %get-tuple-element.27), channel_id=1, source_target_pairs={{0,1},{1,0},{2,3},{3,2},{4,5},{5,4},{6,7},{7,6},{8,9},{9,8},{10,11... | collective-permute-start | bytes 786440 | tf_op jit(solution)/shard_map/ppermute | solution.py:353
  19.7 0.7 %shard_map.63.keep_ref = bf16[256,1024]{1,0:T(8,128)(2,1)S(1)} custom-call(bf16[256,1024]{1,0:T(8,128)(2,1)S(1)} %get-tuple-element.25.att_ref, bf16[1024,4096]{1,0:T(8,128)(2,1)S(1)} %copy-done), custom_call_target="tpu_custom_call" | custom-call | tf_op jit(solution)/shard_map/pallas_call | solution.py:32
  20.4 0.3 %collective-permute-done.4.rest_0_ = bf16[256,512]{1,0:T(8,128)(2,1)S(1)} collective-permute-done((bf16[256,512]{1,0:T(8,128)(2,1)S(1)}, bf16[256,512]{1,0:T(8,128)(2,1)S(1)}, u32[]{:S(2)}, u32[]{:S(2)}) %collective-permute-start.4) | collective-permute-done | bytes 262176 | tf_op jit(solution)/shard_map/ppermute | solution.py:353
  20.7 0.4 %collective-permute-done.5.rest_1_ = bf16[256,512]{1,0:T(8,128)(2,1)S(1)} collective-permute-done((bf16[256,512]{1,0:T(8,128)(2,1)S(1)}, bf16[256,512]{1,0:T(8,128)(2,1)S(1)}, u32[]{:S(2)}, u32[]{:S(2)}) %collective-permute-start.5) | collective-permute-done | bytes 262176 | tf_op jit(solution)/shard_map/ppermute | solution.py:353
  21.1 0.1 shard_map.64.local_ref
  21.2 0.7 %shard_map.67.rest_1_ = bf16[256,1024]{1,0:T(8,128)(2,1)} custom-call(f32[256,1024]{1,0:T(8,128)S(1)} %shard_map.64.local_ref, bf16[96,1024]{1,0:T(8,128)(2,1)S(1)} %collective-permute-done.3.after.rest_0_), custom_call_target="tpu_custom_call" | custom-call | tf_op jit(solution)/shard_map/pallas_call | solution.py:356
  21.9 3.8 %collective-permute-done.7.rest_0_ = bf16[160,1024]{1,0:T(8,128)(2,1)S(1)} collective-permute-done((bf16[160,1024]{1,0:T(8,128)(2,1)S(1)}, bf16[160,1024]{1,0:T(8,128)(2,1)S(1)}, u32[]{:S(2)}, u32[]{:S(2)}) %collective-permute-start.7) | collective-permute-done | bytes 327712 | tf_op jit(solution)/shard_map/ppermute | solution.py:339
  25.7 0.8 %shard_map.68 = bf16[256,1024]{1,0:T(8,128)(2,1)} custom-call(f32[256,1024]{1,0:T(8,128)S(1)} %shard_map.64.local_ref, bf16[160,1024]{1,0:T(8,128)(2,1)S(1)} %collective-permute-done.7.rest_0_, bf16[256,1024]{1,0:T(8,128)(2,1)} %shard_map.67.rest_1_), custom_call_target="tpu_custom_call", output_to_operand_aliasing={{}: (2, {})} | custom-call | tf_op jit(solution)/shard_map/pallas_call | solution.py:356
  (8 shorter events, 0.1 us)
Async XLA Ops:
  0.0 4.1 %copy-start.2 = (bf16[256,256]{1,0:T(8,128)(2,1)S(1)}, bf16[256,256]{1,0:T(8,128)(2,1)}, u32[]{:S(2)}) copy-start(bf16[256,256]{1,0:T(8,128)(2,1)} %k_ref.7) | copy-start | bytes 393220
  0.0 4.1 %copy-start.3 = (bf16[256,256]{1,0:T(8,128)(2,1)S(1)}, bf16[256,256]{1,0:T(8,128)(2,1)}, u32[]{:S(2)}) copy-start(bf16[256,256]{1,0:T(8,128)(2,1)} %v_ref.7) | copy-start | bytes 393220
  0.0 4.1 %copy-start.4 = (s32[256]{0:T(256)S(1)}, s32[256]{0:T(256)}, u32[]{:S(2)}) copy-start(s32[256]{0:T(256)} %param.8) | copy-start | bytes 3076
  0.0 7.6 %copy-start = (bf16[1024,4096]{1,0:T(8,128)(2,1)S(1)}, bf16[1024,4096]{1,0:T(8,128)(2,1)}, u32[]{:S(2)}) copy-start(bf16[1024,4096]{1,0:T(8,128)(2,1)} %w_ref.13) | copy-start | bytes 25165828
  0.0 7.7 %copy-start.1 = (bf16[256,1024]{1,0:T(8,128)(2,1)S(1)}, bf16[256,1024]{1,0:T(8,128)(2,1)}, u32[]{:S(2)}) copy-start(bf16[256,1024]{1,0:T(8,128)(2,1)} %q_ref.5) | copy-start | bytes 1572868
  1.1 8.1 %collective-permute-start = (bf16[208,256]{1,0:T(8,128)(2,1)S(1)}, bf16[208,256]{1,0:T(8,128)(2,1)S(1)}, u32[]{:S(2)}, u32[]{:S(2)}) collective-permute-start(bf16[208,256]{1,0:T(8,128)(2,1)S(1)} %shard_map.56), channel_id=1, source_target_pairs={{0,4},{4,8},{8,12},{12,16},{16,20},{20,24},{24,28},{28,0},{1,5},{5... | collective-permute-start | bytes 319496 | tf_op jit(solution)/shard_map/ppermute | solution.py:289
  4.2 8.9 %collective-permute-start.1 = (bf16[320,256]{1,0:T(8,128)(2,1)S(1)}, bf16[320,256]{1,0:T(8,128)(2,1)S(1)}, u32[]{:S(2)}, u32[]{:S(2)}) collective-permute-start(bf16[320,256]{1,0:T(8,128)(2,1)S(1)} %get-tuple-element.19), channel_id=1, source_target_pairs={{0,4},{4,8},{8,12},{12,16},{16,20},{20,24},{24,28},{1,5},{5,9},{9,... | collective-permute-start | bytes 491528 | tf_op jit(solution)/shard_map/ppermute | solution.py:290
  9.2 1.5 %collective-permute-start.2 = (bf16[96,1024]{1,0:T(8,128)(2,1)S(1)}, bf16[96,1024]{1,0:T(8,128)(2,1)S(1)}, u32[]{:S(2)}, u32[]{:S(2)}) collective-permute-start(bf16[96,1024]{1,0:T(8,128)(2,1)S(1)} %get-tuple-element.23), channel_id=1, source_target_pairs={{0,1},{1,0},{2,3},{3,2},{4,5},{5,4},{6,7},{7,6},{8,9},{9,8},{10,11... | collective-permute-start | bytes 589832 | tf_op jit(solution)/shard_map/ppermute | solution.py:336
  10.7 7.7 %collective-permute-start.3 = (bf16[96,1024]{1,0:T(8,128)(2,1)S(1)}, bf16[96,1024]{1,0:T(8,128)(2,1)S(1)}, u32[]{:S(2)}, u32[]{:S(2)}) collective-permute-start(bf16[96,1024]{1,0:T(8,128)(2,1)S(1)} %shard_map.60.rest_2_), channel_id=1, source_target_pairs={{0,2},{1,3},{2,0},{3,1},{4,6},{5,7},{6,4},{7,5},{8,10},{9,11},{10,... | collective-permute-start | bytes 589832 | tf_op jit(solution)/shard_map/ppermute | solution.py:339
  14.1 1.7 %collective-permute-start.6 = (bf16[160,1024]{1,0:T(8,128)(2,1)S(1)}, bf16[160,1024]{1,0:T(8,128)(2,1)S(1)}, u32[]{:S(2)}, u32[]{:S(2)}) collective-permute-start(bf16[160,1024]{1,0:T(8,128)(2,1)S(1)} %get-tuple-element.28), channel_id=1, source_target_pairs={{0,1},{1,0},{2,3},{3,2},{4,5},{5,4},{6,7},{7,6},{8,9},{9,8},{10,11... | collective-permute-start | bytes 983048 | tf_op jit(solution)/shard_map/ppermute | solution.py:336
  15.9 9.8 %collective-permute-start.7 = (bf16[160,1024]{1,0:T(8,128)(2,1)S(1)}, bf16[160,1024]{1,0:T(8,128)(2,1)S(1)}, u32[]{:S(2)}, u32[]{:S(2)}) collective-permute-start(bf16[160,1024]{1,0:T(8,128)(2,1)S(1)} %shard_map.66), channel_id=1, source_target_pairs={{0,2},{1,3},{2,0},{3,1},{4,6},{5,7},{6,4},{7,5},{8,10},{9,11},{10,... | collective-permute-start | bytes 983048 | tf_op jit(solution)/shard_map/ppermute | solution.py:339
  19.1 1.6 %collective-permute-start.4 = (bf16[256,512]{1,0:T(8,128)(2,1)S(1)}, bf16[256,512]{1,0:T(8,128)(2,1)S(1)}, u32[]{:S(2)}, u32[]{:S(2)}) collective-permute-start(bf16[256,512]{1,0:T(8,128)(2,1)S(1)} %get-tuple-element.26), channel_id=1, source_target_pairs={{0,1},{1,0},{2,3},{3,2},{4,5},{5,4},{6,7},{7,6},{8,9},{9,8},{10,11... | collective-permute-start | bytes 786440 | tf_op jit(solution)/shard_map/ppermute | solution.py:353
  19.2 1.9 %collective-permute-start.5 = (bf16[256,512]{1,0:T(8,128)(2,1)S(1)}, bf16[256,512]{1,0:T(8,128)(2,1)S(1)}, u32[]{:S(2)}, u32[]{:S(2)}) collective-permute-start(bf16[256,512]{1,0:T(8,128)(2,1)S(1)} %get-tuple-element.27), channel_id=1, source_target_pairs={{0,1},{1,0},{2,3},{3,2},{4,5},{5,4},{6,7},{7,6},{8,9},{9,8},{10,11... | collective-permute-start | bytes 786440 | tf_op jit(solution)/shard_map/ppermute | solution.py:353

commit v5 on v4

--- a/solution.py
+++ b/solution.py
@@ -180,29 +180,30 @@
         project(att, w_ref, d, 1, gives[d - 1])
 
 
-def first_kernel(first, chips, q_ref, k_ref, v_ref, bias_ref, column_ref, w_ref, att_ref, *gives):
+def first_kernel(cut, chips, q_ref, k_ref, v_ref, bias_ref, column_ref, w_ref, *outs):
+    refs = (q_ref, bias_ref, column_ref, k_ref, v_ref)
+    highs, lows = outs[:chips], outs[chips:]
+
     @pl.when(lax.axis_index("ctx") == 0)
     def _():
-        give_shares(first, chips, (q_ref, bias_ref, column_ref, k_ref, v_ref), [], [], w_ref, att_ref, gives)
+        for first, (att_ref, *gives) in ((cut, highs), (0, lows)):
+            give_shares(first, chips, refs, [], [], w_ref, att_ref, gives)
 
 
 def give_kernel(
-    first, chips, n_high, n_low, n_done, q_ref, k_ref, v_ref, bias_ref, column_ref, w_ref, *rest
+    first, chips, n_high, n_low, q_ref, k_ref, v_ref, bias_ref, column_ref, w_ref, *rest
 ):
     outs = rest[-chips:]
     highs, lows = list(rest[:n_high]), list(rest[n_high : n_high + n_low])
-    done = rest[n_high + n_low : n_high + n_low + n_done]
+    done = rest[n_high + n_low : n_high + n_low + chips]
     lows += [None] * (n_high - n_low)
     refs = (q_ref, bias_ref, column_ref, k_ref, v_ref)
     here = lax.axis_index("ctx")
 
     @pl.when(here == 0)
     def _():
-        if done:
-            for ref, out in zip(done, outs):
-                out[...] = ref[...]
-        else:
-            give_shares(first, chips, refs, [], [], w_ref, outs[0], outs[1:])
+        for ref, out in zip(done, outs):
+            out[...] = ref[...]
 
     @pl.when(here > 0)
     def _():
@@ -315,7 +316,7 @@
     always = (queries, keys, values, near(bias), near(column), out_weight)
     done = call(
         functools.partial(first_kernel, cut, chips),
-        outputs(tokens - cut),
+        outputs(tokens - cut) + outputs(cut),
         [VMEM] * len(always),
         always,
         flops=2**27,
@@ -324,7 +325,7 @@
     def shares(first, rows, lows, done, *after):
         prevs = highs + lows + done
         att, *gives = call(
-            functools.partial(give_kernel, first, chips, len(highs), len(lows), len(done)),
+            functools.partial(give_kernel, first, chips, len(highs), len(lows)),
             outputs(rows),
             [VMEM] * (len(always) + len(prevs)) + [ANY] * len(after),
             (*always, *map(near, prevs), *after),
@@ -339,8 +340,8 @@
             arrived.append(lax.ppermute(total, "head", pairs))
         return att, sums, arrived
 
-    att_high, sums, high = shares(cut, tokens - cut, lows[:-1], list(done))
-    att_low, sums, low = shares(0, cut, lows, [], sums[-1])
+    att_high, sums, high = shares(cut, tokens - cut, lows[:-1], list(done[:chips]))
+    att_low, sums, low = shares(0, cut, lows, list(done[chips:]), sums[-1])
 
     att, *gives = call(
         local_kernel,

time: 26.7 us -> 26.3 us (0.985)
  starting transfers between devices: 9.66 us -> 9.33 us
    ppermute x1, waiting for transfers between devices: 0.57 us -> 0.01 us  [body(): highs.append(lax.ppermute(packed_high, 'ctx', ring))]
    ppermute x2, waiting for transfers between devices: 6.18 us -> 6.74 us  [shares(): arrived.append(lax.ppermute(total, 'head', pairs))]
    ppermute x2, starting transfers between devices: 2.49 us -> 2.16 us  [shares(): arrived.append(lax.ppermute(total, 'head', pairs))]
  transfers between devices with their start and end apart: 8 -> 8, of which waited for: 7 -> 6; matrix products, arithmetic and copies ran while one was open for 0% -> 0% of each run, Pallas kernels for 21% -> 21%
where the time goes in v5:
time: 26.3 us; the launch traced here: 26.1 us
  waiting for transfers between devices  9.44 us (36%)
  starting transfers between devices  9.33 us (35%)
  Pallas kernels  7.2 us (27%)
    ppermute x2, waiting for transfers between devices, shares(): arrived.append(lax.ppermute(total, 'head', pairs))  6.74 us
    pallas_call x12, Pallas kernels, call(): pl.pallas_call(kernel, out_shape=out_shape, in_specs=in_specs, out_specs=...  5.68 us
    ppermute x1, starting transfers between devices, body(): lows.append(lax.ppermute(packed_low, 'ctx', ring[:place_count - s]))  3.43 us
    ppermute x1, starting transfers between devices, body(): highs.append(lax.ppermute(packed_high, 'ctx', ring))  3.03 us
    ppermute x2, starting transfers between devices, shares(): arrived.append(lax.ppermute(total, 'head', pairs))  2.16 us
    ppermute x2, waiting for transfers between devices, shares(): lax.ppermute(gives[d - 1], 'head', other_core)  2.01 us
    pallas_call x2, Pallas kernels, finish(): pl.pallas_call(functools.partial(final_kernel, first, len(arrived)), out_...  1.51 us
    ppermute x2, waiting for transfers between devices, body(): lax.ppermute(give, 'head', other_core)  0.68 us
  transfers between devices with their start and end apart: 8, of which 6 were waited for; matrix products, arithmetic and copies ran while one was open for 0% of the time, Pallas kernels for 21%

profile of v5, /device:TPU:0, one launch (start us, length us, event | category | flops | bytes accessed | tf_op | source)
XLA Modules:
  0.0 26.1 jit_solution(6983273977864959608)
XLA Ops:
  0.0 1.0 %shard_map.56 = bf16[208,256]{1,0:T(8,128)(2,1)S(1)} custom-call(bf16[256,256]{1,0:T(8,128)(2,1)} %k_ref.7, bf16[256,256]{1,0:T(8,128)(2,1)} %v_ref.7, s32[1,256]{1,0:T(1,128)} %bitcast.1), custom_call_target="tpu_custom_call" | custom-call | flops 8589934592 | tf_op jit(solution)/shard_map/pallas_call | solution.py:32
  1.1 3.0 %collective-permute-start = (bf16[208,256]{1,0:T(8,128)(2,1)S(1)}, bf16[208,256]{1,0:T(8,128)(2,1)S(1)}, u32[]{:S(2)}, u32[]{:S(2)}) collective-permute-start(bf16[208,256]{1,0:T(8,128)(2,1)S(1)} %shard_map.56), channel_id=1, source_target_pairs={{0,4},{4,8},{8,12},{12,16},{16,20},{20,24},{24,28},{28,0},{1,5},{5... | collective-permute-start | bytes 319496 | tf_op jit(solution)/shard_map/ppermute | solution.py:290
  4.1 0.0 copy-done.2
  4.1 0.0 copy-done.3
  4.1 0.0 copy-done.4
  4.1 0.1 shard_map.55
  4.2 3.4 %collective-permute-start.1 = (bf16[320,256]{1,0:T(8,128)(2,1)S(1)}, bf16[320,256]{1,0:T(8,128)(2,1)S(1)}, u32[]{:S(2)}, u32[]{:S(2)}) collective-permute-start(bf16[320,256]{1,0:T(8,128)(2,1)S(1)} %get-tuple-element.21), channel_id=1, source_target_pairs={{0,4},{4,8},{8,12},{12,16},{16,20},{20,24},{24,28},{1,5},{5,9},{9,... | collective-permute-start | bytes 491528 | tf_op jit(solution)/shard_map/ppermute | solution.py:291
  7.6 0.0 copy-done
  7.7 0.0 copy-done.1
  7.7 1.8 %shard_map.57 = (bf16[96,1024]{1,0:T(8,128)(2,1)S(1)}, bf16[96,1024]{1,0:T(8,128)(2,1)S(1)}, bf16[160,1024]{1,0:T(8,128)(2,1)S(1)}, bf16[160,1024]{1,0:T(8,128)(2,1)S(1)}) custom-call(bf16[256,1024]{1,0:T(8,128)(2,1)S(1)} %copy-done.1, bf16[256,256]{1,0:T(8,128)(2,1)S(1)} %copy-done.2, bf16[256,256]{1,0:T(8,128)(2,1)S(1)} %copy-done.3, ...), custom_call_target="tpu_custom_call" | custom-call | flops 134217728 | tf_op jit(solution)/shard_map/pallas_call | solution.py:32
  9.5 0.0 collective-permute-done.rest_0_
  9.5 0.1 collective-permute-start.2
  9.6 0.5 %shard_map.59.keep_ref = bf16[96,1024]{1,0:T(8,128)(2,1)S(1)} custom-call(bf16[96,1024]{1,0:T(8,128)(2,1)S(1)} %get-tuple-element.26.att_ref.high_ref, bf16[1024,4096]{1,0:T(8,128)(2,1)S(1)} %copy-done), custom_call_target="tpu_custom_call" | custom-call | flops 8589934592 | tf_op jit(solution)/shard_map/pallas_call | solution.py:32
  10.1 0.9 %collective-permute-done.2.rest_0_ = bf16[96,1024]{1,0:T(8,128)(2,1)S(1)} collective-permute-done((bf16[96,1024]{1,0:T(8,128)(2,1)S(1)}, bf16[96,1024]{1,0:T(8,128)(2,1)S(1)}, u32[]{:S(2)}, u32[]{:S(2)}) %collective-permute-start.2) | collective-permute-done | bytes 196640 | tf_op jit(solution)/shard_map/ppermute | solution.py:337
  11.1 2.0 %collective-permute-start.3 = (bf16[96,1024]{1,0:T(8,128)(2,1)S(1)}, bf16[96,1024]{1,0:T(8,128)(2,1)S(1)}, u32[]{:S(2)}, u32[]{:S(2)}) collective-permute-start(bf16[96,1024]{1,0:T(8,128)(2,1)S(1)} %shard_map.60.rest_4_), channel_id=1, source_target_pairs={{0,2},{1,3},{2,0},{3,1},{4,6},{5,7},{6,4},{7,5},{8,10},{9,11},{10,... | collective-permute-start | bytes 589832 | tf_op jit(solution)/shard_map/ppermute | solution.py:340
  13.1 0.0 collective-permute-done.1.rest_1_
  13.2 0.1 collective-permute-start.6
  13.3 0.5 %shard_map.65.keep_ref = bf16[160,1024]{1,0:T(8,128)(2,1)S(1)} custom-call(bf16[160,1024]{1,0:T(8,128)(2,1)S(1)} %get-tuple-element.28.low_ref.att_ref, bf16[1024,4096]{1,0:T(8,128)(2,1)S(1)} %copy-done), custom_call_target="tpu_custom_call" | custom-call | flops 8589934592 | tf_op jit(solution)/shard_map/pallas_call | solution.py:32
  13.8 1.1 %collective-permute-done.6.rest_0_ = bf16[160,1024]{1,0:T(8,128)(2,1)S(1)} collective-permute-done((bf16[160,1024]{1,0:T(8,128)(2,1)S(1)}, bf16[160,1024]{1,0:T(8,128)(2,1)S(1)}, u32[]{:S(2)}, u32[]{:S(2)}) %collective-permute-start.6) | collective-permute-done | bytes 327712 | tf_op jit(solution)/shard_map/ppermute | solution.py:337
  14.9 0.1 shard_map.66
  15.0 0.1 collective-permute-start.7
  15.1 3.8 %collective-permute-done.3.after.rest_0_ = bf16[96,1024]{1,0:T(8,128)(2,1)S(1)} collective-permute-done((bf16[96,1024]{1,0:T(8,128)(2,1)S(1)}, bf16[96,1024]{1,0:T(8,128)(2,1)S(1)}, u32[]{:S(2)}, u32[]{:S(2)}) %collective-permute-start.3) | collective-permute-done | bytes 196640 | tf_op jit(solution)/shard_map/ppermute | solution.py:340
  18.9 0.7 %shard_map.62 = (bf16[256,1024]{1,0:T(8,128)(2,1)S(1)}, bf16[256,512]{1,0:T(8,128)(2,1)S(1)}, bf16[256,512]{1,0:T(8,128)(2,1)S(1)}) custom-call(bf16[160,1024]{1,0:T(8,128)(2,1)S(1)} %get-tuple-element.28.low_ref.att_ref, bf16[96,1024]{1,0:T(8,128)(2,1)S(1)} %get-tuple-element.26.att_ref.high_ref, bf16[1024,4096]{1,0:T(8,128)(2,1)S(1)} %copy-done, ...), custom_call_target="tpu_custom_call" | custom-call | flops 1073741824 | tf_op jit(solution)/shard_map/pallas_call | solution.py:32
  19.6 0.1 collective-permute-start.4
  19.7 0.5 %collective-permute-start.5 = (bf16[256,512]{1,0:T(8,128)(2,1)S(1)}, bf16[256,512]{1,0:T(8,128)(2,1)S(1)}, u32[]{:S(2)}, u32[]{:S(2)}) collective-permute-start(bf16[256,512]{1,0:T(8,128)(2,1)S(1)} %get-tuple-element.31), channel_id=1, source_target_pairs={{0,1},{1,0},{2,3},{3,2},{4,5},{5,4},{6,7},{7,6},{8,9},{9,8},{10,11... | collective-permute-start | bytes 786440 | tf_op jit(solution)/shard_map/ppermute | solution.py:354
  20.2 0.7 %shard_map.63.keep_ref = bf16[256,1024]{1,0:T(8,128)(2,1)S(1)} custom-call(bf16[256,1024]{1,0:T(8,128)(2,1)S(1)} %get-tuple-element.29.att_ref, bf16[1024,4096]{1,0:T(8,128)(2,1)S(1)} %copy-done), custom_call_target="tpu_custom_call" | custom-call | tf_op jit(solution)/shard_map/pallas_call | solution.py:32
  20.9 0.3 %collective-permute-done.4.rest_0_ = bf16[256,512]{1,0:T(8,128)(2,1)S(1)} collective-permute-done((bf16[256,512]{1,0:T(8,128)(2,1)S(1)}, bf16[256,512]{1,0:T(8,128)(2,1)S(1)}, u32[]{:S(2)}, u32[]{:S(2)}) %collective-permute-start.4) | collective-permute-done | bytes 262176 | tf_op jit(solution)/shard_map/ppermute | solution.py:354
  21.2 0.4 %collective-permute-done.5.rest_1_ = bf16[256,512]{1,0:T(8,128)(2,1)S(1)} collective-permute-done((bf16[256,512]{1,0:T(8,128)(2,1)S(1)}, bf16[256,512]{1,0:T(8,128)(2,1)S(1)}, u32[]{:S(2)}, u32[]{:S(2)}) %collective-permute-start.5) | collective-permute-done | bytes 262176 | tf_op jit(solution)/shard_map/ppermute | solution.py:354
  21.6 0.1 shard_map.64.local_ref
  21.7 0.7 %shard_map.67.rest_1_ = bf16[256,1024]{1,0:T(8,128)(2,1)} custom-call(f32[256,1024]{1,0:T(8,128)S(1)} %shard_map.64.local_ref, bf16[96,1024]{1,0:T(8,128)(2,1)S(1)} %collective-permute-done.3.after.rest_0_), custom_call_target="tpu_custom_call" | custom-call | tf_op jit(solution)/shard_map/pallas_call | solution.py:357
  22.4 3.0 %collective-permute-done.7.rest_0_ = bf16[160,1024]{1,0:T(8,128)(2,1)S(1)} collective-permute-done((bf16[160,1024]{1,0:T(8,128)(2,1)S(1)}, bf16[160,1024]{1,0:T(8,128)(2,1)S(1)}, u32[]{:S(2)}, u32[]{:S(2)}) %collective-permute-start.7) | collective-permute-done | bytes 327712 | tf_op jit(solution)/shard_map/ppermute | solution.py:340
  25.4 0.8 %shard_map.68 = bf16[256,1024]{1,0:T(8,128)(2,1)} custom-call(f32[256,1024]{1,0:T(8,128)S(1)} %shard_map.64.local_ref, bf16[160,1024]{1,0:T(8,128)(2,1)S(1)} %collective-permute-done.7.rest_0_, bf16[256,1024]{1,0:T(8,128)(2,1)} %shard_map.67.rest_1_), custom_call_target="tpu_custom_call", output_to_operand_aliasing={{}: (2, {})} | custom-call | tf_op jit(solution)/shard_map/pallas_call | solution.py:357
  (8 shorter events, 0.1 us)
Async XLA Ops:
  0.0 4.1 %copy-start.2 = (bf16[256,256]{1,0:T(8,128)(2,1)S(1)}, bf16[256,256]{1,0:T(8,128)(2,1)}, u32[]{:S(2)}) copy-start(bf16[256,256]{1,0:T(8,128)(2,1)} %k_ref.7) | copy-start | bytes 393220
  0.0 4.1 %copy-start.3 = (bf16[256,256]{1,0:T(8,128)(2,1)S(1)}, bf16[256,256]{1,0:T(8,128)(2,1)}, u32[]{:S(2)}) copy-start(bf16[256,256]{1,0:T(8,128)(2,1)} %v_ref.7) | copy-start | bytes 393220
  0.0 4.1 %copy-start.4 = (s32[256]{0:T(256)S(1)}, s32[256]{0:T(256)}, u32[]{:S(2)}) copy-start(s32[256]{0:T(256)} %param.8) | copy-start | bytes 3076
  0.0 7.6 %copy-start = (bf16[1024,4096]{1,0:T(8,128)(2,1)S(1)}, bf16[1024,4096]{1,0:T(8,128)(2,1)}, u32[]{:S(2)}) copy-start(bf16[1024,4096]{1,0:T(8,128)(2,1)} %w_ref.13) | copy-start | bytes 25165828
  0.0 7.7 %copy-start.1 = (bf16[256,1024]{1,0:T(8,128)(2,1)S(1)}, bf16[256,1024]{1,0:T(8,128)(2,1)}, u32[]{:S(2)}) copy-start(bf16[256,1024]{1,0:T(8,128)(2,1)} %q_ref.5) | copy-start | bytes 1572868
  1.1 8.4 %collective-permute-start = (bf16[208,256]{1,0:T(8,128)(2,1)S(1)}, bf16[208,256]{1,0:T(8,128)(2,1)S(1)}, u32[]{:S(2)}, u32[]{:S(2)}) collective-permute-start(bf16[208,256]{1,0:T(8,128)(2,1)S(1)} %shard_map.56), channel_id=1, source_target_pairs={{0,4},{4,8},{8,12},{12,16},{16,20},{20,24},{24,28},{28,0},{1,5},{5... | collective-permute-start | bytes 319496 | tf_op jit(solution)/shard_map/ppermute | solution.py:290
  4.2 8.9 %collective-permute-start.1 = (bf16[320,256]{1,0:T(8,128)(2,1)S(1)}, bf16[320,256]{1,0:T(8,128)(2,1)S(1)}, u32[]{:S(2)}, u32[]{:S(2)}) collective-permute-start(bf16[320,256]{1,0:T(8,128)(2,1)S(1)} %get-tuple-element.21), channel_id=1, source_target_pairs={{0,4},{4,8},{8,12},{12,16},{16,20},{20,24},{24,28},{1,5},{5,9},{9,... | collective-permute-start | bytes 491528 | tf_op jit(solution)/shard_map/ppermute | solution.py:291
  9.5 1.5 %collective-permute-start.2 = (bf16[96,1024]{1,0:T(8,128)(2,1)S(1)}, bf16[96,1024]{1,0:T(8,128)(2,1)S(1)}, u32[]{:S(2)}, u32[]{:S(2)}) collective-permute-start(bf16[96,1024]{1,0:T(8,128)(2,1)S(1)} %get-tuple-element.27), channel_id=1, source_target_pairs={{0,1},{1,0},{2,3},{3,2},{4,5},{5,4},{6,7},{7,6},{8,9},{9,8},{10,11... | collective-permute-start | bytes 589832 | tf_op jit(solution)/shard_map/ppermute | solution.py:337
  11.1 7.8 %collective-permute-start.3 = (bf16[96,1024]{1,0:T(8,128)(2,1)S(1)}, bf16[96,1024]{1,0:T(8,128)(2,1)S(1)}, u32[]{:S(2)}, u32[]{:S(2)}) collective-permute-start(bf16[96,1024]{1,0:T(8,128)(2,1)S(1)} %shard_map.60.rest_4_), channel_id=1, source_target_pairs={{0,2},{1,3},{2,0},{3,1},{4,6},{5,7},{6,4},{7,5},{8,10},{9,11},{10,... | collective-permute-start | bytes 589832 | tf_op jit(solution)/shard_map/ppermute | solution.py:340
  13.2 1.7 %collective-permute-start.6 = (bf16[160,1024]{1,0:T(8,128)(2,1)S(1)}, bf16[160,1024]{1,0:T(8,128)(2,1)S(1)}, u32[]{:S(2)}, u32[]{:S(2)}) collective-permute-start(bf16[160,1024]{1,0:T(8,128)(2,1)S(1)} %get-tuple-element.32), channel_id=1, source_target_pairs={{0,1},{1,0},{2,3},{3,2},{4,5},{5,4},{6,7},{7,6},{8,9},{9,8},{10,11... | collective-permute-start | bytes 983048 | tf_op jit(solution)/shard_map/ppermute | solution.py:337
  15.0 10.4 %collective-permute-start.7 = (bf16[160,1024]{1,0:T(8,128)(2,1)S(1)}, bf16[160,1024]{1,0:T(8,128)(2,1)S(1)}, u32[]{:S(2)}, u32[]{:S(2)}) collective-permute-start(bf16[160,1024]{1,0:T(8,128)(2,1)S(1)} %shard_map.66), channel_id=1, source_target_pairs={{0,2},{1,3},{2,0},{3,1},{4,6},{5,7},{6,4},{7,5},{8,10},{9,11},{10,... | collective-permute-start | bytes 983048 | tf_op jit(solution)/shard_map/ppermute | solution.py:340
  19.6 1.6 %collective-permute-start.4 = (bf16[256,512]{1,0:T(8,128)(2,1)S(1)}, bf16[256,512]{1,0:T(8,128)(2,1)S(1)}, u32[]{:S(2)}, u32[]{:S(2)}) collective-permute-start(bf16[256,512]{1,0:T(8,128)(2,1)S(1)} %get-tuple-element.30), channel_id=1, source_target_pairs={{0,1},{1,0},{2,3},{3,2},{4,5},{5,4},{6,7},{7,6},{8,9},{9,8},{10,11... | collective-permute-start | bytes 786440 | tf_op jit(solution)/shard_map/ppermute | solution.py:354
  19.7 1.9 %collective-permute-start.5 = (bf16[256,512]{1,0:T(8,128)(2,1)S(1)}, bf16[256,512]{1,0:T(8,128)(2,1)S(1)}, u32[]{:S(2)}, u32[]{:S(2)}) collective-permute-start(bf16[256,512]{1,0:T(8,128)(2,1)S(1)} %get-tuple-element.31), channel_id=1, source_target_pairs={{0,1},{1,0},{2,3},{3,2},{4,5},{5,4},{6,7},{7,6},{8,9},{9,8},{10,11... | collective-permute-start | bytes 786440 | tf_op jit(solution)/shard_map/ppermute | solution.py:354

commit v6 on v5

--- a/solution.py
+++ b/solution.py
@@ -12,6 +12,7 @@
 CORES = 2
 CUT = 160 / 256
 DOC_ROWS = 16
+PIECES = 2
 LOG2_SCALE = math.log2(math.e) / math.sqrt(HEAD_DIM)
 HIDDEN = -1e30
 NT = (((1,), (1,)), ((), ()))
@@ -165,24 +166,26 @@
     return lax.rem(chip + d, chips) * CORES + lax.rem(core + which, CORES)
 
 
-def project(att, w_ref, d, which, out_ref):
+def project(att, w_ref, d, which, out_refs):
     block = w_ref.shape[1] // lax.axis_size("head")
     start = pl.multiple_of(owner(d, which) * block, block)
-    out_ref[...] = jnp.dot(
-        att, w_ref[:, pl.ds(start, block)], preferred_element_type=jnp.float32
-    ).astype(jnp.bfloat16)
+    share = jnp.dot(att, w_ref[:, pl.ds(start, block)], preferred_element_type=jnp.float32)
+    cols = block // len(out_refs)
+    for i, ref in enumerate(out_refs):
+        ref[...] = share[:, i * cols : (i + 1) * cols].astype(jnp.bfloat16)
 
 
 def give_shares(first, chips, refs, highs, lows, w_ref, att_ref, gives):
     attend(first, *refs, highs, lows, att_ref)
     att = att_ref[...]
+    pieces = len(gives) // (chips - 1)
     for d in range(1, chips):
-        project(att, w_ref, d, 1, gives[d - 1])
-
-
-def first_kernel(cut, chips, q_ref, k_ref, v_ref, bias_ref, column_ref, w_ref, *outs):
+        project(att, w_ref, d, 1, gives[(d - 1) * pieces : d * pieces])
+
+
+def first_kernel(cut, chips, n_outs, q_ref, k_ref, v_ref, bias_ref, column_ref, w_ref, *outs):
     refs = (q_ref, bias_ref, column_ref, k_ref, v_ref)
-    highs, lows = outs[:chips], outs[chips:]
+    highs, lows = outs[:n_outs], outs[n_outs:]
 
     @pl.when(lax.axis_index("ctx") == 0)
     def _():
@@ -191,11 +194,11 @@
 
 
 def give_kernel(
-    first, chips, n_high, n_low, q_ref, k_ref, v_ref, bias_ref, column_ref, w_ref, *rest
+    first, chips, n_outs, n_high, n_low, q_ref, k_ref, v_ref, bias_ref, column_ref, w_ref, *rest
 ):
-    outs = rest[-chips:]
+    outs = rest[-n_outs:]
     highs, lows = list(rest[:n_high]), list(rest[n_high : n_high + n_low])
-    done = rest[n_high + n_low : n_high + n_low + chips]
+    done = rest[n_high + n_low : n_high + n_low + n_outs]
     lows += [None] * (n_high - n_low)
     refs = (q_ref, bias_ref, column_ref, k_ref, v_ref)
     here = lax.axis_index("ctx")
@@ -210,13 +213,15 @@
         give_shares(first, chips, refs, highs, lows, w_ref, outs[0], outs[1:])
 
 
-def keep_kernel(first, att_ref, w_ref, *outs):
+def keep_kernel(first, chips, att_ref, w_ref, *outs):
     att = att_ref[...]
-    for i, out_ref in enumerate(outs):
-        project(att, w_ref, first + i, 0, out_ref)
-
-
-def local_kernel(low_ref, high_ref, w_ref, after, att_ref, *gives):
+    pieces = len(outs) // chips
+    for i in range(chips):
+        project(att, w_ref, first + i, 0, outs[i * pieces : (i + 1) * pieces])
+
+
+def local_kernel(low_ref, high_ref, w_ref, *rest):
+    att_ref, *gives = rest[-3:]
     rows = low_ref.shape[0]
     att_ref[:rows] = low_ref[...]
     att_ref[rows:] = high_ref[...]
@@ -238,14 +243,17 @@
         at += got.shape[1]
 
 
-def final_kernel(first, count, local_ref, *rest):
+def final_kernel(first, pieces, count, local_ref, *rest):
     out_hbm, held, sem = rest[-3:]
-    here = pl.ds(first, held.shape[0])
-    total = local_ref[here, :]
-    for got in rest[:count]:
-        total = total + got[...].astype(jnp.float32)
-    held[...] = total.astype(jnp.bfloat16)
-    copy = pltpu.make_async_copy(held, out_hbm.at[here], sem)
+    rows, block = held.shape
+    cols = block // pieces
+    for i in range(pieces):
+        here = slice(i * cols, (i + 1) * cols)
+        total = local_ref[first : first + rows, here]
+        for got in rest[i:count:pieces]:
+            total = total + got[...].astype(jnp.float32)
+        held[:, here] = total.astype(jnp.bfloat16)
+    copy = pltpu.make_async_copy(held, out_hbm.at[pl.ds(first, rows)], sem)
     copy.start()
     copy.wait()
 
@@ -292,11 +300,11 @@
 
     other_core = [(i, i ^ 1) for i in range(devices)]
 
-    def keep_shares(att, first, count, flops):
-        keep = pltpu.VMEM((att.shape[0], block), bf16)
+    def keep_shares(att, first, count, pieces, flops):
+        keep = pltpu.VMEM((att.shape[0], block // pieces), bf16)
         return call(
-            functools.partial(keep_kernel, first),
-            [keep] * count,
+            functools.partial(keep_kernel, first, count),
+            [keep] * (count * pieces),
             [VMEM] * 2,
             (near(att), out_weight),
             flops=flops,
@@ -310,52 +318,58 @@
             tuple(map(near, (keep, *got))),
         )
 
-    def outputs(rows):
-        return [pltpu.VMEM((rows, width), bf16)] + [pltpu.VMEM((rows, block), bf16)] * (chips - 1)
+    def outputs(rows, pieces):
+        share = pltpu.VMEM((rows, block // pieces), bf16)
+        return [pltpu.VMEM((rows, width), bf16)] + [share] * ((chips - 1) * pieces)
 
     always = (queries, keys, values, near(bias), near(column), out_weight)
     done = call(
-        functools.partial(first_kernel, cut, chips),
-        outputs(tokens - cut) + outputs(cut),
+        functools.partial(first_kernel, cut, chips, 1 + (chips - 1) * PIECES),
+        outputs(tokens - cut, PIECES) + outputs(cut, 1),
         [VMEM] * len(always),
         always,
         flops=2**27,
     )
 
-    def shares(first, rows, lows, done, *after):
+    def shares(first, rows, pieces, keep_flops, lows, done, *after):
         prevs = highs + lows + done
         att, *gives = call(
-            functools.partial(give_kernel, first, chips, len(highs), len(lows)),
-            outputs(rows),
+            functools.partial(give_kernel, first, chips, len(done), len(highs), len(lows)),
+            outputs(rows, pieces),
             [VMEM] * (len(always) + len(prevs)) + [ANY] * len(after),
             (*always, *map(near, prevs), *after),
             flops=8 * tokens * width * block,
         )
-        keeps = keep_shares(att, 1, chips - 1, 2**33)
+        keeps = keep_shares(att, 1, chips - 1, pieces, keep_flops)
         sums, arrived = [], []
-        for d in range(1, chips):
-            total = add(keeps[d - 1], bf16, lax.ppermute(gives[d - 1], "head", other_core))
-            pairs = [(i, (i + d * CORES) % devices) for i in range(devices)]
+        for i, (keep, give) in enumerate(zip(keeps, gives)):
+            total = add(keep, bf16, lax.ppermute(give, "head", other_core))
+            step = (i // pieces + 1) * CORES
             sums.append(total)
-            arrived.append(lax.ppermute(total, "head", pairs))
+            arrived.append(
+                lax.ppermute(total, "head", [(j, (j + step) % devices) for j in range(devices)])
+            )
         return att, sums, arrived
 
-    att_high, sums, high = shares(cut, tokens - cut, lows[:-1], list(done[:chips]))
-    att_low, sums, low = shares(0, cut, lows, list(done[chips:]), sums[-1])
+    n_done = 1 + (chips - 1) * PIECES
+    att_high, sums, high = shares(
+        cut, tokens - cut, PIECES, 2**33, lows[:-1], list(done[:n_done])
+    )
+    att_low, sums, low = shares(0, cut, 1, 2**33, lows, list(done[n_done:]), *sums)
 
     att, *gives = call(
         local_kernel,
         [pltpu.VMEM((tokens, width), bf16)] + [pltpu.VMEM((tokens, block // 2), bf16)] * 2,
-        [VMEM] * 3 + [ANY],
-        (near(att_low), near(att_high), out_weight, high[-1]),
+        [VMEM] * 3 + [ANY] * len(high),
+        (near(att_low), near(att_high), out_weight, *high),
         flops=4 * tokens * width * block,
     )
-    (keep,) = keep_shares(att, 0, 1, 0)
+    (keep,) = keep_shares(att, 0, 1, 1, 0)
     local = add(keep, f32, *[lax.ppermute(give, "head", other_core) for give in gives])
 
-    def finish(first, rows, arrived, *out):
+    def finish(first, rows, pieces, arrived, *out):
         return pl.pallas_call(
-            functools.partial(final_kernel, first, len(arrived)),
+            functools.partial(final_kernel, first, pieces, len(arrived)),
             out_shape=pltpu.HBM((tokens, block), bf16),
             in_specs=[VMEM] * (1 + len(arrived)) + [HBM] * len(out),
             out_specs=HBM,
@@ -364,7 +378,7 @@
             cost_estimate=pl.CostEstimate(flops=0, bytes_accessed=0, transcendentals=0),
         )(near(local), *map(near, arrived), *out)
 
-    return finish(0, cut, low, finish(cut, tokens - cut, high))
+    return finish(0, cut, 1, low, finish(cut, tokens - cut, PIECES, high))
 
 
 def solution(mesh):

time: 26.3 us -> 26.5 us (level)
  starting transfers between devices: 9.33 us -> 11.9 us
  waiting for transfers between devices: 9.44 us -> 7.09 us
    ppermute x4 -> x6, starting transfers between devices: 2.3 us -> 4.88 us  [the longest x3 4.2 us: shares(): lax.ppermute(total, 'head', [(j, (j + step) % devices) for j in range(dev...]
    ppermute x4 -> x6, waiting for transfers between devices: 8.75 us -> 6.41 us  [the longest x3 4.87 us: shares(): lax.ppermute(total, 'head', [(j, (j + step) % devices) for j in range(dev...]
    pallas_call x12 -> x13, Pallas kernels: 5.68 us -> 5.66 us  [call(): pl.pallas_call(kernel, out_shape=out_shape, in_specs=in_specs, out_specs=...]
  transfers between devices with their start and end apart: 8 -> 10, of which waited for: 6 -> 6; matrix products, arithmetic and copies ran while one was open for 0% -> 0% of each run, Pallas kernels for 21% -> 20%
where the time goes in v6:
time: 26.5 us; the launch traced here: 26.4 us
  starting transfers between devices  11.9 us (45%)
  Pallas kernels  7.18 us (27%)
  waiting for transfers between devices  7.09 us (27%)
    pallas_call x13, Pallas kernels, call(): pl.pallas_call(kernel, out_shape=out_shape, in_specs=in_specs, out_specs=...  5.66 us
    ppermute x3, waiting for transfers between devices, shares(): lax.ppermute(total, 'head', [(j, (j + step) % devices) for j in range(dev...  4.87 us
    ppermute x3, starting transfers between devices, shares(): lax.ppermute(total, 'head', [(j, (j + step) % devices) for j in range(dev...  4.2 us
    ppermute x1, starting transfers between devices, body(): lows.append(lax.ppermute(packed_low, 'ctx', ring[:place_count - s]))  3.43 us
    ppermute x1, starting transfers between devices, body(): highs.append(lax.ppermute(packed_high, 'ctx', ring))  3.03 us
    ppermute x3, waiting for transfers between devices, shares(): total = add(keep, bf16, lax.ppermute(give, 'head', other_core))  1.54 us
    pallas_call x2, Pallas kernels, finish(): pl.pallas_call(functools.partial(final_kernel, first, pieces, len(arrived...  1.51 us
    ppermute x2, waiting for transfers between devices, body(): lax.ppermute(give, 'head', other_core)  0.68 us
  transfers between devices with their start and end apart: 10, of which 6 were waited for; matrix products, arithmetic and copies ran while one was open for 0% of the time, Pallas kernels for 20%

profile of v6, /device:TPU:0, one launch (start us, length us, event | category | flops | bytes accessed | tf_op | source)
XLA Modules:
  0.0 26.4 jit_solution(134678891694612729)
XLA Ops:
  0.0 1.0 %shard_map.56 = bf16[208,256]{1,0:T(8,128)(2,1)S(1)} custom-call(bf16[256,256]{1,0:T(8,128)(2,1)} %k_ref.7, bf16[256,256]{1,0:T(8,128)(2,1)} %v_ref.7, s32[1,256]{1,0:T(1,128)} %bitcast.1), custom_call_target="tpu_custom_call" | custom-call | flops 8589934592 | tf_op jit(solution)/shard_map/pallas_call | solution.py:33
  1.1 3.0 %collective-permute-start = (bf16[208,256]{1,0:T(8,128)(2,1)S(1)}, bf16[208,256]{1,0:T(8,128)(2,1)S(1)}, u32[]{:S(2)}, u32[]{:S(2)}) collective-permute-start(bf16[208,256]{1,0:T(8,128)(2,1)S(1)} %shard_map.56), channel_id=1, source_target_pairs={{0,4},{4,8},{8,12},{12,16},{16,20},{20,24},{24,28},{28,0},{1,5},{5... | collective-permute-start | bytes 319496 | tf_op jit(solution)/shard_map/ppermute | solution.py:298
  4.1 0.0 copy-done.2
  4.1 0.1 shard_map.55
  4.2 3.4 %collective-permute-start.1 = (bf16[320,256]{1,0:T(8,128)(2,1)S(1)}, bf16[320,256]{1,0:T(8,128)(2,1)S(1)}, u32[]{:S(2)}, u32[]{:S(2)}) collective-permute-start(bf16[320,256]{1,0:T(8,128)(2,1)S(1)} %get-tuple-element.25), channel_id=1, source_target_pairs={{0,4},{4,8},{8,12},{12,16},{16,20},{20,24},{24,28},{1,5},{5,9},{9,... | collective-permute-start | bytes 491528 | tf_op jit(solution)/shard_map/ppermute | solution.py:299
  7.7 1.8 %shard_map.57 = (bf16[96,1024]{1,0:T(8,128)(2,1)S(1)}, bf16[96,512]{1,0:T(8,128)(2,1)S(1)}, bf16[96,512]{1,0:T(8,128)(2,1)S(1)}, bf16[160,1024]{1,0:T(8,128)(2,1)S(1)}, bf16[160,1024]{1,0:T(8,128)(2,1)S(1)}) custom-call(bf16[256,1024]{1,0:T(8,128)(2,1)S(1)} %copy-done.1, bf16[256,256]{1,0:T(8,128)(2,1)S(1)} %copy-done.2, bf16[256,256]{1,0:T(8,128)(2,1)S(1)} %copy-done.3, ...), custom_call_target="tpu_custom_call" | custom-call | flops 134217728 | tf_op jit(solution)/shard_map/pallas_call | solution.py:33
  9.5 0.0 collective-permute-done.rest_0_
  9.5 0.1 collective-permute-start.2
  9.6 0.5 %collective-permute-start.3 = (bf16[96,512]{1,0:T(8,128)(2,1)S(1)}, bf16[96,512]{1,0:T(8,128)(2,1)S(1)}, u32[]{:S(2)}, u32[]{:S(2)}) collective-permute-start(bf16[96,512]{1,0:T(8,128)(2,1)S(1)} %get-tuple-element.35), channel_id=1, source_target_pairs={{0,1},{1,0},{2,3},{3,2},{4,5},{5,4},{6,7},{7,6},{8,9},{9,8},{10,11... | collective-permute-start | bytes 294920 | tf_op jit(solution)/shard_map/ppermute | solution.py:346
  10.1 0.5 %shard_map.59 = (bf16[96,512]{1,0:T(8,128)(2,1)S(1)}, bf16[96,512]{1,0:T(8,128)(2,1)S(1)}) custom-call(bf16[96,1024]{1,0:T(8,128)(2,1)S(1)} %get-tuple-element.31.att_ref.high_ref, bf16[1024,4096]{1,0:T(8,128)(2,1)S(1)} %copy-done), custom_call_target="tpu_custom_call" | custom-call | flops 8589934592 | tf_op jit(solution)/shard_map/pallas_call | solution.py:33
  10.6 0.5 %collective-permute-done.3.rest_0_ = bf16[96,512]{1,0:T(8,128)(2,1)S(1)} collective-permute-done((bf16[96,512]{1,0:T(8,128)(2,1)S(1)}, bf16[96,512]{1,0:T(8,128)(2,1)S(1)}, u32[]{:S(2)}, u32[]{:S(2)}) %collective-permute-start.3) | collective-permute-done | bytes 98336 | tf_op jit(solution)/shard_map/ppermute | solution.py:346
  11.1 2.0 %collective-permute-start.5 = (bf16[96,512]{1,0:T(8,128)(2,1)S(1)}, bf16[96,512]{1,0:T(8,128)(2,1)S(1)}, u32[]{:S(2)}, u32[]{:S(2)}) collective-permute-start(bf16[96,512]{1,0:T(8,128)(2,1)S(1)} %shard_map.61.rest_5_), channel_id=1, source_target_pairs={{0,2},{1,3},{2,0},{3,1},{4,6},{5,7},{6,4},{7,5},{8,10},{9,11},{10,... | collective-permute-start | bytes 294920 | tf_op jit(solution)/shard_map/ppermute | solution.py:350
  13.1 0.0 collective-permute-done.2.rest_0_
  13.2 0.1 collective-permute-start.4
  13.3 0.0 collective-permute-done.1.rest_1_
  13.3 0.1 collective-permute-start.8
  13.5 0.5 %shard_map.66.keep_ref = bf16[160,1024]{1,0:T(8,128)(2,1)S(1)} custom-call(bf16[160,1024]{1,0:T(8,128)(2,1)S(1)} %get-tuple-element.36.low_ref.att_ref, bf16[1024,4096]{1,0:T(8,128)(2,1)S(1)} %copy-done), custom_call_target="tpu_custom_call" | custom-call | flops 8589934592 | tf_op jit(solution)/shard_map/pallas_call | solution.py:33
  14.0 1.1 %collective-permute-done.8.rest_0_ = bf16[160,1024]{1,0:T(8,128)(2,1)S(1)} collective-permute-done((bf16[160,1024]{1,0:T(8,128)(2,1)S(1)}, bf16[160,1024]{1,0:T(8,128)(2,1)S(1)}, u32[]{:S(2)}, u32[]{:S(2)}) %collective-permute-start.8) | collective-permute-done | bytes 327712 | tf_op jit(solution)/shard_map/ppermute | solution.py:346
  15.0 0.1 shard_map.67
  15.1 2.0 %collective-permute-start.9 = (bf16[160,1024]{1,0:T(8,128)(2,1)S(1)}, bf16[160,1024]{1,0:T(8,128)(2,1)S(1)}, u32[]{:S(2)}, u32[]{:S(2)}) collective-permute-start(bf16[160,1024]{1,0:T(8,128)(2,1)S(1)} %shard_map.67), channel_id=1, source_target_pairs={{0,2},{1,3},{2,0},{3,1},{4,6},{5,7},{6,4},{7,5},{8,10},{9,11},{10,... | collective-permute-start | bytes 983048 | tf_op jit(solution)/shard_map/ppermute | solution.py:350
  17.2 0.0 collective-permute-done.5.rest_1_
  17.2 1.7 %collective-permute-done.4.rest_0_ = bf16[96,512]{1,0:T(8,128)(2,1)S(1)} collective-permute-done((bf16[96,512]{1,0:T(8,128)(2,1)S(1)}, bf16[96,512]{1,0:T(8,128)(2,1)S(1)}, u32[]{:S(2)}, u32[]{:S(2)}) %collective-permute-start.4) | collective-permute-done | bytes 98336 | tf_op jit(solution)/shard_map/ppermute | solution.py:350
  18.9 0.7 %shard_map.63 = (bf16[256,1024]{1,0:T(8,128)(2,1)S(1)}, bf16[256,512]{1,0:T(8,128)(2,1)S(1)}, bf16[256,512]{1,0:T(8,128)(2,1)S(1)}) custom-call(bf16[160,1024]{1,0:T(8,128)(2,1)S(1)} %get-tuple-element.36.low_ref.att_ref, bf16[96,1024]{1,0:T(8,128)(2,1)S(1)} %get-tuple-element.31.att_ref.high_ref, bf16[1024,4096]{1,0:T(8,128)(2,1)S(1)} %copy-done, ...), custom_call_target="tpu_custom_call" | custom-call | flops 1073741824 | tf_op jit(solution)/shard_map/pallas_call | solution.py:33
  19.6 0.1 collective-permute-start.6
  19.7 0.5 %collective-permute-start.7 = (bf16[256,512]{1,0:T(8,128)(2,1)S(1)}, bf16[256,512]{1,0:T(8,128)(2,1)S(1)}, u32[]{:S(2)}, u32[]{:S(2)}) collective-permute-start(bf16[256,512]{1,0:T(8,128)(2,1)S(1)} %get-tuple-element.39), channel_id=1, source_target_pairs={{0,1},{1,0},{2,3},{3,2},{4,5},{5,4},{6,7},{7,6},{8,9},{9,8},{10,11... | collective-permute-start | bytes 786440 | tf_op jit(solution)/shard_map/ppermute | solution.py:368
  20.2 0.7 %shard_map.64.keep_ref = bf16[256,1024]{1,0:T(8,128)(2,1)S(1)} custom-call(bf16[256,1024]{1,0:T(8,128)(2,1)S(1)} %get-tuple-element.37.att_ref, bf16[1024,4096]{1,0:T(8,128)(2,1)S(1)} %copy-done), custom_call_target="tpu_custom_call" | custom-call | tf_op jit(solution)/shard_map/pallas_call | solution.py:33
  20.9 0.3 %collective-permute-done.6.rest_0_ = bf16[256,512]{1,0:T(8,128)(2,1)S(1)} collective-permute-done((bf16[256,512]{1,0:T(8,128)(2,1)S(1)}, bf16[256,512]{1,0:T(8,128)(2,1)S(1)}, u32[]{:S(2)}, u32[]{:S(2)}) %collective-permute-start.6) | collective-permute-done | bytes 262176 | tf_op jit(solution)/shard_map/ppermute | solution.py:368
  21.2 0.4 %collective-permute-done.7.rest_1_ = bf16[256,512]{1,0:T(8,128)(2,1)S(1)} collective-permute-done((bf16[256,512]{1,0:T(8,128)(2,1)S(1)}, bf16[256,512]{1,0:T(8,128)(2,1)S(1)}, u32[]{:S(2)}, u32[]{:S(2)}) %collective-permute-start.7) | collective-permute-done | bytes 262176 | tf_op jit(solution)/shard_map/ppermute | solution.py:368
  21.6 0.1 shard_map.65.local_ref
  21.7 0.7 %shard_map.68.rest_1_ = bf16[256,1024]{1,0:T(8,128)(2,1)} custom-call(f32[256,1024]{1,0:T(8,128)S(1)} %shard_map.65.local_ref, bf16[96,512]{1,0:T(8,128)(2,1)S(1)} %collective-permute-done.4.rest_0_, bf16[96,512]{1,0:T(8,128)(2,1)S(1)} %collective-permute-done.5.rest_1_), custom_call_target="tpu_custom_call" | custom-call | tf_op jit(solution)/shard_map/pallas_call | solution.py:371
  22.4 3.1 %collective-permute-done.9.rest_0_ = bf16[160,1024]{1,0:T(8,128)(2,1)S(1)} collective-permute-done((bf16[160,1024]{1,0:T(8,128)(2,1)S(1)}, bf16[160,1024]{1,0:T(8,128)(2,1)S(1)}, u32[]{:S(2)}, u32[]{:S(2)}) %collective-permute-start.9) | collective-permute-done | bytes 327712 | tf_op jit(solution)/shard_map/ppermute | solution.py:350
  25.6 0.8 %shard_map.69 = bf16[256,1024]{1,0:T(8,128)(2,1)} custom-call(f32[256,1024]{1,0:T(8,128)S(1)} %shard_map.65.local_ref, bf16[160,1024]{1,0:T(8,128)(2,1)S(1)} %collective-permute-done.9.rest_0_, bf16[256,1024]{1,0:T(8,128)(2,1)} %shard_map.68.rest_1_), custom_call_target="tpu_custom_call", output_to_operand_aliasing={{}: (2, {})} | custom-call | tf_op jit(solution)/shard_map/pallas_call | solution.py:371
  (13 shorter events, 0.2 us)
Async XLA Ops:
  0.0 4.1 %copy-start.2 = (bf16[256,256]{1,0:T(8,128)(2,1)S(1)}, bf16[256,256]{1,0:T(8,128)(2,1)}, u32[]{:S(2)}) copy-start(bf16[256,256]{1,0:T(8,128)(2,1)} %k_ref.7) | copy-start | bytes 393220
  0.0 4.1 %copy-start.3 = (bf16[256,256]{1,0:T(8,128)(2,1)S(1)}, bf16[256,256]{1,0:T(8,128)(2,1)}, u32[]{:S(2)}) copy-start(bf16[256,256]{1,0:T(8,128)(2,1)} %v_ref.7) | copy-start | bytes 393220
  0.0 4.1 %copy-start.4 = (s32[256]{0:T(256)S(1)}, s32[256]{0:T(256)}, u32[]{:S(2)}) copy-start(s32[256]{0:T(256)} %param.8) | copy-start | bytes 3076
  0.0 7.6 %copy-start = (bf16[1024,4096]{1,0:T(8,128)(2,1)S(1)}, bf16[1024,4096]{1,0:T(8,128)(2,1)}, u32[]{:S(2)}) copy-start(bf16[1024,4096]{1,0:T(8,128)(2,1)} %w_ref.13) | copy-start | bytes 25165828
  0.0 7.7 %copy-start.1 = (bf16[256,1024]{1,0:T(8,128)(2,1)S(1)}, bf16[256,1024]{1,0:T(8,128)(2,1)}, u32[]{:S(2)}) copy-start(bf16[256,1024]{1,0:T(8,128)(2,1)} %q_ref.5) | copy-start | bytes 1572868
  1.1 8.4 %collective-permute-start = (bf16[208,256]{1,0:T(8,128)(2,1)S(1)}, bf16[208,256]{1,0:T(8,128)(2,1)S(1)}, u32[]{:S(2)}, u32[]{:S(2)}) collective-permute-start(bf16[208,256]{1,0:T(8,128)(2,1)S(1)} %shard_map.56), channel_id=1, source_target_pairs={{0,4},{4,8},{8,12},{12,16},{16,20},{20,24},{24,28},{28,0},{1,5},{5... | collective-permute-start | bytes 319496 | tf_op jit(solution)/shard_map/ppermute | solution.py:298
  4.2 9.1 %collective-permute-start.1 = (bf16[320,256]{1,0:T(8,128)(2,1)S(1)}, bf16[320,256]{1,0:T(8,128)(2,1)S(1)}, u32[]{:S(2)}, u32[]{:S(2)}) collective-permute-start(bf16[320,256]{1,0:T(8,128)(2,1)S(1)} %get-tuple-element.25), channel_id=1, source_target_pairs={{0,4},{4,8},{8,12},{12,16},{16,20},{20,24},{24,28},{1,5},{5,9},{9,... | collective-permute-start | bytes 491528 | tf_op jit(solution)/shard_map/ppermute | solution.py:299
  9.5 3.6 %collective-permute-start.2 = (bf16[96,512]{1,0:T(8,128)(2,1)S(1)}, bf16[96,512]{1,0:T(8,128)(2,1)S(1)}, u32[]{:S(2)}, u32[]{:S(2)}) collective-permute-start(bf16[96,512]{1,0:T(8,128)(2,1)S(1)} %get-tuple-element.33), channel_id=1, source_target_pairs={{0,1},{1,0},{2,3},{3,2},{4,5},{5,4},{6,7},{7,6},{8,9},{9,8},{10,11... | collective-permute-start | bytes 294920 | tf_op jit(solution)/shard_map/ppermute | solution.py:346
  9.6 1.4 %collective-permute-start.3 = (bf16[96,512]{1,0:T(8,128)(2,1)S(1)}, bf16[96,512]{1,0:T(8,128)(2,1)S(1)}, u32[]{:S(2)}, u32[]{:S(2)}) collective-permute-start(bf16[96,512]{1,0:T(8,128)(2,1)S(1)} %get-tuple-element.35), channel_id=1, source_target_pairs={{0,1},{1,0},{2,3},{3,2},{4,5},{5,4},{6,7},{7,6},{8,9},{9,8},{10,11... | collective-permute-start | bytes 294920 | tf_op jit(solution)/shard_map/ppermute | solution.py:346
  11.1 6.1 %collective-permute-start.5 = (bf16[96,512]{1,0:T(8,128)(2,1)S(1)}, bf16[96,512]{1,0:T(8,128)(2,1)S(1)}, u32[]{:S(2)}, u32[]{:S(2)}) collective-permute-start(bf16[96,512]{1,0:T(8,128)(2,1)S(1)} %shard_map.61.rest_5_), channel_id=1, source_target_pairs={{0,2},{1,3},{2,0},{3,1},{4,6},{5,7},{6,4},{7,5},{8,10},{9,11},{10,... | collective-permute-start | bytes 294920 | tf_op jit(solution)/shard_map/ppermute | solution.py:350
  13.2 5.7 %collective-permute-start.4 = (bf16[96,512]{1,0:T(8,128)(2,1)S(1)}, bf16[96,512]{1,0:T(8,128)(2,1)S(1)}, u32[]{:S(2)}, u32[]{:S(2)}) collective-permute-start(bf16[96,512]{1,0:T(8,128)(2,1)S(1)} %shard_map.60.rest_4_), channel_id=1, source_target_pairs={{0,2},{1,3},{2,0},{3,1},{4,6},{5,7},{6,4},{7,5},{8,10},{9,11},{10,... | collective-permute-start | bytes 294920 | tf_op jit(solution)/shard_map/ppermute | solution.py:350
  13.3 1.7 %collective-permute-start.8 = (bf16[160,1024]{1,0:T(8,128)(2,1)S(1)}, bf16[160,1024]{1,0:T(8,128)(2,1)S(1)}, u32[]{:S(2)}, u32[]{:S(2)}) collective-permute-start(bf16[160,1024]{1,0:T(8,128)(2,1)S(1)} %get-tuple-element.40), channel_id=1, source_target_pairs={{0,1},{1,0},{2,3},{3,2},{4,5},{5,4},{6,7},{7,6},{8,9},{9,8},{10,11... | collective-permute-start | bytes 983048 | tf_op jit(solution)/shard_map/ppermute | solution.py:346
  15.1 10.4 %collective-permute-start.9 = (bf16[160,1024]{1,0:T(8,128)(2,1)S(1)}, bf16[160,1024]{1,0:T(8,128)(2,1)S(1)}, u32[]{:S(2)}, u32[]{:S(2)}) collective-permute-start(bf16[160,1024]{1,0:T(8,128)(2,1)S(1)} %shard_map.67), channel_id=1, source_target_pairs={{0,2},{1,3},{2,0},{3,1},{4,6},{5,7},{6,4},{7,5},{8,10},{9,11},{10,... | collective-permute-start | bytes 983048 | tf_op jit(solution)/shard_map/ppermute | solution.py:350
  19.6 1.6 %collective-permute-start.6 = (bf16[256,512]{1,0:T(8,128)(2,1)S(1)}, bf16[256,512]{1,0:T(8,128)(2,1)S(1)}, u32[]{:S(2)}, u32[]{:S(2)}) collective-permute-start(bf16[256,512]{1,0:T(8,128)(2,1)S(1)} %get-tuple-element.38), channel_id=1, source_target_pairs={{0,1},{1,0},{2,3},{3,2},{4,5},{5,4},{6,7},{7,6},{8,9},{9,8},{10,11... | collective-permute-start | bytes 786440 | tf_op jit(solution)/shard_map/ppermute | solution.py:368
  19.7 1.9 %collective-permute-start.7 = (bf16[256,512]{1,0:T(8,128)(2,1)S(1)}, bf16[256,512]{1,0:T(8,128)(2,1)S(1)}, u32[]{:S(2)}, u32[]{:S(2)}) collective-permute-start(bf16[256,512]{1,0:T(8,128)(2,1)S(1)} %get-tuple-element.39), channel_id=1, source_target_pairs={{0,1},{1,0},{2,3},{3,2},{4,5},{5,4},{6,7},{7,6},{8,9},{9,8},{10,11... | collective-permute-start | bytes 786440 | tf_op jit(solution)/shard_map/ppermute | solution.py:368

commit v7 on v6

--- a/solution.py
+++ b/solution.py
@@ -12,7 +12,8 @@
 CORES = 2
 CUT = 160 / 256
 DOC_ROWS = 16
-PIECES = 2
+PIECES = 1
+LOW_PIECES = 2
 LOG2_SCALE = math.log2(math.e) / math.sqrt(HEAD_DIM)
 HIDDEN = -1e30
 NT = (((1,), (1,)), ((), ()))
@@ -221,7 +222,7 @@
 
 
 def local_kernel(low_ref, high_ref, w_ref, *rest):
-    att_ref, *gives = rest[-3:]
+    att_ref, *gives = rest[-2:]
     rows = low_ref.shape[0]
     att_ref[:rows] = low_ref[...]
     att_ref[rows:] = high_ref[...]
@@ -325,7 +326,7 @@
     always = (queries, keys, values, near(bias), near(column), out_weight)
     done = call(
         functools.partial(first_kernel, cut, chips, 1 + (chips - 1) * PIECES),
-        outputs(tokens - cut, PIECES) + outputs(cut, 1),
+        outputs(tokens - cut, PIECES) + outputs(cut, LOW_PIECES),
         [VMEM] * len(always),
         always,
         flops=2**27,
@@ -355,16 +356,16 @@
     att_high, sums, high = shares(
         cut, tokens - cut, PIECES, 2**33, lows[:-1], list(done[:n_done])
     )
-    att_low, sums, low = shares(0, cut, 1, 2**33, lows, list(done[n_done:]), *sums)
+    att_low, sums, low = shares(0, cut, LOW_PIECES, 2**33, lows, list(done[n_done:]), *sums)
 
     att, *gives = call(
         local_kernel,
-        [pltpu.VMEM((tokens, width), bf16)] + [pltpu.VMEM((tokens, block // 2), bf16)] * 2,
+        [pltpu.VMEM((tokens, width), bf16)] + [pltpu.VMEM((tokens, block), bf16)],
         [VMEM] * 3 + [ANY] * len(high),
         (near(att_low), near(att_high), out_weight, *high),
         flops=4 * tokens * width * block,
     )
-    (keep,) = keep_shares(att, 0, 1, 1, 0)
+    (keep,) = keep_shares(att, 0, 1, 1, 2**33)
     local = add(keep, f32, *[lax.ppermute(give, "head", other_core) for give in gives])
 
     def finish(first, rows, pieces, arrived, *out):
@@ -378,7 +379,7 @@
             cost_estimate=pl.CostEstimate(flops=0, bytes_accessed=0, transcendentals=0),
         )(near(local), *map(near, arrived), *out)
 
-    return finish(0, cut, 1, low, finish(cut, tokens - cut, PIECES, high))
+    return finish(0, cut, LOW_PIECES, low, finish(cut, tokens - cut, PIECES, high))
 
 
 def solution(mesh):

time: 26.5 us -> 26.3 us (level)
  starting transfers between devices: 11.9 us -> 11.4 us
  waiting for transfers between devices: 7.09 us -> 7.38 us
    ppermute x2 -> x1, starting transfers between devices: 0.57 us -> 0.07 us  [body(): lax.ppermute(give, 'head', other_core)]
    ppermute x2 -> x1, waiting for transfers between devices: 0.68 us -> 1.16 us  [body(): lax.ppermute(give, 'head', other_core)]
  transfers between devices with their start and end apart: 10 -> 9, of which waited for: 6 -> 5; matrix products, arithmetic and copies ran while one was open for 0% -> 0% of each run, Pallas kernels for 20% -> 21%
where the time goes in v7:
time: 26.3 us; the launch traced here: 26.1 us
  starting transfers between devices  11.4 us (43%)
  waiting for transfers between devices  7.38 us (28%)
  Pallas kernels  7.2 us (27%)
    pallas_call x13, Pallas kernels, call(): pl.pallas_call(kernel, out_shape=out_shape, in_specs=in_specs, out_specs=...  5.69 us
    ppermute x3, waiting for transfers between devices, shares(): lax.ppermute(total, 'head', [(j, (j + step) % devices) for j in range(dev...  4.67 us
    ppermute x3, starting transfers between devices, shares(): lax.ppermute(total, 'head', [(j, (j + step) % devices) for j in range(dev...  4.2 us
    ppermute x1, starting transfers between devices, body(): lows.append(lax.ppermute(packed_low, 'ctx', ring[:place_count - s]))  3.43 us
    ppermute x1, starting transfers between devices, body(): highs.append(lax.ppermute(packed_high, 'ctx', ring))  3.03 us
    ppermute x3, waiting for transfers between devices, shares(): total = add(keep, bf16, lax.ppermute(give, 'head', other_core))  1.54 us
    pallas_call x2, Pallas kernels, finish(): pl.pallas_call(functools.partial(final_kernel, first, pieces, len(arrived...  1.51 us
    ppermute x1, waiting for transfers between devices, body(): lax.ppermute(give, 'head', other_core)  1.16 us
  transfers between devices with their start and end apart: 9, of which 5 were waited for; matrix products, arithmetic and copies ran while one was open for 0% of the time, Pallas kernels for 21%

profile of v7, /device:TPU:0, one launch (start us, length us, event | category | flops | bytes accessed | tf_op | source)
XLA Modules:
  0.0 26.1 jit_solution(16414161303455176708)
XLA Ops:
  0.0 1.0 %shard_map.56 = bf16[208,256]{1,0:T(8,128)(2,1)S(1)} custom-call(bf16[256,256]{1,0:T(8,128)(2,1)} %k_ref.7, bf16[256,256]{1,0:T(8,128)(2,1)} %v_ref.7, s32[1,256]{1,0:T(1,128)} %bitcast.1), custom_call_target="tpu_custom_call" | custom-call | flops 8589934592 | tf_op jit(solution)/shard_map/pallas_call | solution.py:34
  1.1 3.0 %collective-permute-start = (bf16[208,256]{1,0:T(8,128)(2,1)S(1)}, bf16[208,256]{1,0:T(8,128)(2,1)S(1)}, u32[]{:S(2)}, u32[]{:S(2)}) collective-permute-start(bf16[208,256]{1,0:T(8,128)(2,1)S(1)} %shard_map.56), channel_id=1, source_target_pairs={{0,4},{4,8},{8,12},{12,16},{16,20},{20,24},{24,28},{28,0},{1,5},{5... | collective-permute-start | bytes 319496 | tf_op jit(solution)/shard_map/ppermute | solution.py:299
  4.1 0.0 copy-done.2
  4.1 0.0 copy-done.3
  4.1 0.0 copy-done.4
  4.1 0.1 shard_map.55
  4.2 3.4 %collective-permute-start.1 = (bf16[320,256]{1,0:T(8,128)(2,1)S(1)}, bf16[320,256]{1,0:T(8,128)(2,1)S(1)}, u32[]{:S(2)}, u32[]{:S(2)}) collective-permute-start(bf16[320,256]{1,0:T(8,128)(2,1)S(1)} %get-tuple-element.24), channel_id=1, source_target_pairs={{0,4},{4,8},{8,12},{12,16},{16,20},{20,24},{24,28},{1,5},{5,9},{9,... | collective-permute-start | bytes 491528 | tf_op jit(solution)/shard_map/ppermute | solution.py:300
  7.6 0.0 copy-done
  7.7 1.8 %shard_map.57 = (bf16[96,1024]{1,0:T(8,128)(2,1)S(1)}, bf16[96,1024]{1,0:T(8,128)(2,1)S(1)}, bf16[160,1024]{1,0:T(8,128)(2,1)S(1)}, bf16[160,512]{1,0:T(8,128)(2,1)S(1)}, bf16[160,512]{1,0:T(8,128)(2,1)S(1)}) custom-call(bf16[256,1024]{1,0:T(8,128)(2,1)S(1)} %copy-done.1, bf16[256,256]{1,0:T(8,128)(2,1)S(1)} %copy-done.2, bf16[256,256]{1,0:T(8,128)(2,1)S(1)} %copy-done.3, ...), custom_call_target="tpu_custom_call" | custom-call | flops 134217728 | tf_op jit(solution)/shard_map/pallas_call | solution.py:34
  9.5 0.0 collective-permute-done.rest_0_
  9.5 0.1 collective-permute-start.2
  9.6 0.5 %shard_map.59.keep_ref = bf16[96,1024]{1,0:T(8,128)(2,1)S(1)} custom-call(bf16[96,1024]{1,0:T(8,128)(2,1)S(1)} %get-tuple-element.30.att_ref.high_ref, bf16[1024,4096]{1,0:T(8,128)(2,1)S(1)} %copy-done), custom_call_target="tpu_custom_call" | custom-call | flops 8589934592 | tf_op jit(solution)/shard_map/pallas_call | solution.py:34
  10.1 0.9 %collective-permute-done.2.rest_0_ = bf16[96,1024]{1,0:T(8,128)(2,1)S(1)} collective-permute-done((bf16[96,1024]{1,0:T(8,128)(2,1)S(1)}, bf16[96,1024]{1,0:T(8,128)(2,1)S(1)}, u32[]{:S(2)}, u32[]{:S(2)}) %collective-permute-start.2) | collective-permute-done | bytes 196640 | tf_op jit(solution)/shard_map/ppermute | solution.py:347
  11.1 2.0 %collective-permute-start.3 = (bf16[96,1024]{1,0:T(8,128)(2,1)S(1)}, bf16[96,1024]{1,0:T(8,128)(2,1)S(1)}, u32[]{:S(2)}, u32[]{:S(2)}) collective-permute-start(bf16[96,1024]{1,0:T(8,128)(2,1)S(1)} %shard_map.60.rest_5_), channel_id=1, source_target_pairs={{0,2},{1,3},{2,0},{3,1},{4,6},{5,7},{6,4},{7,5},{8,10},{9,11},{10,... | collective-permute-start | bytes 589832 | tf_op jit(solution)/shard_map/ppermute | solution.py:351
  13.1 0.0 collective-permute-done.1.rest_1_
  13.2 0.1 collective-permute-start.5
  13.3 0.5 %collective-permute-start.7 = (bf16[160,512]{1,0:T(8,128)(2,1)S(1)}, bf16[160,512]{1,0:T(8,128)(2,1)S(1)}, u32[]{:S(2)}, u32[]{:S(2)}) collective-permute-start(bf16[160,512]{1,0:T(8,128)(2,1)S(1)} %get-tuple-element.38), channel_id=1, source_target_pairs={{0,1},{1,0},{2,3},{3,2},{4,5},{5,4},{6,7},{7,6},{8,9},{9,8},{10,11... | collective-permute-start | bytes 491528 | tf_op jit(solution)/shard_map/ppermute | solution.py:347
  13.8 0.5 %shard_map.65 = (bf16[160,512]{1,0:T(8,128)(2,1)S(1)}, bf16[160,512]{1,0:T(8,128)(2,1)S(1)}) custom-call(bf16[160,1024]{1,0:T(8,128)(2,1)S(1)} %get-tuple-element.32.low_ref.att_ref, bf16[1024,4096]{1,0:T(8,128)(2,1)S(1)} %copy-done), custom_call_target="tpu_custom_call" | custom-call | flops 8589934592 | tf_op jit(solution)/shard_map/pallas_call | solution.py:34
  14.3 0.6 %collective-permute-done.7.rest_0_ = bf16[160,512]{1,0:T(8,128)(2,1)S(1)} collective-permute-done((bf16[160,512]{1,0:T(8,128)(2,1)S(1)}, bf16[160,512]{1,0:T(8,128)(2,1)S(1)}, u32[]{:S(2)}, u32[]{:S(2)}) %collective-permute-start.7) | collective-permute-done | bytes 163872 | tf_op jit(solution)/shard_map/ppermute | solution.py:347
  14.9 0.1 collective-permute-start.8
  15.0 0.0 collective-permute-done.5.rest_0_
  15.1 2.0 %collective-permute-start.6 = (bf16[160,512]{1,0:T(8,128)(2,1)S(1)}, bf16[160,512]{1,0:T(8,128)(2,1)S(1)}, u32[]{:S(2)}, u32[]{:S(2)}) collective-permute-start(bf16[160,512]{1,0:T(8,128)(2,1)S(1)} %shard_map.66), channel_id=1, source_target_pairs={{0,2},{1,3},{2,0},{3,1},{4,6},{5,7},{6,4},{7,5},{8,10},{9,11},{10,... | collective-permute-start | bytes 491528 | tf_op jit(solution)/shard_map/ppermute | solution.py:351
  17.1 1.6 %collective-permute-done.3.rest_0_ = bf16[96,1024]{1,0:T(8,128)(2,1)S(1)} collective-permute-done((bf16[96,1024]{1,0:T(8,128)(2,1)S(1)}, bf16[96,1024]{1,0:T(8,128)(2,1)S(1)}, u32[]{:S(2)}, u32[]{:S(2)}) %collective-permute-start.3) | collective-permute-done | bytes 196640 | tf_op jit(solution)/shard_map/ppermute | solution.py:351
  18.7 0.7 %shard_map.62 = (bf16[256,1024]{1,0:T(8,128)(2,1)S(1)}, bf16[256,1024]{1,0:T(8,128)(2,1)S(1)}) custom-call(bf16[160,1024]{1,0:T(8,128)(2,1)S(1)} %get-tuple-element.32.low_ref.att_ref, bf16[96,1024]{1,0:T(8,128)(2,1)S(1)} %get-tuple-element.30.att_ref.high_ref, bf16[1024,4096]{1,0:T(8,128)(2,1)S(1)} %copy-done, ...), custom_call_target="tpu_custom_call" | custom-call | flops 1073741824 | tf_op jit(solution)/shard_map/pallas_call | solution.py:34
  19.5 0.1 collective-permute-start.4
  19.5 0.7 %shard_map.63.keep_ref = bf16[256,1024]{1,0:T(8,128)(2,1)S(1)} custom-call(bf16[256,1024]{1,0:T(8,128)(2,1)S(1)} %get-tuple-element.33.att_ref, bf16[1024,4096]{1,0:T(8,128)(2,1)S(1)} %copy-done), custom_call_target="tpu_custom_call" | custom-call | flops 8589934592 | tf_op jit(solution)/shard_map/pallas_call | solution.py:34
  20.3 1.2 %collective-permute-done.4.rest_0_ = bf16[256,1024]{1,0:T(8,128)(2,1)S(1)} collective-permute-done((bf16[256,1024]{1,0:T(8,128)(2,1)S(1)}, bf16[256,1024]{1,0:T(8,128)(2,1)S(1)}, u32[]{:S(2)}, u32[]{:S(2)}) %collective-permute-start.4) | collective-permute-done | bytes 524320 | tf_op jit(solution)/shard_map/ppermute | solution.py:369
  21.4 0.1 shard_map.64.local_ref
  21.6 0.7 %shard_map.68.rest_2_ = bf16[256,1024]{1,0:T(8,128)(2,1)} custom-call(f32[256,1024]{1,0:T(8,128)S(1)} %shard_map.64.local_ref, bf16[96,1024]{1,0:T(8,128)(2,1)S(1)} %collective-permute-done.3.rest_0_), custom_call_target="tpu_custom_call" | custom-call | tf_op jit(solution)/shard_map/pallas_call | solution.py:372
  22.3 0.0 collective-permute-done.8.rest_1_
  22.3 3.1 %collective-permute-done.6.rest_0_ = bf16[160,512]{1,0:T(8,128)(2,1)S(1)} collective-permute-done((bf16[160,512]{1,0:T(8,128)(2,1)S(1)}, bf16[160,512]{1,0:T(8,128)(2,1)S(1)}, u32[]{:S(2)}, u32[]{:S(2)}) %collective-permute-start.6) | collective-permute-done | bytes 163872 | tf_op jit(solution)/shard_map/ppermute | solution.py:351
  25.4 0.8 %shard_map.69 = bf16[256,1024]{1,0:T(8,128)(2,1)} custom-call(f32[256,1024]{1,0:T(8,128)S(1)} %shard_map.64.local_ref, bf16[160,512]{1,0:T(8,128)(2,1)S(1)} %collective-permute-done.6.rest_0_, bf16[160,512]{1,0:T(8,128)(2,1)S(1)} %collective-permute-done.8.rest_1_, bf16[256,1024]{1,0:T(8,128)(2,1)} %shard_map.68.rest_2_), custom_call_target="tpu_custom_call", output_to_operand_aliasing={{}: (3, {})} | custom-call | tf_op jit(solution)/shard_map/pallas_call | solution.py:372
  (11 shorter events, 0.2 us)
Async XLA Ops:
  0.0 4.1 %copy-start.2 = (bf16[256,256]{1,0:T(8,128)(2,1)S(1)}, bf16[256,256]{1,0:T(8,128)(2,1)}, u32[]{:S(2)}) copy-start(bf16[256,256]{1,0:T(8,128)(2,1)} %k_ref.7) | copy-start | bytes 393220
  0.0 4.1 %copy-start.3 = (bf16[256,256]{1,0:T(8,128)(2,1)S(1)}, bf16[256,256]{1,0:T(8,128)(2,1)}, u32[]{:S(2)}) copy-start(bf16[256,256]{1,0:T(8,128)(2,1)} %v_ref.7) | copy-start | bytes 393220
  0.0 4.1 %copy-start.4 = (s32[256]{0:T(256)S(1)}, s32[256]{0:T(256)}, u32[]{:S(2)}) copy-start(s32[256]{0:T(256)} %param.8) | copy-start | bytes 3076
  0.0 7.6 %copy-start = (bf16[1024,4096]{1,0:T(8,128)(2,1)S(1)}, bf16[1024,4096]{1,0:T(8,128)(2,1)}, u32[]{:S(2)}) copy-start(bf16[1024,4096]{1,0:T(8,128)(2,1)} %w_ref.13) | copy-start | bytes 25165828
  0.0 7.7 %copy-start.1 = (bf16[256,1024]{1,0:T(8,128)(2,1)S(1)}, bf16[256,1024]{1,0:T(8,128)(2,1)}, u32[]{:S(2)}) copy-start(bf16[256,1024]{1,0:T(8,128)(2,1)} %q_ref.5) | copy-start | bytes 1572868
  1.1 8.4 %collective-permute-start = (bf16[208,256]{1,0:T(8,128)(2,1)S(1)}, bf16[208,256]{1,0:T(8,128)(2,1)S(1)}, u32[]{:S(2)}, u32[]{:S(2)}) collective-permute-start(bf16[208,256]{1,0:T(8,128)(2,1)S(1)} %shard_map.56), channel_id=1, source_target_pairs={{0,4},{4,8},{8,12},{12,16},{16,20},{20,24},{24,28},{28,0},{1,5},{5... | collective-permute-start | bytes 319496 | tf_op jit(solution)/shard_map/ppermute | solution.py:299
  4.2 8.9 %collective-permute-start.1 = (bf16[320,256]{1,0:T(8,128)(2,1)S(1)}, bf16[320,256]{1,0:T(8,128)(2,1)S(1)}, u32[]{:S(2)}, u32[]{:S(2)}) collective-permute-start(bf16[320,256]{1,0:T(8,128)(2,1)S(1)} %get-tuple-element.24), channel_id=1, source_target_pairs={{0,4},{4,8},{8,12},{12,16},{16,20},{20,24},{24,28},{1,5},{5,9},{9,... | collective-permute-start | bytes 491528 | tf_op jit(solution)/shard_map/ppermute | solution.py:300
  9.5 1.5 %collective-permute-start.2 = (bf16[96,1024]{1,0:T(8,128)(2,1)S(1)}, bf16[96,1024]{1,0:T(8,128)(2,1)S(1)}, u32[]{:S(2)}, u32[]{:S(2)}) collective-permute-start(bf16[96,1024]{1,0:T(8,128)(2,1)S(1)} %get-tuple-element.31), channel_id=1, source_target_pairs={{0,1},{1,0},{2,3},{3,2},{4,5},{5,4},{6,7},{7,6},{8,9},{9,8},{10,11... | collective-permute-start | bytes 589832 | tf_op jit(solution)/shard_map/ppermute | solution.py:347
  11.1 7.7 %collective-permute-start.3 = (bf16[96,1024]{1,0:T(8,128)(2,1)S(1)}, bf16[96,1024]{1,0:T(8,128)(2,1)S(1)}, u32[]{:S(2)}, u32[]{:S(2)}) collective-permute-start(bf16[96,1024]{1,0:T(8,128)(2,1)S(1)} %shard_map.60.rest_5_), channel_id=1, source_target_pairs={{0,2},{1,3},{2,0},{3,1},{4,6},{5,7},{6,4},{7,5},{8,10},{9,11},{10,... | collective-permute-start | bytes 589832 | tf_op jit(solution)/shard_map/ppermute | solution.py:351
  13.2 1.9 %collective-permute-start.5 = (bf16[160,512]{1,0:T(8,128)(2,1)S(1)}, bf16[160,512]{1,0:T(8,128)(2,1)S(1)}, u32[]{:S(2)}, u32[]{:S(2)}) collective-permute-start(bf16[160,512]{1,0:T(8,128)(2,1)S(1)} %get-tuple-element.36), channel_id=1, source_target_pairs={{0,1},{1,0},{2,3},{3,2},{4,5},{5,4},{6,7},{7,6},{8,9},{9,8},{10,11... | collective-permute-start | bytes 491528 | tf_op jit(solution)/shard_map/ppermute | solution.py:347
  13.3 1.6 %collective-permute-start.7 = (bf16[160,512]{1,0:T(8,128)(2,1)S(1)}, bf16[160,512]{1,0:T(8,128)(2,1)S(1)}, u32[]{:S(2)}, u32[]{:S(2)}) collective-permute-start(bf16[160,512]{1,0:T(8,128)(2,1)S(1)} %get-tuple-element.38), channel_id=1, source_target_pairs={{0,1},{1,0},{2,3},{3,2},{4,5},{5,4},{6,7},{7,6},{8,9},{9,8},{10,11... | collective-permute-start | bytes 491528 | tf_op jit(solution)/shard_map/ppermute | solution.py:347
  14.9 7.4 %collective-permute-start.8 = (bf16[160,512]{1,0:T(8,128)(2,1)S(1)}, bf16[160,512]{1,0:T(8,128)(2,1)S(1)}, u32[]{:S(2)}, u32[]{:S(2)}) collective-permute-start(bf16[160,512]{1,0:T(8,128)(2,1)S(1)} %shard_map.67), channel_id=1, source_target_pairs={{0,2},{1,3},{2,0},{3,1},{4,6},{5,7},{6,4},{7,5},{8,10},{9,11},{10,... | collective-permute-start | bytes 491528 | tf_op jit(solution)/shard_map/ppermute | solution.py:351
  15.1 10.3 %collective-permute-start.6 = (bf16[160,512]{1,0:T(8,128)(2,1)S(1)}, bf16[160,512]{1,0:T(8,128)(2,1)S(1)}, u32[]{:S(2)}, u32[]{:S(2)}) collective-permute-start(bf16[160,512]{1,0:T(8,128)(2,1)S(1)} %shard_map.66), channel_id=1, source_target_pairs={{0,2},{1,3},{2,0},{3,1},{4,6},{5,7},{6,4},{7,5},{8,10},{9,11},{10,... | collective-permute-start | bytes 491528 | tf_op jit(solution)/shard_map/ppermute | solution.py:351
  19.5 2.0 %collective-permute-start.4 = (bf16[256,1024]{1,0:T(8,128)(2,1)S(1)}, bf16[256,1024]{1,0:T(8,128)(2,1)S(1)}, u32[]{:S(2)}, u32[]{:S(2)}) collective-permute-start(bf16[256,1024]{1,0:T(8,128)(2,1)S(1)} %get-tuple-element.34), channel_id=1, source_target_pairs={{0,1},{1,0},{2,3},{3,2},{4,5},{5,4},{6,7},{7,6},{8,9},{9,8},{10,11... | collective-permute-start | bytes 1572872 | tf_op jit(solution)/shard_map/ppermute | solution.py:369

commit v8 on v7

--- a/solution.py
+++ b/solution.py
@@ -235,9 +235,9 @@
         ).astype(jnp.bfloat16)
 
 
-def sum_kernel(keep_ref, *rest):
+def sum_kernel(count, keep_ref, *rest):
     out_ref, at = rest[-1], 0
-    for got in rest[:-1]:
+    for got in rest[:count]:
         lanes = slice(at, at + got.shape[1])
         total = keep_ref[:, lanes].astype(jnp.float32) + got[...].astype(jnp.float32)
         out_ref[:, lanes] = total.astype(out_ref.dtype)
@@ -311,12 +311,12 @@
             flops=flops,
         )
 
-    def add(keep, dtype, *got):
+    def add(keep, dtype, *got, after=()):
         return call(
-            sum_kernel,
+            functools.partial(sum_kernel, len(got)),
             pltpu.VMEM(keep.shape, dtype),
-            [VMEM] * (1 + len(got)),
-            tuple(map(near, (keep, *got))),
+            [VMEM] * (1 + len(got)) + [ANY] * len(after),
+            (*map(near, (keep, *got)), *after),
         )
 
     def outputs(rows, pieces):
@@ -344,7 +344,7 @@
         keeps = keep_shares(att, 1, chips - 1, pieces, keep_flops)
         sums, arrived = [], []
         for i, (keep, give) in enumerate(zip(keeps, gives)):
-            total = add(keep, bf16, lax.ppermute(give, "head", other_core))
+            total = add(keep, bf16, lax.ppermute(give, "head", other_core), after=sums[-1:])
             step = (i // pieces + 1) * CORES
             sums.append(total)
             arrived.append(

time: 26.3 us -> 26.3 us (level)
  transfers between devices with their start and end apart: 9 -> 9, of which waited for: 5 -> 6; matrix products, arithmetic and copies ran while one was open for 0% -> 0% of each run, Pallas kernels for 21% -> 21%
where the time goes in v8:
time: 26.3 us; the launch traced here: 26.1 us
  starting transfers between devices  11.3 us (43%)
  waiting for transfers between devices  7.46 us (28%)
  Pallas kernels  7.21 us (27%)
    pallas_call x13, Pallas kernels, call(): pl.pallas_call(kernel, out_shape=out_shape, in_specs=in_specs, out_specs=...  5.69 us
    ppermute x3, waiting for transfers between devices, shares(): lax.ppermute(total, 'head', [(j, (j + step) % devices) for j in range(dev...  4.92 us
    ppermute x3, starting transfers between devices, shares(): lax.ppermute(total, 'head', [(j, (j + step) % devices) for j in range(dev...  4.13 us
    ppermute x1, starting transfers between devices, body(): lows.append(lax.ppermute(packed_low, 'ctx', ring[:place_count - s]))  3.43 us
    ppermute x1, starting transfers between devices, body(): highs.append(lax.ppermute(packed_high, 'ctx', ring))  3.03 us
    pallas_call x2, Pallas kernels, finish(): pl.pallas_call(functools.partial(final_kernel, first, pieces, len(arrived...  1.51 us
    ppermute x3, waiting for transfers between devices, shares(): lax.ppermute(give, 'head', other_core)  1.37 us
    ppermute x1, waiting for transfers between devices, body(): lax.ppermute(give, 'head', other_core)  1.16 us
  transfers between devices with their start and end apart: 9, of which 6 were waited for; matrix products, arithmetic and copies ran while one was open for 0% of the time, Pallas kernels for 21%

profile of v8, /device:TPU:0, one launch (start us, length us, event | category | flops | bytes accessed | tf_op | source)
XLA Modules:
  0.0 26.1 jit_solution(5049033776073560178)
XLA Ops:
  0.0 1.0 %shard_map.56 = bf16[208,256]{1,0:T(8,128)(2,1)S(1)} custom-call(bf16[256,256]{1,0:T(8,128)(2,1)} %k_ref.7, bf16[256,256]{1,0:T(8,128)(2,1)} %v_ref.7, s32[1,256]{1,0:T(1,128)} %bitcast.1), custom_call_target="tpu_custom_call" | custom-call | flops 8589934592 | tf_op jit(solution)/shard_map/pallas_call | solution.py:34
  1.1 3.0 %collective-permute-start = (bf16[208,256]{1,0:T(8,128)(2,1)S(1)}, bf16[208,256]{1,0:T(8,128)(2,1)S(1)}, u32[]{:S(2)}, u32[]{:S(2)}) collective-permute-start(bf16[208,256]{1,0:T(8,128)(2,1)S(1)} %shard_map.56), channel_id=1, source_target_pairs={{0,4},{4,8},{8,12},{12,16},{16,20},{20,24},{24,28},{28,0},{1,5},{5... | collective-permute-start | bytes 319496 | tf_op jit(solution)/shard_map/ppermute | solution.py:299
  4.1 0.0 copy-done.2
  4.1 0.0 copy-done.3
  4.1 0.1 shard_map.55
  4.2 3.4 %collective-permute-start.1 = (bf16[320,256]{1,0:T(8,128)(2,1)S(1)}, bf16[320,256]{1,0:T(8,128)(2,1)S(1)}, u32[]{:S(2)}, u32[]{:S(2)}) collective-permute-start(bf16[320,256]{1,0:T(8,128)(2,1)S(1)} %get-tuple-element.24), channel_id=1, source_target_pairs={{0,4},{4,8},{8,12},{12,16},{16,20},{20,24},{24,28},{1,5},{5,9},{9,... | collective-permute-start | bytes 491528 | tf_op jit(solution)/shard_map/ppermute | solution.py:300
  7.6 0.0 copy-done
  7.7 0.0 copy-done.1
  7.7 1.8 %shard_map.57 = (bf16[96,1024]{1,0:T(8,128)(2,1)S(1)}, bf16[96,1024]{1,0:T(8,128)(2,1)S(1)}, bf16[160,1024]{1,0:T(8,128)(2,1)S(1)}, bf16[160,512]{1,0:T(8,128)(2,1)S(1)}, bf16[160,512]{1,0:T(8,128)(2,1)S(1)}) custom-call(bf16[256,1024]{1,0:T(8,128)(2,1)S(1)} %copy-done.1, bf16[256,256]{1,0:T(8,128)(2,1)S(1)} %copy-done.2, bf16[256,256]{1,0:T(8,128)(2,1)S(1)} %copy-done.3, ...), custom_call_target="tpu_custom_call" | custom-call | flops 134217728 | tf_op jit(solution)/shard_map/pallas_call | solution.py:34
  9.5 0.0 collective-permute-done.rest_0_
  9.5 0.1 collective-permute-start.2
  9.6 0.5 %shard_map.59.keep_ref = bf16[96,1024]{1,0:T(8,128)(2,1)S(1)} custom-call(bf16[96,1024]{1,0:T(8,128)(2,1)S(1)} %get-tuple-element.30.att_ref.high_ref, bf16[1024,4096]{1,0:T(8,128)(2,1)S(1)} %copy-done), custom_call_target="tpu_custom_call" | custom-call | flops 8589934592 | tf_op jit(solution)/shard_map/pallas_call | solution.py:34
  10.1 0.9 %collective-permute-done.2.rest_0_ = bf16[96,1024]{1,0:T(8,128)(2,1)S(1)} collective-permute-done((bf16[96,1024]{1,0:T(8,128)(2,1)S(1)}, bf16[96,1024]{1,0:T(8,128)(2,1)S(1)}, u32[]{:S(2)}, u32[]{:S(2)}) %collective-permute-start.2) | collective-permute-done | bytes 196640 | tf_op jit(solution)/shard_map/ppermute | solution.py:347
  11.1 2.0 %collective-permute-start.3 = (bf16[96,1024]{1,0:T(8,128)(2,1)S(1)}, bf16[96,1024]{1,0:T(8,128)(2,1)S(1)}, u32[]{:S(2)}, u32[]{:S(2)}) collective-permute-start(bf16[96,1024]{1,0:T(8,128)(2,1)S(1)} %shard_map.60.rest_5_), channel_id=1, source_target_pairs={{0,2},{1,3},{2,0},{3,1},{4,6},{5,7},{6,4},{7,5},{8,10},{9,11},{10,... | collective-permute-start | bytes 589832 | tf_op jit(solution)/shard_map/ppermute | solution.py:351
  13.1 0.0 collective-permute-done.1.rest_1_
  13.2 0.1 collective-permute-start.5
  13.3 0.5 %collective-permute-start.7 = (bf16[160,512]{1,0:T(8,128)(2,1)S(1)}, bf16[160,512]{1,0:T(8,128)(2,1)S(1)}, u32[]{:S(2)}, u32[]{:S(2)}) collective-permute-start(bf16[160,512]{1,0:T(8,128)(2,1)S(1)} %get-tuple-element.38), channel_id=1, source_target_pairs={{0,1},{1,0},{2,3},{3,2},{4,5},{5,4},{6,7},{7,6},{8,9},{9,8},{10,11... | collective-permute-start | bytes 491528 | tf_op jit(solution)/shard_map/ppermute | solution.py:347
  13.8 0.5 %shard_map.65 = (bf16[160,512]{1,0:T(8,128)(2,1)S(1)}, bf16[160,512]{1,0:T(8,128)(2,1)S(1)}) custom-call(bf16[160,1024]{1,0:T(8,128)(2,1)S(1)} %get-tuple-element.32.low_ref.att_ref, bf16[1024,4096]{1,0:T(8,128)(2,1)S(1)} %copy-done), custom_call_target="tpu_custom_call" | custom-call | flops 8589934592 | tf_op jit(solution)/shard_map/pallas_call | solution.py:34
  14.3 0.4 %collective-permute-done.5.rest_0_ = bf16[160,512]{1,0:T(8,128)(2,1)S(1)} collective-permute-done((bf16[160,512]{1,0:T(8,128)(2,1)S(1)}, bf16[160,512]{1,0:T(8,128)(2,1)S(1)}, u32[]{:S(2)}, u32[]{:S(2)}) %collective-permute-start.5) | collective-permute-done | bytes 163872 | tf_op jit(solution)/shard_map/ppermute | solution.py:347
  14.7 0.1 collective-permute-start.6
  14.8 0.1 collective-permute-done.7.rest_0_
  14.9 2.0 %collective-permute-start.8 = (bf16[160,512]{1,0:T(8,128)(2,1)S(1)}, bf16[160,512]{1,0:T(8,128)(2,1)S(1)}, u32[]{:S(2)}, u32[]{:S(2)}) collective-permute-start(bf16[160,512]{1,0:T(8,128)(2,1)S(1)} %shard_map.67), channel_id=1, source_target_pairs={{0,2},{1,3},{2,0},{3,1},{4,6},{5,7},{6,4},{7,5},{8,10},{9,11},{10,... | collective-permute-start | bytes 491528 | tf_op jit(solution)/shard_map/ppermute | solution.py:351
  16.9 2.0 %collective-permute-done.3.rest_0_ = bf16[96,1024]{1,0:T(8,128)(2,1)S(1)} collective-permute-done((bf16[96,1024]{1,0:T(8,128)(2,1)S(1)}, bf16[96,1024]{1,0:T(8,128)(2,1)S(1)}, u32[]{:S(2)}, u32[]{:S(2)}) %collective-permute-start.3) | collective-permute-done | bytes 196640 | tf_op jit(solution)/shard_map/ppermute | solution.py:351
  18.9 0.7 %shard_map.62 = (bf16[256,1024]{1,0:T(8,128)(2,1)S(1)}, bf16[256,1024]{1,0:T(8,128)(2,1)S(1)}) custom-call(bf16[160,1024]{1,0:T(8,128)(2,1)S(1)} %get-tuple-element.32.low_ref.att_ref, bf16[96,1024]{1,0:T(8,128)(2,1)S(1)} %get-tuple-element.30.att_ref.high_ref, bf16[1024,4096]{1,0:T(8,128)(2,1)S(1)} %copy-done, ...), custom_call_target="tpu_custom_call" | custom-call | flops 1073741824 | tf_op jit(solution)/shard_map/pallas_call | solution.py:34
  19.6 0.1 collective-permute-start.4
  19.7 0.7 %shard_map.63.keep_ref = bf16[256,1024]{1,0:T(8,128)(2,1)S(1)} custom-call(bf16[256,1024]{1,0:T(8,128)(2,1)S(1)} %get-tuple-element.33.att_ref, bf16[1024,4096]{1,0:T(8,128)(2,1)S(1)} %copy-done), custom_call_target="tpu_custom_call" | custom-call | flops 8589934592 | tf_op jit(solution)/shard_map/pallas_call | solution.py:34
  20.4 1.2 %collective-permute-done.4.rest_0_ = bf16[256,1024]{1,0:T(8,128)(2,1)S(1)} collective-permute-done((bf16[256,1024]{1,0:T(8,128)(2,1)S(1)}, bf16[256,1024]{1,0:T(8,128)(2,1)S(1)}, u32[]{:S(2)}, u32[]{:S(2)}) %collective-permute-start.4) | collective-permute-done | bytes 524320 | tf_op jit(solution)/shard_map/ppermute | solution.py:369
  21.6 0.1 shard_map.64.local_ref
  21.7 0.7 %shard_map.68.rest_2_ = bf16[256,1024]{1,0:T(8,128)(2,1)} custom-call(f32[256,1024]{1,0:T(8,128)S(1)} %shard_map.64.local_ref, bf16[96,1024]{1,0:T(8,128)(2,1)S(1)} %collective-permute-done.3.rest_0_), custom_call_target="tpu_custom_call" | custom-call | tf_op jit(solution)/shard_map/pallas_call | solution.py:372
  22.4 2.9 %collective-permute-done.8.rest_1_ = bf16[160,512]{1,0:T(8,128)(2,1)S(1)} collective-permute-done((bf16[160,512]{1,0:T(8,128)(2,1)S(1)}, bf16[160,512]{1,0:T(8,128)(2,1)S(1)}, u32[]{:S(2)}, u32[]{:S(2)}) %collective-permute-start.8) | collective-permute-done | bytes 163872 | tf_op jit(solution)/shard_map/ppermute | solution.py:351
  25.4 0.0 collective-permute-done.6.rest_0_
  25.4 0.8 %shard_map.69 = bf16[256,1024]{1,0:T(8,128)(2,1)} custom-call(f32[256,1024]{1,0:T(8,128)S(1)} %shard_map.64.local_ref, bf16[160,512]{1,0:T(8,128)(2,1)S(1)} %collective-permute-done.6.rest_0_, bf16[160,512]{1,0:T(8,128)(2,1)S(1)} %collective-permute-done.8.rest_1_, bf16[256,1024]{1,0:T(8,128)(2,1)} %shard_map.68.rest_2_), custom_call_target="tpu_custom_call", output_to_operand_aliasing={{}: (3, {})} | custom-call | tf_op jit(solution)/shard_map/pallas_call | solution.py:372
  (11 shorter events, 0.2 us)
Async XLA Ops:
  0.0 4.1 %copy-start.2 = (bf16[256,256]{1,0:T(8,128)(2,1)S(1)}, bf16[256,256]{1,0:T(8,128)(2,1)}, u32[]{:S(2)}) copy-start(bf16[256,256]{1,0:T(8,128)(2,1)} %k_ref.7) | copy-start | bytes 393220
  0.0 4.1 %copy-start.3 = (bf16[256,256]{1,0:T(8,128)(2,1)S(1)}, bf16[256,256]{1,0:T(8,128)(2,1)}, u32[]{:S(2)}) copy-start(bf16[256,256]{1,0:T(8,128)(2,1)} %v_ref.7) | copy-start | bytes 393220
  0.0 4.1 %copy-start.4 = (s32[256]{0:T(256)S(1)}, s32[256]{0:T(256)}, u32[]{:S(2)}) copy-start(s32[256]{0:T(256)} %param.8) | copy-start | bytes 3076
  0.0 7.6 %copy-start = (bf16[1024,4096]{1,0:T(8,128)(2,1)S(1)}, bf16[1024,4096]{1,0:T(8,128)(2,1)}, u32[]{:S(2)}) copy-start(bf16[1024,4096]{1,0:T(8,128)(2,1)} %w_ref.13) | copy-start | bytes 25165828
  0.0 7.7 %copy-start.1 = (bf16[256,1024]{1,0:T(8,128)(2,1)S(1)}, bf16[256,1024]{1,0:T(8,128)(2,1)}, u32[]{:S(2)}) copy-start(bf16[256,1024]{1,0:T(8,128)(2,1)} %q_ref.5) | copy-start | bytes 1572868
  1.1 8.4 %collective-permute-start = (bf16[208,256]{1,0:T(8,128)(2,1)S(1)}, bf16[208,256]{1,0:T(8,128)(2,1)S(1)}, u32[]{:S(2)}, u32[]{:S(2)}) collective-permute-start(bf16[208,256]{1,0:T(8,128)(2,1)S(1)} %shard_map.56), channel_id=1, source_target_pairs={{0,4},{4,8},{8,12},{12,16},{16,20},{20,24},{24,28},{28,0},{1,5},{5... | collective-permute-start | bytes 319496 | tf_op jit(solution)/shard_map/ppermute | solution.py:299
  4.2 8.9 %collective-permute-start.1 = (bf16[320,256]{1,0:T(8,128)(2,1)S(1)}, bf16[320,256]{1,0:T(8,128)(2,1)S(1)}, u32[]{:S(2)}, u32[]{:S(2)}) collective-permute-start(bf16[320,256]{1,0:T(8,128)(2,1)S(1)} %get-tuple-element.24), channel_id=1, source_target_pairs={{0,4},{4,8},{8,12},{12,16},{16,20},{20,24},{24,28},{1,5},{5,9},{9,... | collective-permute-start | bytes 491528 | tf_op jit(solution)/shard_map/ppermute | solution.py:300
  9.5 1.5 %collective-permute-start.2 = (bf16[96,1024]{1,0:T(8,128)(2,1)S(1)}, bf16[96,1024]{1,0:T(8,128)(2,1)S(1)}, u32[]{:S(2)}, u32[]{:S(2)}) collective-permute-start(bf16[96,1024]{1,0:T(8,128)(2,1)S(1)} %get-tuple-element.31), channel_id=1, source_target_pairs={{0,1},{1,0},{2,3},{3,2},{4,5},{5,4},{6,7},{7,6},{8,9},{9,8},{10,11... | collective-permute-start | bytes 589832 | tf_op jit(solution)/shard_map/ppermute | solution.py:347
  11.1 7.8 %collective-permute-start.3 = (bf16[96,1024]{1,0:T(8,128)(2,1)S(1)}, bf16[96,1024]{1,0:T(8,128)(2,1)S(1)}, u32[]{:S(2)}, u32[]{:S(2)}) collective-permute-start(bf16[96,1024]{1,0:T(8,128)(2,1)S(1)} %shard_map.60.rest_5_), channel_id=1, source_target_pairs={{0,2},{1,3},{2,0},{3,1},{4,6},{5,7},{6,4},{7,5},{8,10},{9,11},{10,... | collective-permute-start | bytes 589832 | tf_op jit(solution)/shard_map/ppermute | solution.py:351
  13.2 1.5 %collective-permute-start.5 = (bf16[160,512]{1,0:T(8,128)(2,1)S(1)}, bf16[160,512]{1,0:T(8,128)(2,1)S(1)}, u32[]{:S(2)}, u32[]{:S(2)}) collective-permute-start(bf16[160,512]{1,0:T(8,128)(2,1)S(1)} %get-tuple-element.36), channel_id=1, source_target_pairs={{0,1},{1,0},{2,3},{3,2},{4,5},{5,4},{6,7},{7,6},{8,9},{9,8},{10,11... | collective-permute-start | bytes 491528 | tf_op jit(solution)/shard_map/ppermute | solution.py:347
  13.3 1.6 %collective-permute-start.7 = (bf16[160,512]{1,0:T(8,128)(2,1)S(1)}, bf16[160,512]{1,0:T(8,128)(2,1)S(1)}, u32[]{:S(2)}, u32[]{:S(2)}) collective-permute-start(bf16[160,512]{1,0:T(8,128)(2,1)S(1)} %get-tuple-element.38), channel_id=1, source_target_pairs={{0,1},{1,0},{2,3},{3,2},{4,5},{5,4},{6,7},{7,6},{8,9},{9,8},{10,11... | collective-permute-start | bytes 491528 | tf_op jit(solution)/shard_map/ppermute | solution.py:347
  14.7 10.7 %collective-permute-start.6 = (bf16[160,512]{1,0:T(8,128)(2,1)S(1)}, bf16[160,512]{1,0:T(8,128)(2,1)S(1)}, u32[]{:S(2)}, u32[]{:S(2)}) collective-permute-start(bf16[160,512]{1,0:T(8,128)(2,1)S(1)} %shard_map.66.rest_1_), channel_id=1, source_target_pairs={{0,2},{1,3},{2,0},{3,1},{4,6},{5,7},{6,4},{7,5},{8,10},{9,11},{10,... | collective-permute-start | bytes 491528 | tf_op jit(solution)/shard_map/ppermute | solution.py:351
  14.9 10.4 %collective-permute-start.8 = (bf16[160,512]{1,0:T(8,128)(2,1)S(1)}, bf16[160,512]{1,0:T(8,128)(2,1)S(1)}, u32[]{:S(2)}, u32[]{:S(2)}) collective-permute-start(bf16[160,512]{1,0:T(8,128)(2,1)S(1)} %shard_map.67), channel_id=1, source_target_pairs={{0,2},{1,3},{2,0},{3,1},{4,6},{5,7},{6,4},{7,5},{8,10},{9,11},{10,... | collective-permute-start | bytes 491528 | tf_op jit(solution)/shard_map/ppermute | solution.py:351
  19.6 2.0 %collective-permute-start.4 = (bf16[256,1024]{1,0:T(8,128)(2,1)S(1)}, bf16[256,1024]{1,0:T(8,128)(2,1)S(1)}, u32[]{:S(2)}, u32[]{:S(2)}) collective-permute-start(bf16[256,1024]{1,0:T(8,128)(2,1)S(1)} %get-tuple-element.34), channel_id=1, source_target_pairs={{0,1},{1,0},{2,3},{3,2},{4,5},{5,4},{6,7},{7,6},{8,9},{9,8},{10,11... | collective-permute-start | bytes 1572872 | tf_op jit(solution)/shard_map/ppermute | solution.py:369

commit v9 on v6

--- a/solution.py
+++ b/solution.py
@@ -12,7 +12,7 @@
 CORES = 2
 CUT = 160 / 256
 DOC_ROWS = 16
-PIECES = 2
+PIECES = 1
 LOG2_SCALE = math.log2(math.e) / math.sqrt(HEAD_DIM)
 HIDDEN = -1e30
 NT = (((1,), (1,)), ((), ()))
@@ -159,6 +159,83 @@
     column_ref[...] = columns
 
 
+def own_kernel(q_ref, k_ref, v_ref, bias_ref, acc_ref, total_ref, top_ref):
+    groups = k_ref.shape[1] // HEAD_DIM
+    repeats = q_ref.shape[1] // HEAD_DIM // groups
+    rows = acc_ref.shape[1] // repeats
+
+    @pl.when(lax.axis_index("ctx") > 0)
+    def _():
+        lanes = [slice(g * HEAD_DIM, (g + 1) * HEAD_DIM) for g in range(groups)]
+        scores = [
+            lax.dot_general(
+                stacked(q_ref, 0, rows, g * repeats, repeats),
+                k_ref[:rows, lanes[g]],
+                NT,
+                preferred_element_type=jnp.float32,
+            )
+            for g in range(groups)
+        ]
+        scores = [hide(s, bias_ref[:rows, :rows]) for s in scores]
+        tops = [jnp.max(s, axis=1, keepdims=True) for s in scores]
+        weights = [weights_of(s, top) for s, top in zip(scores, tops)]
+        for g in range(groups):
+            summed = jnp.dot(
+                weights[g], with_ones(v_ref[:rows, lanes[g]]), preferred_element_type=jnp.float32
+            )
+            acc_ref[g] = summed[:, :HEAD_DIM]
+            total_ref[g] = summed[:, HEAD_DIM:]
+            top_ref[g] = jnp.broadcast_to(tops[g], acc_ref.shape[1:])
+
+
+def attend_before(q_ref, column_ref, state, highs, lows, att_ref):
+    acc_ref, total_ref, top_ref = state
+    tokens, width = q_ref.shape
+    rows = att_ref.shape[0]
+    groups = acc_ref.shape[0]
+    repeats = width // HEAD_DIM // groups
+    column = column_ref[:rows, :]
+    biases, keys, values = [], [], []
+    for s, (high, low) in enumerate(zip(highs, lows), 1):
+        keys += [low[:rows, :], high[: tokens - rows, :]]
+        values += [low[rows:, :], high[tokens - rows : 2 * (tokens - rows), :]]
+        there = (lax.axis_index("ctx") >= s).astype(jnp.float32)
+        same = key_docs(high, tokens) * there == column
+        biases.append(jnp.where(same, 0.0, HIDDEN))
+    bias = jnp.concatenate(biases, axis=1)
+    all_keys = jnp.concatenate(keys, axis=0)
+    all_values = jnp.concatenate(values, axis=0)
+    spread = bias.shape[1] // HEAD_DIM
+    lanes = [slice(g * HEAD_DIM, (g + 1) * HEAD_DIM) for g in range(groups)]
+    scores = [
+        lax.dot_general(
+            stacked(q_ref, 0, rows, g * repeats, repeats),
+            all_keys[:, lanes[g]],
+            NT,
+            preferred_element_type=jnp.float32,
+        )
+        for g in range(groups)
+    ]
+    scores = [hide(x, bias) for x in scores]
+    tops = [
+        jnp.maximum(top_ref[g], jnp.max(scores[g], axis=1, keepdims=True)) for g in range(groups)
+    ]
+    weights = [
+        weights_of(x, jnp.concatenate([top] * spread, axis=1)) for x, top in zip(scores, tops)
+    ]
+    for g in range(groups):
+        factor = jnp.exp2((top_ref[g] - tops[g]) * LOG2_SCALE)
+        summed = jnp.dot(
+            weights[g], with_ones(all_values[:, lanes[g]]), preferred_element_type=jnp.float32
+        )
+        acc = acc_ref[g] * factor + summed[:, :HEAD_DIM]
+        total = total_ref[g] * factor + summed[:, HEAD_DIM:]
+        result = (acc / total).astype(jnp.bfloat16)
+        for r in range(repeats):
+            h = g * repeats + r
+            att_ref[:, h * HEAD_DIM : (h + 1) * HEAD_DIM] = result[r * rows : (r + 1) * rows]
+
+
 def owner(d, which):
     chips = lax.axis_size("head") // CORES
     me = lax.axis_index("head")
@@ -211,6 +288,28 @@
     @pl.when(here > 0)
     def _():
         give_shares(first, chips, refs, highs, lows, w_ref, outs[0], outs[1:])
+
+
+def low_kernel(
+    chips, n_outs, n_prev, q_ref, column_ref, acc_ref, total_ref, top_ref, w_ref, *rest
+):
+    outs = rest[-n_outs:]
+    highs, lows = rest[:n_prev], rest[n_prev : 2 * n_prev]
+    done = rest[2 * n_prev : 2 * n_prev + n_outs]
+    here = lax.axis_index("ctx")
+
+    @pl.when(here == 0)
+    def _():
+        for ref, out in zip(done, outs):
+            out[...] = ref[...]
+
+    @pl.when(here > 0)
+    def _():
+        att_ref, gives = outs[0], outs[1:]
+        attend_before(q_ref, column_ref, (acc_ref, total_ref, top_ref), highs, lows, att_ref)
+        att = att_ref[...]
+        for d in range(1, chips):
+            project(att, w_ref, d, 1, gives[d - 1 : d])
 
 
 def keep_kernel(first, chips, att_ref, w_ref, *outs):
@@ -331,16 +430,15 @@
         flops=2**27,
     )
 
-    def shares(first, rows, pieces, keep_flops, lows, done, *after):
-        prevs = highs + lows + done
+    def shares(rows, pieces, kernel, args, after):
         att, *gives = call(
-            functools.partial(give_kernel, first, chips, len(done), len(highs), len(lows)),
+            kernel,
             outputs(rows, pieces),
-            [VMEM] * (len(always) + len(prevs)) + [ANY] * len(after),
-            (*always, *map(near, prevs), *after),
+            [VMEM] * len(args) + [ANY] * len(after),
+            (*args, *after),
             flops=8 * tokens * width * block,
         )
-        keeps = keep_shares(att, 1, chips - 1, pieces, keep_flops)
+        keeps = keep_shares(att, 1, chips - 1, pieces, 2**33)
         sums, arrived = [], []
         for i, (keep, give) in enumerate(zip(keeps, gives)):
             total = add(keep, bf16, lax.ppermute(give, "head", other_core))
@@ -353,9 +451,30 @@
 
     n_done = 1 + (chips - 1) * PIECES
     att_high, sums, high = shares(
-        cut, tokens - cut, PIECES, 2**33, lows[:-1], list(done[:n_done])
-    )
-    att_low, sums, low = shares(0, cut, 1, 2**33, lows, list(done[n_done:]), *sums)
+        tokens - cut,
+        PIECES,
+        functools.partial(give_kernel, cut, chips, n_done, len(highs), len(lows) - 1),
+        (*always, *map(near, highs + lows[:-1] + list(done[:n_done]))),
+        [],
+    )
+    state = pltpu.VMEM((groups, cut * (width // kv_width), HEAD_DIM), f32)
+    states = call(
+        own_kernel,
+        [state] * 3,
+        [VMEM] * 4,
+        (queries, keys, values, near(bias)),
+        flops=2**20,
+    )
+    att_low, sums, low = shares(
+        cut,
+        1,
+        functools.partial(low_kernel, chips, chips, len(highs)),
+        (
+            *(queries, near(column), *map(near, states), out_weight),
+            *map(near, highs + lows + list(done[n_done:])),
+        ),
+        sums,
+    )
 
     att, *gives = call(
         local_kernel,

time: 26.5 us -> 26.3 us (level)
  starting transfers between devices: 11.9 us -> 9.33 us
  waiting for transfers between devices: 7.09 us -> 9.41 us
    ppermute x3 -> x2, starting transfers between devices: 4.2 us -> 2.16 us  [shares(): lax.ppermute(total, 'head', [(j, (j + step) % devices) for j in range(dev...]
    ppermute x3 -> x2, waiting for transfers between devices: 4.87 us -> 6.71 us  [shares(): lax.ppermute(total, 'head', [(j, (j + step) % devices) for j in range(dev...]
    ppermute x3 -> x2, starting transfers between devices: 0.67 us -> 0.14 us  [shares(): total = add(keep, bf16, lax.ppermute(give, 'head', other_core))]
    ppermute x3 -> x2, waiting for transfers between devices: 1.54 us -> 2.01 us  [shares(): total = add(keep, bf16, lax.ppermute(give, 'head', other_core))]
  transfers between devices with their start and end apart: 10 -> 8, of which waited for: 6 -> 6; matrix products, arithmetic and copies ran while one was open for 0% -> 0% of each run, Pallas kernels for 20% -> 21%
where the time goes in v9:
time: 26.3 us; the launch traced here: 26.1 us
  waiting for transfers between devices  9.41 us (36%)
  starting transfers between devices  9.33 us (35%)
  Pallas kernels  7.21 us (27%)
    ppermute x2, waiting for transfers between devices, shares(): lax.ppermute(total, 'head', [(j, (j + step) % devices) for j in range(dev...  6.71 us
    pallas_call x13, Pallas kernels, call(): pl.pallas_call(kernel, out_shape=out_shape, in_specs=in_specs, out_specs=...  5.7 us
    ppermute x1, starting transfers between devices, body(): lows.append(lax.ppermute(packed_low, 'ctx', ring[:place_count - s]))  3.43 us
    ppermute x1, starting transfers between devices, body(): highs.append(lax.ppermute(packed_high, 'ctx', ring))  3.03 us
    ppermute x2, starting transfers between devices, shares(): lax.ppermute(total, 'head', [(j, (j + step) % devices) for j in range(dev...  2.16 us
    ppermute x2, waiting for transfers between devices, shares(): total = add(keep, bf16, lax.ppermute(give, 'head', other_core))  2.01 us
    pallas_call x2, Pallas kernels, finish(): pl.pallas_call(functools.partial(final_kernel, first, pieces, len(arrived...  1.51 us
    ppermute x2, waiting for transfers between devices, body(): lax.ppermute(give, 'head', other_core)  0.68 us
  transfers between devices with their start and end apart: 8, of which 6 were waited for; matrix products, arithmetic and copies ran while one was open for 0% of the time, Pallas kernels for 21%

profile of v9, /device:TPU:0, one launch (start us, length us, event | category | flops | bytes accessed | tf_op | source)
XLA Modules:
  0.0 26.1 jit_solution(2684294199715523479)
XLA Ops:
  0.0 1.0 %shard_map.57 = bf16[208,256]{1,0:T(8,128)(2,1)S(1)} custom-call(bf16[256,256]{1,0:T(8,128)(2,1)} %k_ref.7, bf16[256,256]{1,0:T(8,128)(2,1)} %v_ref.7, s32[1,256]{1,0:T(1,128)} %bitcast.1), custom_call_target="tpu_custom_call" | custom-call | flops 8589934592 | tf_op jit(solution)/shard_map/pallas_call | solution.py:33
  1.1 3.0 %collective-permute-start = (bf16[208,256]{1,0:T(8,128)(2,1)S(1)}, bf16[208,256]{1,0:T(8,128)(2,1)S(1)}, u32[]{:S(2)}, u32[]{:S(2)}) collective-permute-start(bf16[208,256]{1,0:T(8,128)(2,1)S(1)} %shard_map.57), channel_id=1, source_target_pairs={{0,4},{4,8},{8,12},{12,16},{16,20},{20,24},{24,28},{28,0},{1,5},{5... | collective-permute-start | bytes 319496 | tf_op jit(solution)/shard_map/ppermute | solution.py:397
  4.1 0.0 copy-done.2
  4.1 0.0 copy-done.3
  4.1 0.0 copy-done.4
  4.1 0.1 shard_map.55
  4.2 3.4 %collective-permute-start.1 = (bf16[320,256]{1,0:T(8,128)(2,1)S(1)}, bf16[320,256]{1,0:T(8,128)(2,1)S(1)}, u32[]{:S(2)}, u32[]{:S(2)}) collective-permute-start(bf16[320,256]{1,0:T(8,128)(2,1)S(1)} %get-tuple-element.27), channel_id=1, source_target_pairs={{0,4},{4,8},{8,12},{12,16},{16,20},{20,24},{24,28},{1,5},{5,9},{9,... | collective-permute-start | bytes 491528 | tf_op jit(solution)/shard_map/ppermute | solution.py:398
  7.6 0.0 copy-done.1
  7.7 0.0 copy-done
  7.7 1.8 %shard_map.58 = (bf16[96,1024]{1,0:T(8,128)(2,1)S(1)}, bf16[96,1024]{1,0:T(8,128)(2,1)S(1)}, bf16[160,1024]{1,0:T(8,128)(2,1)S(1)}, bf16[160,1024]{1,0:T(8,128)(2,1)S(1)}) custom-call(bf16[256,1024]{1,0:T(8,128)(2,1)S(1)} %copy-done.1, bf16[256,256]{1,0:T(8,128)(2,1)S(1)} %copy-done.2, bf16[256,256]{1,0:T(8,128)(2,1)S(1)} %copy-done.3, ...), custom_call_target="tpu_custom_call" | custom-call | flops 134217728 | tf_op jit(solution)/shard_map/pallas_call | solution.py:33
  9.5 0.0 collective-permute-done.rest_0_
  9.6 0.1 collective-permute-start.2
  9.6 0.5 %shard_map.60.keep_ref = bf16[96,1024]{1,0:T(8,128)(2,1)S(1)} custom-call(bf16[96,1024]{1,0:T(8,128)(2,1)S(1)} %get-tuple-element.32.att_ref.high_ref, bf16[1024,4096]{1,0:T(8,128)(2,1)S(1)} %copy-done), custom_call_target="tpu_custom_call" | custom-call | flops 8589934592 | tf_op jit(solution)/shard_map/pallas_call | solution.py:33
  10.1 0.9 %collective-permute-done.2.rest_0_ = bf16[96,1024]{1,0:T(8,128)(2,1)S(1)} collective-permute-done((bf16[96,1024]{1,0:T(8,128)(2,1)S(1)}, bf16[96,1024]{1,0:T(8,128)(2,1)S(1)}, u32[]{:S(2)}, u32[]{:S(2)}) %collective-permute-start.2) | collective-permute-done | bytes 196640 | tf_op jit(solution)/shard_map/ppermute | solution.py:444
  11.1 2.0 %collective-permute-start.3 = (bf16[96,1024]{1,0:T(8,128)(2,1)S(1)}, bf16[96,1024]{1,0:T(8,128)(2,1)S(1)}, u32[]{:S(2)}, u32[]{:S(2)}) collective-permute-start(bf16[96,1024]{1,0:T(8,128)(2,1)S(1)} %shard_map.61.rest_4_), channel_id=1, source_target_pairs={{0,2},{1,3},{2,0},{3,1},{4,6},{5,7},{6,4},{7,5},{8,10},{9,11},{10,... | collective-permute-start | bytes 589832 | tf_op jit(solution)/shard_map/ppermute | solution.py:448
  13.1 0.0 collective-permute-done.1.rest_1_
  13.2 0.1 collective-permute-start.6
  13.3 0.5 %shard_map.66.keep_ref = bf16[160,1024]{1,0:T(8,128)(2,1)S(1)} custom-call(bf16[160,1024]{1,0:T(8,128)(2,1)S(1)} %get-tuple-element.34.low_ref.att_ref, bf16[1024,4096]{1,0:T(8,128)(2,1)S(1)} %copy-done), custom_call_target="tpu_custom_call" | custom-call | flops 8589934592 | tf_op jit(solution)/shard_map/pallas_call | solution.py:33
  13.8 1.1 %collective-permute-done.6.rest_0_ = bf16[160,1024]{1,0:T(8,128)(2,1)S(1)} collective-permute-done((bf16[160,1024]{1,0:T(8,128)(2,1)S(1)}, bf16[160,1024]{1,0:T(8,128)(2,1)S(1)}, u32[]{:S(2)}, u32[]{:S(2)}) %collective-permute-start.6) | collective-permute-done | bytes 327712 | tf_op jit(solution)/shard_map/ppermute | solution.py:444
  14.9 0.1 shard_map.67
  15.0 0.1 collective-permute-start.7
  15.1 3.8 %collective-permute-done.3.rest_0_ = bf16[96,1024]{1,0:T(8,128)(2,1)S(1)} collective-permute-done((bf16[96,1024]{1,0:T(8,128)(2,1)S(1)}, bf16[96,1024]{1,0:T(8,128)(2,1)S(1)}, u32[]{:S(2)}, u32[]{:S(2)}) %collective-permute-start.3) | collective-permute-done | bytes 196640 | tf_op jit(solution)/shard_map/ppermute | solution.py:448
  18.9 0.7 %shard_map.63 = (bf16[256,1024]{1,0:T(8,128)(2,1)S(1)}, bf16[256,512]{1,0:T(8,128)(2,1)S(1)}, bf16[256,512]{1,0:T(8,128)(2,1)S(1)}) custom-call(bf16[160,1024]{1,0:T(8,128)(2,1)S(1)} %get-tuple-element.34.low_ref.att_ref, bf16[96,1024]{1,0:T(8,128)(2,1)S(1)} %get-tuple-element.32.att_ref.high_ref, bf16[1024,4096]{1,0:T(8,128)(2,1)S(1)} %copy-done, ...), custom_call_target="tpu_custom_call" | custom-call | flops 1073741824 | tf_op jit(solution)/shard_map/pallas_call | solution.py:33
  19.6 0.1 collective-permute-start.4
  19.7 0.5 %collective-permute-start.5 = (bf16[256,512]{1,0:T(8,128)(2,1)S(1)}, bf16[256,512]{1,0:T(8,128)(2,1)S(1)}, u32[]{:S(2)}, u32[]{:S(2)}) collective-permute-start(bf16[256,512]{1,0:T(8,128)(2,1)S(1)} %get-tuple-element.37), channel_id=1, source_target_pairs={{0,1},{1,0},{2,3},{3,2},{4,5},{5,4},{6,7},{7,6},{8,9},{9,8},{10,11... | collective-permute-start | bytes 786440 | tf_op jit(solution)/shard_map/ppermute | solution.py:487
  20.2 0.7 %shard_map.64.keep_ref = bf16[256,1024]{1,0:T(8,128)(2,1)S(1)} custom-call(bf16[256,1024]{1,0:T(8,128)(2,1)S(1)} %get-tuple-element.35.att_ref, bf16[1024,4096]{1,0:T(8,128)(2,1)S(1)} %copy-done), custom_call_target="tpu_custom_call" | custom-call | tf_op jit(solution)/shard_map/pallas_call | solution.py:33
  20.9 0.3 %collective-permute-done.4.rest_0_ = bf16[256,512]{1,0:T(8,128)(2,1)S(1)} collective-permute-done((bf16[256,512]{1,0:T(8,128)(2,1)S(1)}, bf16[256,512]{1,0:T(8,128)(2,1)S(1)}, u32[]{:S(2)}, u32[]{:S(2)}) %collective-permute-start.4) | collective-permute-done | bytes 262176 | tf_op jit(solution)/shard_map/ppermute | solution.py:487
  21.2 0.4 %collective-permute-done.5.rest_1_ = bf16[256,512]{1,0:T(8,128)(2,1)S(1)} collective-permute-done((bf16[256,512]{1,0:T(8,128)(2,1)S(1)}, bf16[256,512]{1,0:T(8,128)(2,1)S(1)}, u32[]{:S(2)}, u32[]{:S(2)}) %collective-permute-start.5) | collective-permute-done | bytes 262176 | tf_op jit(solution)/shard_map/ppermute | solution.py:487
  21.6 0.1 shard_map.65.local_ref
  21.7 0.7 %shard_map.68.rest_1_ = bf16[256,1024]{1,0:T(8,128)(2,1)} custom-call(f32[256,1024]{1,0:T(8,128)S(1)} %shard_map.65.local_ref, bf16[96,1024]{1,0:T(8,128)(2,1)S(1)} %collective-permute-done.3.rest_0_), custom_call_target="tpu_custom_call" | custom-call | tf_op jit(solution)/shard_map/pallas_call | solution.py:490
  22.4 2.9 %collective-permute-done.7.rest_0_ = bf16[160,1024]{1,0:T(8,128)(2,1)S(1)} collective-permute-done((bf16[160,1024]{1,0:T(8,128)(2,1)S(1)}, bf16[160,1024]{1,0:T(8,128)(2,1)S(1)}, u32[]{:S(2)}, u32[]{:S(2)}) %collective-permute-start.7) | collective-permute-done | bytes 327712 | tf_op jit(solution)/shard_map/ppermute | solution.py:448
  25.4 0.8 %shard_map.69 = bf16[256,1024]{1,0:T(8,128)(2,1)} custom-call(f32[256,1024]{1,0:T(8,128)S(1)} %shard_map.65.local_ref, bf16[160,1024]{1,0:T(8,128)(2,1)S(1)} %collective-permute-done.7.rest_0_, bf16[256,1024]{1,0:T(8,128)(2,1)} %shard_map.68.rest_1_), custom_call_target="tpu_custom_call", output_to_operand_aliasing={{}: (2, {})} | custom-call | tf_op jit(solution)/shard_map/pallas_call | solution.py:490
  (9 shorter events, 0.2 us)
Async XLA Ops:
  0.0 4.1 %copy-start.2 = (bf16[256,256]{1,0:T(8,128)(2,1)S(1)}, bf16[256,256]{1,0:T(8,128)(2,1)}, u32[]{:S(2)}) copy-start(bf16[256,256]{1,0:T(8,128)(2,1)} %k_ref.7) | copy-start | bytes 393220
  0.0 4.1 %copy-start.3 = (bf16[256,256]{1,0:T(8,128)(2,1)S(1)}, bf16[256,256]{1,0:T(8,128)(2,1)}, u32[]{:S(2)}) copy-start(bf16[256,256]{1,0:T(8,128)(2,1)} %v_ref.7) | copy-start | bytes 393220
  0.0 4.1 %copy-start.4 = (s32[256]{0:T(256)S(1)}, s32[256]{0:T(256)}, u32[]{:S(2)}) copy-start(s32[256]{0:T(256)} %param.8) | copy-start | bytes 3076
  0.0 7.6 %copy-start.1 = (bf16[256,1024]{1,0:T(8,128)(2,1)S(1)}, bf16[256,1024]{1,0:T(8,128)(2,1)}, u32[]{:S(2)}) copy-start(bf16[256,1024]{1,0:T(8,128)(2,1)} %q_ref.7) | copy-start | bytes 1572868
  0.0 7.7 %copy-start = (bf16[1024,4096]{1,0:T(8,128)(2,1)S(1)}, bf16[1024,4096]{1,0:T(8,128)(2,1)}, u32[]{:S(2)}) copy-start(bf16[1024,4096]{1,0:T(8,128)(2,1)} %w_ref.13) | copy-start | bytes 25165828
  1.1 8.4 %collective-permute-start = (bf16[208,256]{1,0:T(8,128)(2,1)S(1)}, bf16[208,256]{1,0:T(8,128)(2,1)S(1)}, u32[]{:S(2)}, u32[]{:S(2)}) collective-permute-start(bf16[208,256]{1,0:T(8,128)(2,1)S(1)} %shard_map.57), channel_id=1, source_target_pairs={{0,4},{4,8},{8,12},{12,16},{16,20},{20,24},{24,28},{28,0},{1,5},{5... | collective-permute-start | bytes 319496 | tf_op jit(solution)/shard_map/ppermute | solution.py:397
  4.2 8.9 %collective-permute-start.1 = (bf16[320,256]{1,0:T(8,128)(2,1)S(1)}, bf16[320,256]{1,0:T(8,128)(2,1)S(1)}, u32[]{:S(2)}, u32[]{:S(2)}) collective-permute-start(bf16[320,256]{1,0:T(8,128)(2,1)S(1)} %get-tuple-element.27), channel_id=1, source_target_pairs={{0,4},{4,8},{8,12},{12,16},{16,20},{20,24},{24,28},{1,5},{5,9},{9,... | collective-permute-start | bytes 491528 | tf_op jit(solution)/shard_map/ppermute | solution.py:398
  9.6 1.5 %collective-permute-start.2 = (bf16[96,1024]{1,0:T(8,128)(2,1)S(1)}, bf16[96,1024]{1,0:T(8,128)(2,1)S(1)}, u32[]{:S(2)}, u32[]{:S(2)}) collective-permute-start(bf16[96,1024]{1,0:T(8,128)(2,1)S(1)} %get-tuple-element.33), channel_id=1, source_target_pairs={{0,1},{1,0},{2,3},{3,2},{4,5},{5,4},{6,7},{7,6},{8,9},{9,8},{10,11... | collective-permute-start | bytes 589832 | tf_op jit(solution)/shard_map/ppermute | solution.py:444
  11.1 7.8 %collective-permute-start.3 = (bf16[96,1024]{1,0:T(8,128)(2,1)S(1)}, bf16[96,1024]{1,0:T(8,128)(2,1)S(1)}, u32[]{:S(2)}, u32[]{:S(2)}) collective-permute-start(bf16[96,1024]{1,0:T(8,128)(2,1)S(1)} %shard_map.61.rest_4_), channel_id=1, source_target_pairs={{0,2},{1,3},{2,0},{3,1},{4,6},{5,7},{6,4},{7,5},{8,10},{9,11},{10,... | collective-permute-start | bytes 589832 | tf_op jit(solution)/shard_map/ppermute | solution.py:448
  13.2 1.7 %collective-permute-start.6 = (bf16[160,1024]{1,0:T(8,128)(2,1)S(1)}, bf16[160,1024]{1,0:T(8,128)(2,1)S(1)}, u32[]{:S(2)}, u32[]{:S(2)}) collective-permute-start(bf16[160,1024]{1,0:T(8,128)(2,1)S(1)} %get-tuple-element.38), channel_id=1, source_target_pairs={{0,1},{1,0},{2,3},{3,2},{4,5},{5,4},{6,7},{7,6},{8,9},{9,8},{10,11... | collective-permute-start | bytes 983048 | tf_op jit(solution)/shard_map/ppermute | solution.py:444
  15.0 10.4 %collective-permute-start.7 = (bf16[160,1024]{1,0:T(8,128)(2,1)S(1)}, bf16[160,1024]{1,0:T(8,128)(2,1)S(1)}, u32[]{:S(2)}, u32[]{:S(2)}) collective-permute-start(bf16[160,1024]{1,0:T(8,128)(2,1)S(1)} %shard_map.67), channel_id=1, source_target_pairs={{0,2},{1,3},{2,0},{3,1},{4,6},{5,7},{6,4},{7,5},{8,10},{9,11},{10,... | collective-permute-start | bytes 983048 | tf_op jit(solution)/shard_map/ppermute | solution.py:448
  19.6 1.6 %collective-permute-start.4 = (bf16[256,512]{1,0:T(8,128)(2,1)S(1)}, bf16[256,512]{1,0:T(8,128)(2,1)S(1)}, u32[]{:S(2)}, u32[]{:S(2)}) collective-permute-start(bf16[256,512]{1,0:T(8,128)(2,1)S(1)} %get-tuple-element.36), channel_id=1, source_target_pairs={{0,1},{1,0},{2,3},{3,2},{4,5},{5,4},{6,7},{7,6},{8,9},{9,8},{10,11... | collective-permute-start | bytes 786440 | tf_op jit(solution)/shard_map/ppermute | solution.py:487
  19.7 1.9 %collective-permute-start.5 = (bf16[256,512]{1,0:T(8,128)(2,1)S(1)}, bf16[256,512]{1,0:T(8,128)(2,1)S(1)}, u32[]{:S(2)}, u32[]{:S(2)}) collective-permute-start(bf16[256,512]{1,0:T(8,128)(2,1)S(1)} %get-tuple-element.37), channel_id=1, source_target_pairs={{0,1},{1,0},{2,3},{3,2},{4,5},{5,4},{6,7},{7,6},{8,9},{9,8},{10,11... | collective-permute-start | bytes 786440 | tf_op jit(solution)/shard_map/ppermute | solution.py:487

commit v10 on v9

--- a/solution.py
+++ b/solution.py
@@ -10,7 +10,7 @@
 
 HEAD_DIM = 128
 CORES = 2
-CUT = 160 / 256
+CUT = 176 / 256
 DOC_ROWS = 16
 PIECES = 1
 LOG2_SCALE = math.log2(math.e) / math.sqrt(HEAD_DIM)

time: 26.3 us -> 26.2 us (level)
  no operation moved by 1% of the time
where the time goes in v10:
time: 26.2 us; the launch traced here: 26.1 us
  starting transfers between devices  9.34 us (36%)
  waiting for transfers between devices  9.24 us (35%)
  Pallas kernels  7.32 us (28%)
    ppermute x2, waiting for transfers between devices, shares(): lax.ppermute(total, 'head', [(j, (j + step) % devices) for j in range(dev...  6.6 us
    pallas_call x13, Pallas kernels, call(): pl.pallas_call(kernel, out_shape=out_shape, in_specs=in_specs, out_specs=...  5.81 us
    ppermute x1, starting transfers between devices, body(): lows.append(lax.ppermute(packed_low, 'ctx', ring[:place_count - s]))  3.43 us
    ppermute x1, starting transfers between devices, body(): highs.append(lax.ppermute(packed_high, 'ctx', ring))  3.03 us
    ppermute x2, starting transfers between devices, shares(): lax.ppermute(total, 'head', [(j, (j + step) % devices) for j in range(dev...  2.16 us
    ppermute x2, waiting for transfers between devices, shares(): total = add(keep, bf16, lax.ppermute(give, 'head', other_core))  1.96 us
    pallas_call x2, Pallas kernels, finish(): pl.pallas_call(functools.partial(final_kernel, first, pieces, len(arrived...  1.51 us
    ppermute x2, waiting for transfers between devices, body(): lax.ppermute(give, 'head', other_core)  0.68 us
  transfers between devices with their start and end apart: 8, of which 6 were waited for; matrix products, arithmetic and copies ran while one was open for 0% of the time, Pallas kernels for 21%

profile of v10, /device:TPU:0, one launch (start us, length us, event | category | flops | bytes accessed | tf_op | source)
XLA Modules:
  0.0 26.1 jit_solution(17824304736241295014)
XLA Ops:
  0.0 1.0 %shard_map.57 = bf16[176,256]{1,0:T(8,128)(2,1)S(1)} custom-call(bf16[256,256]{1,0:T(8,128)(2,1)} %k_ref.7, bf16[256,256]{1,0:T(8,128)(2,1)} %v_ref.7, s32[1,256]{1,0:T(1,128)} %bitcast.1), custom_call_target="tpu_custom_call" | custom-call | flops 8589934592 | tf_op jit(solution)/shard_map/pallas_call | solution.py:33
  1.0 3.0 %collective-permute-start = (bf16[176,256]{1,0:T(8,128)(2,1)S(1)}, bf16[176,256]{1,0:T(8,128)(2,1)S(1)}, u32[]{:S(2)}, u32[]{:S(2)}) collective-permute-start(bf16[176,256]{1,0:T(8,128)(2,1)S(1)} %shard_map.57), channel_id=1, source_target_pairs={{0,4},{4,8},{8,12},{12,16},{16,20},{20,24},{24,28},{28,0},{1,5},{5... | collective-permute-start | bytes 270344 | tf_op jit(solution)/shard_map/ppermute | solution.py:397
  4.1 0.0 copy-done.2
  4.1 0.0 copy-done.3
  4.1 0.0 copy-done.4
  4.1 0.1 shard_map.55
  4.2 3.4 %collective-permute-start.1 = (bf16[352,256]{1,0:T(8,128)(2,1)S(1)}, bf16[352,256]{1,0:T(8,128)(2,1)S(1)}, u32[]{:S(2)}, u32[]{:S(2)}) collective-permute-start(bf16[352,256]{1,0:T(8,128)(2,1)S(1)} %get-tuple-element.27), channel_id=1, source_target_pairs={{0,4},{4,8},{8,12},{12,16},{16,20},{20,24},{24,28},{1,5},{5,9},{9,... | collective-permute-start | bytes 540680 | tf_op jit(solution)/shard_map/ppermute | solution.py:398
  7.6 0.0 copy-done.1
  7.7 0.0 copy-done
  7.7 1.9 %shard_map.58 = (bf16[80,1024]{1,0:T(8,128)(2,1)S(1)}, bf16[80,1024]{1,0:T(8,128)(2,1)S(1)}, bf16[176,1024]{1,0:T(8,128)(2,1)S(1)}, bf16[176,1024]{1,0:T(8,128)(2,1)S(1)}) custom-call(bf16[256,1024]{1,0:T(8,128)(2,1)S(1)} %copy-done.1, bf16[256,256]{1,0:T(8,128)(2,1)S(1)} %copy-done.2, bf16[256,256]{1,0:T(8,128)(2,1)S(1)} %copy-done.3, ...), custom_call_target="tpu_custom_call" | custom-call | flops 134217728 | tf_op jit(solution)/shard_map/pallas_call | solution.py:33
  9.5 0.0 collective-permute-done.rest_0_
  9.6 0.1 collective-permute-start.2
  9.7 0.5 %shard_map.60.keep_ref = bf16[80,1024]{1,0:T(8,128)(2,1)S(1)} custom-call(bf16[80,1024]{1,0:T(8,128)(2,1)S(1)} %get-tuple-element.32.att_ref.high_ref, bf16[1024,4096]{1,0:T(8,128)(2,1)S(1)} %copy-done), custom_call_target="tpu_custom_call" | custom-call | flops 8589934592 | tf_op jit(solution)/shard_map/pallas_call | solution.py:33
  10.2 0.9 %collective-permute-done.2.rest_0_ = bf16[80,1024]{1,0:T(8,128)(2,1)S(1)} collective-permute-done((bf16[80,1024]{1,0:T(8,128)(2,1)S(1)}, bf16[80,1024]{1,0:T(8,128)(2,1)S(1)}, u32[]{:S(2)}, u32[]{:S(2)}) %collective-permute-start.2) | collective-permute-done | bytes 163872 | tf_op jit(solution)/shard_map/ppermute | solution.py:444
  11.1 1.8 %collective-permute-start.3 = (bf16[80,1024]{1,0:T(8,128)(2,1)S(1)}, bf16[80,1024]{1,0:T(8,128)(2,1)S(1)}, u32[]{:S(2)}, u32[]{:S(2)}) collective-permute-start(bf16[80,1024]{1,0:T(8,128)(2,1)S(1)} %shard_map.61.rest_4_), channel_id=1, source_target_pairs={{0,2},{1,3},{2,0},{3,1},{4,6},{5,7},{6,4},{7,5},{8,10},{9,11},{10,... | collective-permute-start | bytes 491528 | tf_op jit(solution)/shard_map/ppermute | solution.py:448
  12.9 0.0 collective-permute-done.1.rest_1_
  12.9 0.1 collective-permute-start.6
  13.0 0.6 %shard_map.66.keep_ref = bf16[176,1024]{1,0:T(8,128)(2,1)S(1)} custom-call(bf16[176,1024]{1,0:T(8,128)(2,1)S(1)} %get-tuple-element.34.low_ref.att_ref, bf16[1024,4096]{1,0:T(8,128)(2,1)S(1)} %copy-done), custom_call_target="tpu_custom_call" | custom-call | flops 8589934592 | tf_op jit(solution)/shard_map/pallas_call | solution.py:33
  13.6 1.1 %collective-permute-done.6.rest_0_ = bf16[176,1024]{1,0:T(8,128)(2,1)S(1)} collective-permute-done((bf16[176,1024]{1,0:T(8,128)(2,1)S(1)}, bf16[176,1024]{1,0:T(8,128)(2,1)S(1)}, u32[]{:S(2)}, u32[]{:S(2)}) %collective-permute-start.6) | collective-permute-done | bytes 360480 | tf_op jit(solution)/shard_map/ppermute | solution.py:444
  14.7 0.1 shard_map.67
  14.8 0.4 %collective-permute-start.7 = (bf16[176,1024]{1,0:T(8,128)(2,1)S(1)}, bf16[176,1024]{1,0:T(8,128)(2,1)S(1)}, u32[]{:S(2)}, u32[]{:S(2)}) collective-permute-start(bf16[176,1024]{1,0:T(8,128)(2,1)S(1)} %shard_map.67), channel_id=1, source_target_pairs={{0,2},{1,3},{2,0},{3,1},{4,6},{5,7},{6,4},{7,5},{8,10},{9,11},{10,... | collective-permute-start | bytes 1081352 | tf_op jit(solution)/shard_map/ppermute | solution.py:448
  15.1 2.3 %collective-permute-done.3.rest_0_ = bf16[80,1024]{1,0:T(8,128)(2,1)S(1)} collective-permute-done((bf16[80,1024]{1,0:T(8,128)(2,1)S(1)}, bf16[80,1024]{1,0:T(8,128)(2,1)S(1)}, u32[]{:S(2)}, u32[]{:S(2)}) %collective-permute-start.3) | collective-permute-done | bytes 163872 | tf_op jit(solution)/shard_map/ppermute | solution.py:448
  17.4 0.7 %shard_map.63 = (bf16[256,1024]{1,0:T(8,128)(2,1)S(1)}, bf16[256,512]{1,0:T(8,128)(2,1)S(1)}, bf16[256,512]{1,0:T(8,128)(2,1)S(1)}) custom-call(bf16[176,1024]{1,0:T(8,128)(2,1)S(1)} %get-tuple-element.34.low_ref.att_ref, bf16[80,1024]{1,0:T(8,128)(2,1)S(1)} %get-tuple-element.32.att_ref.high_ref, bf16[1024,4096]{1,0:T(8,128)(2,1)S(1)} %copy-done, ...), custom_call_target="tpu_custom_call" | custom-call | flops 1073741824 | tf_op jit(solution)/shard_map/pallas_call | solution.py:33
  18.2 0.1 collective-permute-start.4
  18.2 0.5 %collective-permute-start.5 = (bf16[256,512]{1,0:T(8,128)(2,1)S(1)}, bf16[256,512]{1,0:T(8,128)(2,1)S(1)}, u32[]{:S(2)}, u32[]{:S(2)}) collective-permute-start(bf16[256,512]{1,0:T(8,128)(2,1)S(1)} %get-tuple-element.37), channel_id=1, source_target_pairs={{0,1},{1,0},{2,3},{3,2},{4,5},{5,4},{6,7},{7,6},{8,9},{9,8},{10,11... | collective-permute-start | bytes 786440 | tf_op jit(solution)/shard_map/ppermute | solution.py:487
  18.7 0.7 %shard_map.64.keep_ref = bf16[256,1024]{1,0:T(8,128)(2,1)S(1)} custom-call(bf16[256,1024]{1,0:T(8,128)(2,1)S(1)} %get-tuple-element.35.att_ref, bf16[1024,4096]{1,0:T(8,128)(2,1)S(1)} %copy-done), custom_call_target="tpu_custom_call" | custom-call | tf_op jit(solution)/shard_map/pallas_call | solution.py:33
  19.4 0.3 %collective-permute-done.4.rest_0_ = bf16[256,512]{1,0:T(8,128)(2,1)S(1)} collective-permute-done((bf16[256,512]{1,0:T(8,128)(2,1)S(1)}, bf16[256,512]{1,0:T(8,128)(2,1)S(1)}, u32[]{:S(2)}, u32[]{:S(2)}) %collective-permute-start.4) | collective-permute-done | bytes 262176 | tf_op jit(solution)/shard_map/ppermute | solution.py:487
  19.8 0.4 %collective-permute-done.5.rest_1_ = bf16[256,512]{1,0:T(8,128)(2,1)S(1)} collective-permute-done((bf16[256,512]{1,0:T(8,128)(2,1)S(1)}, bf16[256,512]{1,0:T(8,128)(2,1)S(1)}, u32[]{:S(2)}, u32[]{:S(2)}) %collective-permute-start.5) | collective-permute-done | bytes 262176 | tf_op jit(solution)/shard_map/ppermute | solution.py:487
  20.1 0.1 shard_map.65.local_ref
  20.2 0.7 %shard_map.68.rest_1_ = bf16[256,1024]{1,0:T(8,128)(2,1)} custom-call(f32[256,1024]{1,0:T(8,128)S(1)} %shard_map.65.local_ref, bf16[80,1024]{1,0:T(8,128)(2,1)S(1)} %collective-permute-done.3.rest_0_), custom_call_target="tpu_custom_call" | custom-call | tf_op jit(solution)/shard_map/pallas_call | solution.py:490
  21.0 4.3 %collective-permute-done.7.rest_0_ = bf16[176,1024]{1,0:T(8,128)(2,1)S(1)} collective-permute-done((bf16[176,1024]{1,0:T(8,128)(2,1)S(1)}, bf16[176,1024]{1,0:T(8,128)(2,1)S(1)}, u32[]{:S(2)}, u32[]{:S(2)}) %collective-permute-start.7) | collective-permute-done | bytes 360480 | tf_op jit(solution)/shard_map/ppermute | solution.py:448
  25.3 0.8 %shard_map.69 = bf16[256,1024]{1,0:T(8,128)(2,1)} custom-call(f32[256,1024]{1,0:T(8,128)S(1)} %shard_map.65.local_ref, bf16[176,1024]{1,0:T(8,128)(2,1)S(1)} %collective-permute-done.7.rest_0_, bf16[256,1024]{1,0:T(8,128)(2,1)} %shard_map.68.rest_1_), custom_call_target="tpu_custom_call", output_to_operand_aliasing={{}: (2, {})} | custom-call | tf_op jit(solution)/shard_map/pallas_call | solution.py:490
  (9 shorter events, 0.2 us)
Async XLA Ops:
  0.0 4.1 %copy-start.2 = (bf16[256,256]{1,0:T(8,128)(2,1)S(1)}, bf16[256,256]{1,0:T(8,128)(2,1)}, u32[]{:S(2)}) copy-start(bf16[256,256]{1,0:T(8,128)(2,1)} %k_ref.7) | copy-start | bytes 393220
  0.0 4.1 %copy-start.3 = (bf16[256,256]{1,0:T(8,128)(2,1)S(1)}, bf16[256,256]{1,0:T(8,128)(2,1)}, u32[]{:S(2)}) copy-start(bf16[256,256]{1,0:T(8,128)(2,1)} %v_ref.7) | copy-start | bytes 393220
  0.0 4.1 %copy-start.4 = (s32[256]{0:T(256)S(1)}, s32[256]{0:T(256)}, u32[]{:S(2)}) copy-start(s32[256]{0:T(256)} %param.8) | copy-start | bytes 3076
  0.0 7.6 %copy-start.1 = (bf16[256,1024]{1,0:T(8,128)(2,1)S(1)}, bf16[256,1024]{1,0:T(8,128)(2,1)}, u32[]{:S(2)}) copy-start(bf16[256,1024]{1,0:T(8,128)(2,1)} %q_ref.7) | copy-start | bytes 1572868
  0.0 7.7 %copy-start = (bf16[1024,4096]{1,0:T(8,128)(2,1)S(1)}, bf16[1024,4096]{1,0:T(8,128)(2,1)}, u32[]{:S(2)}) copy-start(bf16[1024,4096]{1,0:T(8,128)(2,1)} %w_ref.13) | copy-start | bytes 25165828
  1.0 8.5 %collective-permute-start = (bf16[176,256]{1,0:T(8,128)(2,1)S(1)}, bf16[176,256]{1,0:T(8,128)(2,1)S(1)}, u32[]{:S(2)}, u32[]{:S(2)}) collective-permute-start(bf16[176,256]{1,0:T(8,128)(2,1)S(1)} %shard_map.57), channel_id=1, source_target_pairs={{0,4},{4,8},{8,12},{12,16},{16,20},{20,24},{24,28},{28,0},{1,5},{5... | collective-permute-start | bytes 270344 | tf_op jit(solution)/shard_map/ppermute | solution.py:397
  4.2 8.7 %collective-permute-start.1 = (bf16[352,256]{1,0:T(8,128)(2,1)S(1)}, bf16[352,256]{1,0:T(8,128)(2,1)S(1)}, u32[]{:S(2)}, u32[]{:S(2)}) collective-permute-start(bf16[352,256]{1,0:T(8,128)(2,1)S(1)} %get-tuple-element.27), channel_id=1, source_target_pairs={{0,4},{4,8},{8,12},{12,16},{16,20},{20,24},{24,28},{1,5},{5,9},{9,... | collective-permute-start | bytes 540680 | tf_op jit(solution)/shard_map/ppermute | solution.py:398
  9.6 1.5 %collective-permute-start.2 = (bf16[80,1024]{1,0:T(8,128)(2,1)S(1)}, bf16[80,1024]{1,0:T(8,128)(2,1)S(1)}, u32[]{:S(2)}, u32[]{:S(2)}) collective-permute-start(bf16[80,1024]{1,0:T(8,128)(2,1)S(1)} %get-tuple-element.33), channel_id=1, source_target_pairs={{0,1},{1,0},{2,3},{3,2},{4,5},{5,4},{6,7},{7,6},{8,9},{9,8},{10,11... | collective-permute-start | bytes 491528 | tf_op jit(solution)/shard_map/ppermute | solution.py:444
  11.1 6.3 %collective-permute-start.3 = (bf16[80,1024]{1,0:T(8,128)(2,1)S(1)}, bf16[80,1024]{1,0:T(8,128)(2,1)S(1)}, u32[]{:S(2)}, u32[]{:S(2)}) collective-permute-start(bf16[80,1024]{1,0:T(8,128)(2,1)S(1)} %shard_map.61.rest_4_), channel_id=1, source_target_pairs={{0,2},{1,3},{2,0},{3,1},{4,6},{5,7},{6,4},{7,5},{8,10},{9,11},{10,... | collective-permute-start | bytes 491528 | tf_op jit(solution)/shard_map/ppermute | solution.py:448
  12.9 1.7 %collective-permute-start.6 = (bf16[176,1024]{1,0:T(8,128)(2,1)S(1)}, bf16[176,1024]{1,0:T(8,128)(2,1)S(1)}, u32[]{:S(2)}, u32[]{:S(2)}) collective-permute-start(bf16[176,1024]{1,0:T(8,128)(2,1)S(1)} %get-tuple-element.38), channel_id=1, source_target_pairs={{0,1},{1,0},{2,3},{3,2},{4,5},{5,4},{6,7},{7,6},{8,9},{9,8},{10,11... | collective-permute-start | bytes 1081352 | tf_op jit(solution)/shard_map/ppermute | solution.py:444
  14.8 10.5 %collective-permute-start.7 = (bf16[176,1024]{1,0:T(8,128)(2,1)S(1)}, bf16[176,1024]{1,0:T(8,128)(2,1)S(1)}, u32[]{:S(2)}, u32[]{:S(2)}) collective-permute-start(bf16[176,1024]{1,0:T(8,128)(2,1)S(1)} %shard_map.67), channel_id=1, source_target_pairs={{0,2},{1,3},{2,0},{3,1},{4,6},{5,7},{6,4},{7,5},{8,10},{9,11},{10,... | collective-permute-start | bytes 1081352 | tf_op jit(solution)/shard_map/ppermute | solution.py:448
  18.2 1.6 %collective-permute-start.4 = (bf16[256,512]{1,0:T(8,128)(2,1)S(1)}, bf16[256,512]{1,0:T(8,128)(2,1)S(1)}, u32[]{:S(2)}, u32[]{:S(2)}) collective-permute-start(bf16[256,512]{1,0:T(8,128)(2,1)S(1)} %get-tuple-element.36), channel_id=1, source_target_pairs={{0,1},{1,0},{2,3},{3,2},{4,5},{5,4},{6,7},{7,6},{8,9},{9,8},{10,11... | collective-permute-start | bytes 786440 | tf_op jit(solution)/shard_map/ppermute | solution.py:487
  18.2 1.9 %collective-permute-start.5 = (bf16[256,512]{1,0:T(8,128)(2,1)S(1)}, bf16[256,512]{1,0:T(8,128)(2,1)S(1)}, u32[]{:S(2)}, u32[]{:S(2)}) collective-permute-start(bf16[256,512]{1,0:T(8,128)(2,1)S(1)} %get-tuple-element.37), channel_id=1, source_target_pairs={{0,1},{1,0},{2,3},{3,2},{4,5},{5,4},{6,7},{7,6},{8,9},{9,8},{10,11... | collective-permute-start | bytes 786440 | tf_op jit(solution)/shard_map/ppermute | solution.py:487
